TPU v7x, 128 devices: a whole 4x4x4 slice. The times are simulated.
128 devices in a mesh: ctx: 8 (over y_lo, x), tp: 16 (over y_hi, z, core).
Axes of the slice: x: 4, y: 4 (y_hi: 2, y_lo: 2; y = y_hi * 2 + y_lo), z: 4, core: 2. Of those that a mesh axis runs over, the one named last changes fastest.
Arguments:
- hidden: bfloat16 [4, 2048, 6144], P(None, 'ctx', 'tp'), may hold values from -6 to 6
- w_query: bfloat16 [6144, 8192], P(None, 'tp'), may hold values from -0.078125 to 0.078125
- w_key: bfloat16 [6144, 8192], P(None, 'tp'), may hold values from -0.078125 to 0.078125
- w_value: bfloat16 [6144, 8192], P(None, 'tp'), may hold values from -0.078125 to 0.078125
- w_gate: bfloat16 [6144, 8192], P(None, 'tp'), may hold values from -0.078125 to 0.078125
- decay_rate: float32 [64], P('tp'), as said below
- norm_gain: float32 [8192], P('tp'), may hold values from 0.5 to 1.5
- doc_lengths: int32 [4, 4], replicated, may hold values from 1 to 1024, 2048 in all within a row
Outputs:
- attended: bfloat16 [4, 2048, 8192], P(None, 'ctx', 'tp')
Inputs may be any that keep to these rules, and one draw needn't show every extreme that they name: Each head's state is multiplied by exp(-decay_rate) at every position; positive. `doc_lengths`: each sequence's documents fill its 2048 positions; the longest document of each sequence has exactly half of 2048 positions.
All inputs are finite; a program needn't handle non-finite values.
Results may differ from a plain program's by a relative error of at most 0.006.
Values may be sent and summed in bfloat16 or wider, within the bound.
No kernel may reach another device: no remote copies, remote signals or barrier semaphores. Data moves between devices by JAX's collectives and lax.ppermute only.
A program may use at most 128 MiB of HBM per device.

v0:
```python
import jax
import jax.numpy as jnp
from jax import lax
from jax.sharding import PartitionSpec as P

epsilon = 1e-06


def shifted(block, axis, distance):
    devices = range(lax.axis_size(axis))
    route = [(i - distance, i) for i in devices if i - distance in devices]
    return lax.ppermute(block, axis, route)


def doc_numbers(positions, lengths):
    ends = jnp.cumsum(lengths, axis=1)[:, :-1]
    return jnp.sum((positions[None, :, None] >= ends[:, None, :]).astype(jnp.int32), axis=2)


def block_terms(query, keys, values, decay, documents, before):
    block_len = query.shape[1]
    local = lax.iota(jnp.int32, block_len)
    offsets = (local[:, None] - local[None, :]).astype(jnp.float32)
    causal = offsets >= 0.0
    pair_decay = jnp.exp(-decay[:, None, None] * jnp.maximum(offsets, 0.0))
    same_doc = documents[:, :, None] == documents[:, None, :]
    allowed = jnp.logical_and(causal[None], same_doc)
    scores = jnp.einsum("sihe,sjhe->shij", query, keys, preferred_element_type=jnp.float32)
    mixed = jnp.where(allowed[:, None], scores * pair_decay[None], 0.0).astype(jnp.bfloat16)
    inner = jnp.einsum("shij,sjhe->sihe", mixed, values, preferred_element_type=jnp.float32)
    position = local.astype(jnp.float32)
    final_doc = documents[:, -1]
    keep_rows = (documents == final_doc[:, None]).astype(jnp.float32)
    out_decay = jnp.exp(-decay[None, :] * (block_len - 1.0 - position)[:, None])
    weighted = (
        keys.astype(jnp.float32) * (keep_rows[:, :, None] * out_decay[None])[..., None]
    ).astype(jnp.bfloat16)
    block_state = jnp.einsum(
        "sjhe,sjhf->shef", weighted, values, preferred_element_type=jnp.float32
    )
    carry_keep = (final_doc == before).astype(jnp.float32)[:, None] * jnp.exp(-decay * block_len)[
        None, :
    ]
    in_decay = jnp.exp(-decay[None, :] * (position + 1.0)[:, None])
    in_rows = (documents == before[:, None]).astype(jnp.float32)
    in_scale = in_rows[:, :, None] * in_decay[None]
    return (inner, block_state, carry_keep, in_scale)


def hand_off(carry_keep, block_state):
    outgoing = block_state
    incoming = jnp.zeros_like(block_state)
    for segment in range(lax.axis_size("ctx") - 1):
        incoming = shifted(outgoing.astype(jnp.bfloat16), "ctx", 1).astype(outgoing.dtype)
        outgoing = carry_keep[:, :, None, None] * incoming + block_state
    return incoming


def attend(section, documents, before, weights, decay):
    count, block_len, _ = section.shape
    width = weights[0].shape[1]
    heads = decay.shape[0]
    head_size = width // heads
    piece = lax.all_gather(section, "tp", axis=2, tiled=True)
    rows = piece.reshape(count * block_len, piece.shape[2])
    totals = tuple(
        (jnp.dot(rows, weight, preferred_element_type=jnp.float32) for weight in weights)
    )
    query, keys, values = [
        jax.nn.silu(total).astype(jnp.bfloat16).reshape(count, block_len, heads, head_size)
        for total in totals[:3]
    ]
    gate_logits = totals[3].reshape(count, block_len, width)
    inner, block_state, carry_keep, in_scale = block_terms(
        query, keys, values, decay, documents, before
    )
    incoming = hand_off(carry_keep, block_state)
    carried = jnp.einsum(
        "sihe,shef->sihf", query.astype(jnp.float32), incoming, precision=lax.Precision.HIGHEST
    )
    attn = inner + carried * in_scale[..., None]
    return (attn.reshape(count, block_len, width), gate_logits)


def on_device(hidden, w_query, w_key, w_value, w_gate, decay_rate, norm_gain, doc_lengths):
    count, block_len, _ = hidden.shape
    offset = lax.axis_index("ctx") * block_len
    positions = offset + lax.iota(jnp.int32, block_len)
    documents = doc_numbers(positions, doc_lengths)
    before = doc_numbers(jnp.reshape(offset - 1, (1,)), doc_lengths)[:, 0]
    weights = (w_query, w_key, w_value, w_gate)
    attn, gate_logits = attend(hidden, documents, before, weights, decay_rate)
    squares = jnp.sum(attn * attn, axis=2)
    totals = lax.psum(squares, "tp")
    width_all = attn.shape[2] * lax.axis_size("tp")
    scale = lax.rsqrt(totals / width_all + epsilon)
    return (attn * scale[:, :, None] * norm_gain * jax.nn.sigmoid(gate_logits)).astype(jnp.bfloat16)


def solution(mesh):
    in_specs = (
        P(None, "ctx", "tp"),
        P(None, "tp"),
        P(None, "tp"),
        P(None, "tp"),
        P(None, "tp"),
        P("tp"),
        P("tp"),
        P(),
    )
    out_specs = P(None, "ctx", "tp")
    return jax.shard_map(
        on_device, mesh=mesh, in_specs=in_specs, out_specs=out_specs, check_vma=False
    )
```

profile of v0, /device:TPU:0, one launch (start us, length us, event | category | flops | bytes accessed | tf_op | source)
XLA Modules:
  0.0 295.1 jit_solution(16731799409616458674)
XLA Ops:
  9.4 100.9 %all-gather.2.cloned.1.call-done = bf16[4,256,6144]{2,1,0:T(8,128)(2,1)} async-done(((bf16[4,256,384]{2,1,0:T(8,128)(2,1)}), bf16[4,256,6144]{2,1,0:T(8,128)(2,1)}) %all-gather.2.cloned.1.call-update) | async-done | bytes 12582928 | tf_op jit(solution)/shard_map/all_gather | solution.py:64
  110.3 11.7 %multiply_convert_fusion.4 = bf16[1024,512]{1,0:T(8,128)(2,1)S(1)} fusion(bf16[1024,6144]{1,0:T(8,128)(2,1)} %bitcast.23, bf16[6144,512]{1,0:T(8,128)(2,1)} %param.11), kind=kOutput, calls=%fused_computation.10 | convolution fusion | flops 6445072384 | bytes 19922944 | tf_op jit(solution)/shard_map/dot_general | solution.py:67
  122.3 11.8 %multiply_convert_fusion.2 = bf16[1024,512]{1,0:T(8,128)(2,1)S(1)} fusion(bf16[1024,6144]{1,0:T(8,128)(2,1)} %bitcast.24, bf16[6144,512]{1,0:T(8,128)(2,1)} %param.10), kind=kOutput, calls=%fused_computation.8 | convolution fusion | flops 6445072384 | bytes 19922944 | tf_op jit(solution)/shard_map/dot_general | solution.py:67
  136.3 4.2 %collective-permute-start = (bf16[4,4,128,128]{3,2,1,0:T(8,128)(2,1)}, bf16[4,4,128,128]{3,2,1,0:T(8,128)(2,1)}, u32[]{:S(2)}, u32[]{:S(2)}) collective-permute-start(bf16[4,4,128,128]{3,2,1,0:T(8,128)(2,1)} %get-tuple-element.13), channel_id=1, source_target_pairs={{0,16},{16,32},{32,48},{48,64},{64,80},{80,96},{96,112},{1,17},{17... | collective-permute-start | bytes 1572872 | tf_op jit(solution)/shard_map/ppermute | solution.py:12
  140.8 10.7 %collective-permute-done = bf16[4,4,128,128]{3,2,1,0:T(8,128)(2,1)} collective-permute-done((bf16[4,4,128,128]{3,2,1,0:T(8,128)(2,1)}, bf16[4,4,128,128]{3,2,1,0:T(8,128)(2,1)}, u32[]{:S(2)}, u32[]{:S(2)}) %collective-permute-start) | collective-permute-done | bytes 524320 | tf_op jit(solution)/shard_map/ppermute | solution.py:12
  151.5 1.4 add_convert_fusion.5
  152.9 4.5 %collective-permute-start.1 = (bf16[4,4,128,128]{3,2,1,0:T(8,128)(2,1)S(1)}, bf16[4,4,128,128]{3,2,1,0:T(8,128)(2,1)S(1)}, u32[]{:S(2)}, u32[]{:S(2)}) collective-permute-start(bf16[4,4,128,128]{3,2,1,0:T(8,128)(2,1)S(1)} %add_convert_fusion.5), channel_id=1, source_target_pairs={{0,16},{16,32},{32,48},{48,64},{64,80},{80,96},{96,112},{1,17},{17... | collective-permute-start | bytes 1572872 | tf_op jit(solution)/shard_map/ppermute | solution.py:12
  157.5 10.7 %collective-permute-done.1 = bf16[4,4,128,128]{3,2,1,0:T(8,128)(2,1)S(1)} collective-permute-done((bf16[4,4,128,128]{3,2,1,0:T(8,128)(2,1)S(1)}, bf16[4,4,128,128]{3,2,1,0:T(8,128)(2,1)S(1)}, u32[]{:S(2)}, u32[]{:S(2)}) %collective-permute-start.1) | collective-permute-done | bytes 524320 | tf_op jit(solution)/shard_map/ppermute | solution.py:12
  168.5 4.5 %collective-permute-start.2 = (bf16[4,4,128,128]{3,2,1,0:T(8,128)(2,1)S(1)}, bf16[4,4,128,128]{3,2,1,0:T(8,128)(2,1)S(1)}, u32[]{:S(2)}, u32[]{:S(2)}) collective-permute-start(bf16[4,4,128,128]{3,2,1,0:T(8,128)(2,1)S(1)} %add_convert_fusion.4), channel_id=1, source_target_pairs={{0,16},{16,32},{32,48},{48,64},{64,80},{80,96},{96,112},{1,17},{17... | collective-permute-start | bytes 1572872 | tf_op jit(solution)/shard_map/ppermute | solution.py:12
  173.0 9.8 %collective-permute-done.2 = bf16[4,4,128,128]{3,2,1,0:T(8,128)(2,1)S(1)} collective-permute-done((bf16[4,4,128,128]{3,2,1,0:T(8,128)(2,1)S(1)}, bf16[4,4,128,128]{3,2,1,0:T(8,128)(2,1)S(1)}, u32[]{:S(2)}, u32[]{:S(2)}) %collective-permute-start.2) | collective-permute-done | bytes 524320 | tf_op jit(solution)/shard_map/ppermute | solution.py:12
  183.0 4.4 %collective-permute-start.3 = (bf16[4,4,128,128]{3,2,1,0:T(8,128)(2,1)S(1)}, bf16[4,4,128,128]{3,2,1,0:T(8,128)(2,1)S(1)}, u32[]{:S(2)}, u32[]{:S(2)}) collective-permute-start(bf16[4,4,128,128]{3,2,1,0:T(8,128)(2,1)S(1)} %add_convert_fusion.3), channel_id=1, source_target_pairs={{0,16},{16,32},{32,48},{48,64},{64,80},{80,96},{96,112},{1,17},{17... | collective-permute-start | bytes 1572872 | tf_op jit(solution)/shard_map/ppermute | solution.py:12
  187.5 8.8 %collective-permute-done.3 = bf16[4,4,128,128]{3,2,1,0:T(8,128)(2,1)S(1)} collective-permute-done((bf16[4,4,128,128]{3,2,1,0:T(8,128)(2,1)S(1)}, bf16[4,4,128,128]{3,2,1,0:T(8,128)(2,1)S(1)}, u32[]{:S(2)}, u32[]{:S(2)}) %collective-permute-start.3) | collective-permute-done | bytes 524320 | tf_op jit(solution)/shard_map/ppermute | solution.py:12
  196.6 4.4 %collective-permute-start.4 = (bf16[4,4,128,128]{3,2,1,0:T(8,128)(2,1)S(1)}, bf16[4,4,128,128]{3,2,1,0:T(8,128)(2,1)S(1)}, u32[]{:S(2)}, u32[]{:S(2)}) collective-permute-start(bf16[4,4,128,128]{3,2,1,0:T(8,128)(2,1)S(1)} %add_convert_fusion.2), channel_id=1, source_target_pairs={{0,16},{16,32},{32,48},{48,64},{64,80},{80,96},{96,112},{1,17},{17... | collective-permute-start | bytes 1572872 | tf_op jit(solution)/shard_map/ppermute | solution.py:12
  202.6 6.4 %collective-permute-done.4 = bf16[4,4,128,128]{3,2,1,0:T(8,128)(2,1)S(1)} collective-permute-done((bf16[4,4,128,128]{3,2,1,0:T(8,128)(2,1)S(1)}, bf16[4,4,128,128]{3,2,1,0:T(8,128)(2,1)S(1)}, u32[]{:S(2)}, u32[]{:S(2)}) %collective-permute-start.4) | collective-permute-done | bytes 524320 | tf_op jit(solution)/shard_map/ppermute | solution.py:12
  209.2 4.8 %collective-permute-start.5 = (bf16[4,4,128,128]{3,2,1,0:T(8,128)(2,1)S(1)}, bf16[4,4,128,128]{3,2,1,0:T(8,128)(2,1)S(1)}, u32[]{:S(2)}, u32[]{:S(2)}) collective-permute-start(bf16[4,4,128,128]{3,2,1,0:T(8,128)(2,1)S(1)} %add_convert_fusion.1), channel_id=1, source_target_pairs={{0,16},{16,32},{32,48},{48,64},{64,80},{80,96},{96,112},{1,17},{17... | collective-permute-start | bytes 1572872 | tf_op jit(solution)/shard_map/ppermute | solution.py:12
  214.1 11.1 %multiply_convert_fusion.3 = bf16[1024,512]{1,0:T(8,128)(2,1)} fusion(bf16[1024,6144]{1,0:T(8,128)(2,1)} %bitcast.25, bf16[6144,512]{1,0:T(8,128)(2,1)S(1)} %bitcast.29), kind=kOutput, calls=%fused_computation.9 | convolution fusion | flops 6445072384 | bytes 19922944 | tf_op jit(solution)/shard_map/dot_general | solution.py:67
  226.2 6.8 %collective-permute-start.6 = (bf16[4,4,128,128]{3,2,1,0:T(8,128)(2,1)}, bf16[4,4,128,128]{3,2,1,0:T(8,128)(2,1)}, u32[]{:S(2)}, u32[]{:S(2)}) collective-permute-start(bf16[4,4,128,128]{3,2,1,0:T(8,128)(2,1)} %add_convert_fusion), channel_id=1, source_target_pairs={{0,16},{16,32},{32,48},{48,64},{64,80},{80,96},{96,112},{1,17},{17... | collective-permute-start | bytes 1572872 | tf_op jit(solution)/shard_map/ppermute | solution.py:12
  233.1 8.0 %fusion = f32[4,256,512]{2,1,0:T(8,128)} fusion(bf16[4,256,6144]{2,1,0:T(8,128)(2,1)S(1)} %bitcast.27, bf16[6144,512]{1,0:T(8,128)(2,1)S(1)} %bitcast.31), kind=kOutput, calls=%fused_computation | convolution fusion | flops 6442450944 | bytes 20971520 | tf_op jit(solution)/shard_map/dot_general | solution.py:67
  241.1 1.3 reshape.200
  242.4 3.9 %fusion.3 = f32[4,4,128,256]{3,2,1,0:T(8,128)} fusion(bf16[4,256,4,128]{1,3,2,0:T(8,128)(2,1)S(1)} %copy.32, f32[4,256,256]{2,1,0:T(8,128)} %multiply_exponential_fusion, pred[4,256,256]{2,1,0:T(8,128)(4,1)S(1)} %compare_and_fusion, bf16[4,256,4,128]{3,2,1,0:T(4,128)(2,1)S(1)} %reshape.199, bf16[4,256,4,128]{3,2,1,0:T(4,128)(2,1)S(1)} %reshape.200), kind=kOutput, calls=%fused_computation.11 | convolution fusion | flops 540016640 | bytes 6553600 | tf_op jit(solution)/shard_map/shij,sjhe->sihe/dot_general | solution.py:30
  246.3 3.6 %multiply_reduce_fusion = (f32[4,256]{1,0:T(4,128)S(1)}, f32[4,256,4,128]{1,3,2,0:T(8,128)}) fusion(f32[4,256,4]{1,2,0:T(4,128)S(1)} %broadcast_multiply_fusion, bf16[4,4,128,128]{3,2,1,0:T(8,128)(2,1)} %collective-permute-done.6, bf16[4,256,4,128]{3,2,1,0:T(4,128)(2,1)S(1)} %reshape.200, f32[4,4,128,256]{3,2,1,0:T(8,128)} %fusion.3), kind=kOutput, calls=%fused_computation.6 | convolution fusion | flops 136313856 | bytes 5787648 | tf_op jit(solution)/shard_map/sihe,shef->sihf/dot_general | solution.py:78
  249.9 1.9 copy.36
  251.9 33.2 %psum.7 = f32[4,256]{1,0:T(4,128)S(1)} all-reduce(f32[4,256]{1,0:T(4,128)S(1)} %get-tuple-element.15), channel_id=1, replica_groups=mesh['ctx'=8,'tp'=16] {'tp'}, use_global_device_ids=true, to_apply=%region_4.5 | all-reduce | flops 1024 | bytes 8192 | tf_op jit(solution)/shard_map/psum | solution.py:94
  285.1 3.2 %multiply_convert_fusion = bf16[4,256,512]{2,1,0:T(8,128)(2,1)} fusion(f32[4,256,512]{2,1,0:T(8,128)} %fusion, f32[4,256,512]{2,1,0:T(8,128)S(1)} %copy.36, f32[512]{0:T(512)S(1)} %copy-done, f32[4,256]{1,0:T(4,128)S(1)} %add_rsqrt_fusion), kind=kLoop, calls=%fused_computation.5 | loop fusion | flops 3670016 | bytes 5249024 | tf_op jit(solution)/shard_map/convert_element_type | solution.py:97
  (52 shorter events, 9.1 us)
Async XLA Ops:
  6.5 103.8 %all-gather.2.cloned.1.call-start = ((), (), s32[]{:S(2)}) async-start(), calls=%async_computation | async-start | bytes 13369344 | tf_op jit(solution)/shard_map/all_gather | solution.py:64
  136.3 15.3 %collective-permute-start = (bf16[4,4,128,128]{3,2,1,0:T(8,128)(2,1)}, bf16[4,4,128,128]{3,2,1,0:T(8,128)(2,1)}, u32[]{:S(2)}, u32[]{:S(2)}) collective-permute-start(bf16[4,4,128,128]{3,2,1,0:T(8,128)(2,1)} %get-tuple-element.13), channel_id=1, source_target_pairs={{0,16},{16,32},{32,48},{48,64},{64,80},{80,96},{96,112},{1,17},{17... | collective-permute-start | bytes 1572872 | tf_op jit(solution)/shard_map/ppermute | solution.py:12
  151.5 62.5 %slice-start.3 = ((s8[6291456]{0:T(1024)(128)(4,1)}), s8[4194304]{0:T(1024)(128)(4,1)S(1)}, s32[]{:S(2)}) async-start(s8[6291456]{0:T(1024)(128)(4,1)} %bitcast.28), calls=%async_computation.4 | async-start | bytes 8388608
  152.9 15.3 %collective-permute-start.1 = (bf16[4,4,128,128]{3,2,1,0:T(8,128)(2,1)S(1)}, bf16[4,4,128,128]{3,2,1,0:T(8,128)(2,1)S(1)}, u32[]{:S(2)}, u32[]{:S(2)}) collective-permute-start(bf16[4,4,128,128]{3,2,1,0:T(8,128)(2,1)S(1)} %add_convert_fusion.5), channel_id=1, source_target_pairs={{0,16},{16,32},{32,48},{48,64},{64,80},{80,96},{96,112},{1,17},{17... | collective-permute-start | bytes 1572872 | tf_op jit(solution)/shard_map/ppermute | solution.py:12
  168.4 45.6 %slice-start.4 = ((s8[6291456]{0:T(1024)(128)(4,1)}), s8[2097152]{0:T(1024)(128)(4,1)S(1)}, s32[]{:S(2)}) async-start(s8[6291456]{0:T(1024)(128)(4,1)} %bitcast.28), calls=%async_computation.5 | async-start | bytes 4194304
  168.5 14.4 %collective-permute-start.2 = (bf16[4,4,128,128]{3,2,1,0:T(8,128)(2,1)S(1)}, bf16[4,4,128,128]{3,2,1,0:T(8,128)(2,1)S(1)}, u32[]{:S(2)}, u32[]{:S(2)}) collective-permute-start(bf16[4,4,128,128]{3,2,1,0:T(8,128)(2,1)S(1)} %add_convert_fusion.4), channel_id=1, source_target_pairs={{0,16},{16,32},{32,48},{48,64},{64,80},{80,96},{96,112},{1,17},{17... | collective-permute-start | bytes 1572872 | tf_op jit(solution)/shard_map/ppermute | solution.py:12
  183.0 13.3 %collective-permute-start.3 = (bf16[4,4,128,128]{3,2,1,0:T(8,128)(2,1)S(1)}, bf16[4,4,128,128]{3,2,1,0:T(8,128)(2,1)S(1)}, u32[]{:S(2)}, u32[]{:S(2)}) collective-permute-start(bf16[4,4,128,128]{3,2,1,0:T(8,128)(2,1)S(1)} %add_convert_fusion.3), channel_id=1, source_target_pairs={{0,16},{16,32},{32,48},{48,64},{64,80},{80,96},{96,112},{1,17},{17... | collective-permute-start | bytes 1572872 | tf_op jit(solution)/shard_map/ppermute | solution.py:12
  196.6 12.4 %collective-permute-start.4 = (bf16[4,4,128,128]{3,2,1,0:T(8,128)(2,1)S(1)}, bf16[4,4,128,128]{3,2,1,0:T(8,128)(2,1)S(1)}, u32[]{:S(2)}, u32[]{:S(2)}) collective-permute-start(bf16[4,4,128,128]{3,2,1,0:T(8,128)(2,1)S(1)} %add_convert_fusion.2), channel_id=1, source_target_pairs={{0,16},{16,32},{32,48},{48,64},{64,80},{80,96},{96,112},{1,17},{17... | collective-permute-start | bytes 1572872 | tf_op jit(solution)/shard_map/ppermute | solution.py:12
  209.0 24.1 %slice-start = ((s8[12582912]{0:T(1024)(128)(4,1)}), s8[4194304]{0:T(1024)(128)(4,1)S(1)}, s32[]{:S(2)}) async-start(s8[12582912]{0:T(1024)(128)(4,1)} %bitcast.26), calls=%async_computation.1 | async-start | bytes 8388608
  209.0 24.1 %slice-start.5 = ((s8[6291456]{0:T(1024)(128)(4,1)}), s8[4194304]{0:T(1024)(128)(4,1)S(1)}, s32[]{:S(2)}) async-start(s8[6291456]{0:T(1024)(128)(4,1)} %bitcast.30), calls=%async_computation.6 | async-start | bytes 8388608
  209.2 23.9 %slice-start.1 = ((s8[12582912]{0:T(1024)(128)(4,1)}), s8[4194304]{0:T(1024)(128)(4,1)S(1)}, s32[]{:S(2)}) async-start(s8[12582912]{0:T(1024)(128)(4,1)} %bitcast.26), calls=%async_computation.2 | async-start | bytes 8388608
  209.2 23.9 %slice-start.2 = ((s8[12582912]{0:T(1024)(128)(4,1)}), s8[4194304]{0:T(1024)(128)(4,1)S(1)}, s32[]{:S(2)}) async-start(s8[12582912]{0:T(1024)(128)(4,1)} %bitcast.26), calls=%async_computation.3 | async-start | bytes 8388608
  209.2 23.9 %slice-start.6 = ((s8[6291456]{0:T(1024)(128)(4,1)}), s8[2097152]{0:T(1024)(128)(4,1)S(1)}, s32[]{:S(2)}) async-start(s8[6291456]{0:T(1024)(128)(4,1)} %bitcast.30), calls=%async_computation.7 | async-start | bytes 4194304
  209.2 16.0 %collective-permute-start.5 = (bf16[4,4,128,128]{3,2,1,0:T(8,128)(2,1)S(1)}, bf16[4,4,128,128]{3,2,1,0:T(8,128)(2,1)S(1)}, u32[]{:S(2)}, u32[]{:S(2)}) collective-permute-start(bf16[4,4,128,128]{3,2,1,0:T(8,128)(2,1)S(1)} %add_convert_fusion.1), channel_id=1, source_target_pairs={{0,16},{16,32},{32,48},{48,64},{64,80},{80,96},{96,112},{1,17},{17... | collective-permute-start | bytes 1572872 | tf_op jit(solution)/shard_map/ppermute | solution.py:12
  226.2 20.1 %collective-permute-start.6 = (bf16[4,4,128,128]{3,2,1,0:T(8,128)(2,1)}, bf16[4,4,128,128]{3,2,1,0:T(8,128)(2,1)}, u32[]{:S(2)}, u32[]{:S(2)}) collective-permute-start(bf16[4,4,128,128]{3,2,1,0:T(8,128)(2,1)} %add_convert_fusion), channel_id=1, source_target_pairs={{0,16},{16,32},{32,48},{48,64},{64,80},{80,96},{96,112},{1,17},{17... | collective-permute-start | bytes 1572872 | tf_op jit(solution)/shard_map/ppermute | solution.py:12
  249.9 35.1 %copy-start = (f32[512]{0:T(512)S(1)}, f32[512]{0:T(512)}, u32[]{:S(2)}) copy-start(f32[512]{0:T(512)} %param.14) | copy-start | bytes 6148
Sparse Core Ops, SparseCore 0:
  9.6 100.6 all-gather.1
where the time goes:
time: 301 us; the launch traced here: 295 us
  waiting for transfers between devices  148 us (49%)
  matrix products  51.4 us (17%)
  starting transfers between devices  33.8 us (11%)
  blocking collectives  33.2 us (11%)
  between operations  13.6 us (5%)
  other arithmetic  10.1 us (3%)
  local copies, waits for them, and re-layouts  4.82 us (2%)
    all_gather x1, waiting for transfers between devices, attend(): piece = lax.all_gather(section, 'tp', axis=2, tiled=True)  101 us
    ppermute x7, waiting for transfers between devices, shifted(): return lax.ppermute(block, axis, route)  46.5 us
    dot_general x4, matrix products, attend(): jnp.dot(rows, weight, preferred_element_type=jnp.float32)  42.6 us
    ppermute x7, starting transfers between devices, shifted(): return lax.ppermute(block, axis, route)  33.8 us
    psum x1, blocking collectives, on_device(): totals = lax.psum(squares, 'tp')  33.2 us
  transfers between devices with their start and end apart: 8, of which 6 were waited for; matrix products, arithmetic and copies ran while one was open for 10% of the time, Pallas kernels for 0%

commit v1 on v0

v1 whole, which is shorter than its diff:
```python
import functools

import jax
import jax.numpy as jnp
from jax import lax
from jax.experimental import pallas as pl
from jax.experimental.pallas import tpu as pltpu
from jax.sharding import PartitionSpec as P

EPSILON = 1e-06
BLOCK = 256
HEAD = 128
SHARD = 384
WIDTH = 512
F32 = jnp.float32
BF16 = jnp.bfloat16
ANY = pl.BlockSpec(memory_space=pl.ANY)
SMEM = pl.BlockSpec(memory_space=pltpu.SMEM)
VMEM = pl.BlockSpec(memory_space=pltpu.VMEM)


def tp_route(step):
    route = []
    for y in range(2):
        for z in range(4):
            for c in range(2):
                y2, z2, c2 = step(y, z, c)
                route.append((y * 8 + z * 2 + c, (y2 % 2) * 8 + (z2 % 4) * 2 + c2 % 2))
    return route


RING = tp_route(lambda y, z, c: (y, z + 1 - 2 * c, c))
ACROSS = tp_route(lambda y, z, c: (y + 1, z, c))
CORE = tp_route(lambda y, z, c: (y, z, c + 1))
PAIR_A = tp_route(lambda y, z, c: (y, z ^ 1, c))
PAIR_B = tp_route(lambda y, z, c: (y, 3 - z, c))


def ring(x):
    return lax.ppermute(x, "tp", RING)


def across(x):
    return lax.ppermute(x, "tp", ACROSS)


def other_core(x):
    return lax.ppermute(x, "tp", CORE)


def ahead(x, distance):
    n = lax.axis_size("ctx")
    return lax.ppermute(x, "ctx", [(i, i + distance) for i in range(n - distance)])


def doc_ends(lengths, seq):
    first = lengths[seq, 0]
    second = first + lengths[seq, 1]
    return first, second, second + lengths[seq, 2]


def doc_of(position, ends):
    return sum((position >= end).astype(jnp.int32) for end in ends)


def decay_of(rate, steps):
    return jnp.exp(-rate * steps.astype(F32))


def matmul_kernel(mode, base, n_x, n_w, *refs):
    refs = list(refs)
    take = lambda n: [refs.pop(0) for _ in range(n)]
    ids, place, lengths, decay = take(4)
    xs, ws = take(n_x), take(n_w)
    has_acc = base
    accs = take(n_w) if has_acc else []
    if mode == "qg":
        k_in, v_in, gain = take(3)
    outs = take({"acc": n_w, "kv": 4, "qg": 3}[mode])
    xbuf, wbuf, xsem, wsem = take(4)
    n_k = 2 * n_x

    def x_copy(i):
        return pltpu.make_async_copy(
            xs[i // 2].at[i % 2], xbuf.at[:, pl.ds(i * SHARD, SHARD)], xsem.at[i]
        )

    def w_copy(n, i):
        row = pl.multiple_of(ids[i] * SHARD, SHARD)
        return pltpu.make_async_copy(
            ws[n].at[pl.ds(row, SHARD), :], wbuf.at[n, pl.ds(i * SHARD, SHARD), :], wsem.at[n, i]
        )

    for i in range(n_k):
        x_copy(i).start()
        w_copy(0, i).start()
    for n in range(1, n_w):
        for i in range(n_k):
            w_copy(n, i).start()

    def product(n):
        if n == 0:
            for i in range(n_k):
                x_copy(i).wait()
        for i in range(n_k):
            w_copy(n, i).wait()
        got = jnp.dot(xbuf[...], wbuf[n], preferred_element_type=F32)
        return got + accs[n][...] if has_acc else got

    rows = xbuf.shape[0]
    seqs = rows // BLOCK
    heads = WIDTH // HEAD
    offset = place[0]
    first_seq = place[1]

    def part(s, h):
        return pl.ds(s * BLOCK, BLOCK), pl.ds(h * HEAD, HEAD)

    if mode == "acc":
        for n in range(n_w):
            outs[n][...] = product(n)
    if mode == "kv":
        k_out, v_out, s_out, sb_out = outs
        k_out[...] = jax.nn.silu(product(0)).astype(BF16)
        v_out[...] = jax.nn.silu(product(1)).astype(BF16)
        local = lax.broadcasted_iota(jnp.int32, (BLOCK, HEAD), 0)
        for s in range(seqs):
            ends = doc_ends(lengths, first_seq + s)
            keep = doc_of(local + offset, ends) == doc_of(offset + BLOCK - 1, ends)
            for h in range(heads):
                scale = jnp.where(keep, decay_of(decay[h], BLOCK - 1 - local), 0.0)
                weighted = (k_out[part(s, h)].astype(F32) * scale).astype(BF16)
                state = lax.dot_general(
                    weighted, v_out[part(s, h)], (((0,), (0,)), ((), ())), preferred_element_type=F32
                )
                s_out[s, h] = state
                sb_out[s, h] = state.astype(BF16)
    if mode == "qg":
        q_out, inner_out, gate_out = outs
        q_out[...] = jax.nn.silu(product(0)).astype(BF16)
        gate_out[...] = gain[...] * jax.nn.sigmoid(product(1))
        row = lax.broadcasted_iota(jnp.int32, (BLOCK, BLOCK), 0)
        column = lax.broadcasted_iota(jnp.int32, (BLOCK, BLOCK), 1)
        causal = row >= column
        for h in range(heads):
            pair_decay = decay_of(decay[h], jnp.maximum(row - column, 0))
            for s in range(seqs):
                ends = doc_ends(lengths, first_seq + s)
                same = doc_of(row + offset, ends) == doc_of(column + offset, ends)
                scores = lax.dot_general(
                    q_out[part(s, h)],
                    k_in[part(s, h)],
                    (((1,), (1,)), ((), ())),
                    preferred_element_type=F32,
                )
                allowed = jnp.logical_and(causal, same)
                mixed = jnp.where(allowed, scores * pair_decay, 0.0).astype(BF16)
                inner_out[part(s, h)] = jnp.dot(
                    mixed, v_in[part(s, h)], preferred_element_type=F32
                )


def matmul(mode, scalars, ids, xs, ws, accs=(), extra=()):
    rows = xs[0].shape[1]
    n_x, n_w = len(xs), len(ws)
    seqs, heads = rows // BLOCK, WIDTH // HEAD
    wide = jax.ShapeDtypeStruct((rows, WIDTH), F32)
    half = jax.ShapeDtypeStruct((rows, WIDTH), BF16)
    state = (seqs, heads, HEAD, HEAD)
    outs = {
        "acc": [wide] * n_w,
        "kv": [half, half, jax.ShapeDtypeStruct(state, F32), jax.ShapeDtypeStruct(state, BF16)],
        "qg": [half, wide, wide],
    }[mode]
    k = 2 * n_x * SHARD
    return pl.pallas_call(
        functools.partial(matmul_kernel, mode, bool(accs), n_x, n_w),
        out_shape=outs,
        in_specs=[SMEM] * 4 + [ANY] * (n_x + n_w) + [VMEM] * (len(accs) + len(extra)),
        out_specs=[VMEM] * len(outs),
        scratch_shapes=[
            pltpu.VMEM((rows, k), BF16),
            pltpu.VMEM((n_w, k, WIDTH), BF16),
            pltpu.SemaphoreType.DMA((2 * n_x,)),
            pltpu.SemaphoreType.DMA((n_w, 2 * n_x)),
        ],
        compiler_params=pltpu.CompilerParams(vmem_limit_bytes=48 * 2**20),
        cost_estimate=pl.CostEstimate(
            flops=2 * rows * k * n_w * WIDTH,
            bytes_accessed=2 * k * (rows + n_w * WIDTH) + 4 * rows * n_w * WIDTH,
            transcendentals=0,
        ),
        name="project_" + mode,
    )(ids, *scalars, *xs, *ws, *accs, *extra)


def carried_share(place, lengths, decay, s, h, block):
    ends = doc_ends(lengths, place[1] + s)
    start = place[0] - block * BLOCK
    keep = doc_of(start + BLOCK - 1, ends) == doc_of(start - 1, ends)
    rate = jnp.full((8, HEAD), decay[h] * (-1.0 * BLOCK), F32)
    return jnp.where(keep, jnp.exp(rate), 0.0)[0:1, :]


def extend_kernel(place, lengths, decay, state, before, out):
    for s in range(state.shape[0]):
        for h in range(state.shape[1]):
            share = carried_share(place, lengths, decay, s, h, 0)
            out[s, h] = (state[s, h] + share * before[s, h].astype(F32)).astype(BF16)


def extend(scalars, state, before):
    return pl.pallas_call(
        extend_kernel,
        out_shape=jax.ShapeDtypeStruct(state.shape, BF16),
        in_specs=[SMEM] * 3 + [VMEM] * 2,
        out_specs=VMEM,
        name="extend",
    )(*scalars, state, before)


def combine_kernel(place, lengths, decay, query, inner, near, far, attn_out, squares_out):
    seqs, heads = near.shape[:2]
    offset = place[0]
    local = lax.broadcasted_iota(jnp.int32, (BLOCK, HEAD), 0)
    for s in range(seqs):
        ends = doc_ends(lengths, place[1] + s)
        inside = doc_of(local + offset, ends) == doc_of(offset - 1, ends)
        total = jnp.zeros((BLOCK, HEAD), F32)
        for h in range(heads):
            rows, columns = pl.ds(s * BLOCK, BLOCK), pl.ds(h * HEAD, HEAD)
            share = carried_share(place, lengths, decay, s, h, 1) * carried_share(
                place, lengths, decay, s, h, 2
            )
            incoming = near[s, h].astype(F32) + share * far[s, h].astype(F32)
            high = incoming.astype(BF16)
            low = (incoming - high.astype(F32)).astype(BF16)
            q = query[rows, columns]
            carried = jnp.dot(q, high, preferred_element_type=F32)
            carried = carried + jnp.dot(q, low, preferred_element_type=F32)
            scale = jnp.where(inside, decay_of(decay[h], local + 1), 0.0)
            attn = inner[rows, columns] + carried * scale
            attn_out[rows, columns] = attn
            total = total + attn * attn
        line = jnp.sum(jnp.transpose(total), axis=0, keepdims=True)
        squares_out[:, pl.ds(s * BLOCK, BLOCK)] = jnp.broadcast_to(line, (8, BLOCK))


def combine(scalars, query, inner, near, far):
    rows = query.shape[0]
    return pl.pallas_call(
        combine_kernel,
        out_shape=[
            jax.ShapeDtypeStruct((rows, WIDTH), F32),
            jax.ShapeDtypeStruct((8, rows), F32),
        ],
        in_specs=[SMEM] * 3 + [VMEM] * 4,
        out_specs=[VMEM] * 2,
        name="combine",
    )(*scalars, query, inner, near, far)


def finish_kernel(width_all, attn, gate, squares, *refs):
    out = refs[-1]
    rows = attn.shape[0]
    mean = squares[0:1, :] * (1.0 / width_all)
    scale = jnp.transpose(jnp.broadcast_to(lax.rsqrt(mean + EPSILON), (HEAD, rows)))
    for h in range(WIDTH // HEAD):
        columns = pl.ds(h * HEAD, HEAD)
        got = (attn[:, columns] * scale * gate[:, columns]).astype(BF16)
        out[:, :, columns] = got.reshape(out.shape[0], BLOCK, HEAD)


def finish(attn, gate, squares, seqs, part, so_far=None):
    rows = attn.shape[0]
    count = rows // BLOCK
    width_all = WIDTH * lax.axis_size("tp")
    more = [] if so_far is None else [so_far]
    return pl.pallas_call(
        functools.partial(finish_kernel, width_all),
        grid=(1,),
        out_shape=jax.ShapeDtypeStruct((seqs, BLOCK, WIDTH), BF16),
        in_specs=[
            pl.BlockSpec((rows, WIDTH), lambda i: (0, 0)),
            pl.BlockSpec((rows, WIDTH), lambda i: (0, 0)),
            pl.BlockSpec((8, rows), lambda i: (0, 0)),
        ]
        + [ANY] * len(more),
        out_specs=pl.BlockSpec((count, BLOCK, WIDTH), lambda i: (part, 0, 0)),
        input_output_aliases={3: 0} if more else {},
        name="finish",
    )(attn, gate, squares, *more)


def all_sum(x):
    for route in (CORE, ACROSS, PAIR_A, PAIR_B):
        x = x + lax.ppermute(x, "tp", route)
    return x


def on_device(hidden, w_query, w_key, w_value, w_gate, decay_rate, norm_gain, doc_lengths):
    seqs = hidden.shape[0]
    me = lax.axis_index("tp")
    my_y, my_z, my_c = me // 8, (me // 2) % 4, me % 2
    offset = lax.axis_index("ctx") * BLOCK
    gain = norm_gain.reshape(1, WIDTH)

    def held(flip, j, core):
        y = (my_y + flip) % 2
        c = (my_c + core) % 2
        z = (my_z + j * (2 * c - 1) + 4) % 4
        return y * 8 + z * 2 + c

    half = seqs // 2
    part_y = hidden[:half].reshape(half * BLOCK, SHARD)
    part_z = hidden[half:].reshape(half * BLOCK, SHARD)

    a = [jnp.stack([part_y, across(part_y)])]
    for _ in range(3):
        a.append(ring(a[-1]))
    b = [other_core(x) for x in a]
    r = [part_z]
    for _ in range(3):
        r.append(ring(r[-1]))
    z_near = [jnp.stack(r[:2]), jnp.stack(r[2:])]
    z_far = [across(x) for x in z_near]
    z_near_other = [other_core(x) for x in z_near]
    z_far_other = [other_core(x) for x in z_far]

    def y_ids(steps):
        return jnp.stack([held(f, j, core) for core in (0, 1) for j in steps for f in (0, 1)])

    def z_ids(flip):
        return jnp.stack([held(flip, j, core) for core in (0, 1) for j in range(4)])

    pieces = [
        (
            (a[:2] + b[:2], y_ids((0, 1))),
            (a[2:] + b[2:], y_ids((2, 3))),
        ),
        (
            (z_near + z_near_other, z_ids(0)),
            (z_far + z_far_other, z_ids(1)),
        ),
    ]
    weights = [w_key, w_value, w_query, w_gate]
    out = None
    for part, ((xs1, ids1), (xs2, ids2)) in enumerate(pieces):
        place = jnp.stack([offset, jnp.int32(part * half)])
        scalars = (place, doc_lengths, decay_rate)
        acc = matmul("acc", scalars, ids1, xs1, weights)
        keys, values, state, state_half = matmul("kv", scalars, ids2, xs2, weights[:2], acc[:2])
        before = ahead(state_half, 1)
        query, inner, gate = matmul(
            "qg", scalars, ids2, xs2, weights[2:], acc[2:], (keys, values, gain)
        )
        longer = extend(scalars, state, before)
        near, far = ahead(longer, 1), ahead(longer, 3)
        attn, squares = combine(scalars, query, inner, near, far)
        out = finish(attn, gate, all_sum(squares), seqs, part, out)
    return out


def solution(mesh):
    in_specs = (
        P(None, "ctx", "tp"),
        P(None, "tp"),
        P(None, "tp"),
        P(None, "tp"),
        P(None, "tp"),
        P("tp"),
        P("tp"),
        P(),
    )
    out_specs = P(None, "ctx", "tp")
    return jax.shard_map(
        on_device, mesh=mesh, in_specs=in_specs, out_specs=out_specs, check_vma=False
    )
```

time: 301 us -> 204 us (0.68); the launches traced: 295 us -> 203 us
  waiting for transfers between devices: 148 us -> 59.8 us
  Pallas kernels: 0 us -> 76.6 us
  matrix products: 51.4 us -> 0 us
  blocking collectives: 33.2 us -> 0 us
  between operations: 13.6 us -> 0.52 us
  starting transfers between devices: 33.8 us -> 45.7 us
  local copies, waits for them, and re-layouts: 4.82 us -> 16.1 us
  other arithmetic: 10.1 us -> 4.23 us
    all_gather x1 -> x0, waiting for transfers between devices: 101 us -> none  [attend(): piece = lax.all_gather(section, 'tp', axis=2, tiled=True)]
    pallas_call x0 -> x12, Pallas kernels: none -> 76.6 us  [the longest x6 61.5 us: matmul(): pl.pallas_call(functools.partial(matmul_kernel, mode, bool(accs), n_x, n_...]
    dot_general x7 -> x0, matrix products: 51.4 us -> none  [the longest x4 42.6 us: attend(): jnp.dot(rows, weight, preferred_element_type=jnp.float32)]
    psum x1 -> x0, blocking collectives: 33.2 us -> none  [on_device(): totals = lax.psum(squares, 'tp')]
    unnamed x16 -> x86, local copies, waits for them, and re-layouts: 0.04 us -> 14.5 us
    ppermute x7 -> x31, waiting for transfers between devices: 46.5 us -> 59.8 us  [the longest x3 31 us: across(): return lax.ppermute(x, 'tp', ACROSS)]
    ppermute x7 -> x31, starting transfers between devices: 33.8 us -> 45.7 us  [the longest x6 19.6 us: ahead(): lax.ppermute(x, 'ctx', [(i, i + distance) for i in range(n - distance)])]
    convert_element_type x9 -> x0, other arithmetic: 6.63 us -> none  [the longest x6 3.22 us: hand_off(): outgoing.astype(jnp.bfloat16)]
  transfers between devices with their start and end apart: 8 -> 31, of which waited for: 6 -> 11; matrix products, arithmetic and copies ran while one was open for 10% -> 2% of each run, Pallas kernels for 0% -> 35%
where the time goes in v1:
time: 204 us; the launch traced here: 203 us
  Pallas kernels  76.6 us (38%)
  waiting for transfers between devices  59.8 us (29%)
  starting transfers between devices  45.7 us (22%)
  local copies, waits for them, and re-layouts  16.1 us (8%)
  other arithmetic  4.23 us (2%)
    pallas_call x6, Pallas kernels, matmul(): pl.pallas_call(functools.partial(matmul_kernel, mode, bool(accs), n_x, n_...  61.5 us
    ppermute x3, waiting for transfers between devices, across(): return lax.ppermute(x, 'tp', ACROSS)  31 us
    ppermute x6, starting transfers between devices, ahead(): lax.ppermute(x, 'ctx', [(i, i + distance) for i in range(n - distance)])  19.6 us
    ppermute x6, waiting for transfers between devices, ring(): return lax.ppermute(x, 'tp', RING)  17.3 us
    unnamed x86, local copies, waits for them, and re-layouts  14.5 us
    ppermute x8, waiting for transfers between devices, all_sum(): x = x + lax.ppermute(x, 'tp', route)  11.5 us
    ppermute x3, starting transfers between devices, across(): return lax.ppermute(x, 'tp', ACROSS)  9.75 us
    ppermute x6, starting transfers between devices, ring(): return lax.ppermute(x, 'tp', RING)  9.7 us
  transfers between devices with their start and end apart: 31, of which 11 were waited for; matrix products, arithmetic and copies ran while one was open for 2% of the time, Pallas kernels for 35%

profile of v1, /device:TPU:0, one launch (start us, length us, event | category | flops | bytes accessed | tf_op | source)
XLA Modules:
  0.0 202.9 jit_solution(7749905746049435555)
XLA Ops:
  1.2 3.4 %collective-permute-start.16 = (bf16[512,384]{1,0:T(8,128)(2,1)S(1)}, bf16[512,384]{1,0:T(8,128)(2,1)S(1)}, u32[]{:S(2)}, u32[]{:S(2)}) collective-permute-start(bf16[512,384]{1,0:T(8,128)(2,1)S(1)} %bitcast.30), channel_id=1, source_target_pairs={{0,8},{1,9},{2,10},{3,11},{4,12},{5,13},{6,14},{7,15},{8,0},{9,1},... | collective-permute-start | bytes 1179656 | tf_op jit(solution)/shard_map/ppermute | solution.py:44
  6.5 7.2 %collective-permute-done.16 = bf16[512,384]{1,0:T(8,128)(2,1)S(1)} collective-permute-done((bf16[512,384]{1,0:T(8,128)(2,1)S(1)}, bf16[512,384]{1,0:T(8,128)(2,1)S(1)}, u32[]{:S(2)}, u32[]{:S(2)}) %collective-permute-start.16) | collective-permute-done | bytes 393248 | tf_op jit(solution)/shard_map/ppermute | solution.py:44
  17.8 14.4 %collective-permute-done.2 = bf16[512,384]{1,0:T(8,128)(2,1)S(1)} collective-permute-done((bf16[512,384]{1,0:T(8,128)(2,1)S(1)}, bf16[512,384]{1,0:T(8,128)(2,1)S(1)}, u32[]{:S(2)}, u32[]{:S(2)}) %collective-permute-start.2) | collective-permute-done | bytes 393248 | tf_op jit(solution)/shard_map/ppermute | solution.py:40
  33.2 3.2 %collective-permute-start.1 = (bf16[2,512,384]{2,1,0:T(8,128)(2,1)}, bf16[2,512,384]{2,1,0:T(8,128)(2,1)S(1)}, u32[]{:S(2)}, u32[]{:S(2)}) collective-permute-start(bf16[2,512,384]{2,1,0:T(8,128)(2,1)} %pad_maximum_fusion.refs_4_), channel_id=1, source_target_pairs={{0,8},{1,9},{2,10},{3,11},{4,12},{5,13},{6,14},{7,15},{8,0},{9,1},... | collective-permute-start | bytes 2359304 | tf_op jit(solution)/shard_map/ppermute | solution.py:44
  38.2 2.9 %collective-permute-done.3 = bf16[512,384]{1,0:T(8,128)(2,1)S(1)} collective-permute-done((bf16[512,384]{1,0:T(8,128)(2,1)S(1)}, bf16[512,384]{1,0:T(8,128)(2,1)S(1)}, u32[]{:S(2)}, u32[]{:S(2)}) %collective-permute-start.3) | collective-permute-done | bytes 393248 | tf_op jit(solution)/shard_map/ppermute | solution.py:40
  42.1 3.2 %collective-permute-start.4 = (bf16[2,512,384]{2,1,0:T(8,128)(2,1)}, bf16[2,512,384]{2,1,0:T(8,128)(2,1)S(1)}, u32[]{:S(2)}, u32[]{:S(2)}) collective-permute-start(bf16[2,512,384]{2,1,0:T(8,128)(2,1)} %pad_maximum_fusion.1.refs_5_), channel_id=1, source_target_pairs={{0,8},{1,9},{2,10},{3,11},{4,12},{5,13},{6,14},{7,15},{8,0},{9,1},... | collective-permute-start | bytes 2359304 | tf_op jit(solution)/shard_map/ppermute | solution.py:44
  46.2 9.1 %collective-permute-done.1.refs_4_ = bf16[2,512,384]{2,1,0:T(8,128)(2,1)S(1)} collective-permute-done((bf16[2,512,384]{2,1,0:T(8,128)(2,1)}, bf16[2,512,384]{2,1,0:T(8,128)(2,1)S(1)}, u32[]{:S(2)}, u32[]{:S(2)}) %collective-permute-start.1) | collective-permute-done | bytes 786464 | tf_op jit(solution)/shard_map/ppermute | solution.py:44
  57.3 14.7 %collective-permute-done.4.refs_5_ = bf16[2,512,384]{2,1,0:T(8,128)(2,1)S(1)} collective-permute-done((bf16[2,512,384]{2,1,0:T(8,128)(2,1)}, bf16[2,512,384]{2,1,0:T(8,128)(2,1)S(1)}, u32[]{:S(2)}, u32[]{:S(2)}) %collective-permute-start.4) | collective-permute-done | bytes 786464 | tf_op jit(solution)/shard_map/ppermute | solution.py:44
  72.7 14.5 %project_acc.2 = (f32[512,512]{1,0:T(8,128)S(1)}, f32[512,512]{1,0:T(8,128)S(1)}, f32[512,512]{1,0:T(8,128)}, f32[512,512]{1,0:T(8,128)}) custom-call(s32[8]{0:T(128)S(1)} %stack.131.refs_0_, s32[2]{0:T(128)S(1)} %pad_add_fusion.refs_1_.place, s32[4,4]{1,0:T(4,128)S(1)} %copy-done.26, f32[4]{0:T(128)S(1)} %copy-done.29, ...), custom_call_target="tpu_custom_call" | custom-call | flops 6442450944 | bytes 19922944 | tf_op jit(solution)/shard_map/project_acc/pallas_call | solution.py:176
  88.9 8.0 %project_kv.2 = (bf16[512,512]{1,0:T(8,128)(2,1)S(1)}, bf16[512,512]{1,0:T(8,128)(2,1)S(1)}, f32[2,4,128,128]{3,2,1,0:T(8,128)S(1)}, bf16[2,4,128,128]{3,2,1,0:T(8,128)(2,1)S(1)}) custom-call(s32[8]{0:T(128)S(1)} %stack.117.refs_0_, s32[2]{0:T(128)S(1)} %pad_add_fusion.refs_1_.place, s32[4,4]{1,0:T(4,128)S(1)} %copy-done.26, f32[4]{0:T(128)S(1)} %copy-done.29, ...), custom_call_target="tpu_custom_call" | custom-call | flops 3221225472 | bytes 11534336 | tf_op jit(solution)/shard_map/project_kv/pallas_call | solution.py:176
  97.0 3.5 %collective-permute-start.9 = (bf16[2,4,128,128]{3,2,1,0:T(8,128)(2,1)S(1)}, bf16[2,4,128,128]{3,2,1,0:T(8,128)(2,1)S(1)}, u32[]{:S(2)}, u32[]{:S(2)}) collective-permute-start(bf16[2,4,128,128]{3,2,1,0:T(8,128)(2,1)S(1)} %get-tuple-element.40), channel_id=1, source_target_pairs={{0,16},{16,32},{32,48},{48,64},{64,80},{80,96},{96,112},{1,17},{17... | collective-permute-start | bytes 786440 | tf_op jit(solution)/shard_map/ppermute | solution.py:53
  100.6 11.1 %project_acc.3 = (f32[512,512]{1,0:T(8,128)S(1)}, f32[512,512]{1,0:T(8,128)S(1)}, f32[512,512]{1,0:T(8,128)}, f32[512,512]{1,0:T(8,128)}) custom-call(s32[8]{0:T(128)S(1)} %stack.136.refs_0_, s32[2]{0:T(128)S(1)} %pad_add_fusion.1.refs_1_.place, s32[4,4]{1,0:T(4,128)S(1)} %copy-done.26, f32[4]{0:T(128)S(1)} %copy-done.29, ...), custom_call_target="tpu_custom_call" | custom-call | flops 6442450944 | bytes 19922944 | tf_op jit(solution)/shard_map/project_acc/pallas_call | solution.py:176
  116.3 3.4 %collective-permute-start.10 = (bf16[2,4,128,128]{3,2,1,0:T(8,128)(2,1)}, bf16[2,4,128,128]{3,2,1,0:T(8,128)(2,1)S(1)}, u32[]{:S(2)}, u32[]{:S(2)}) collective-permute-start(bf16[2,4,128,128]{3,2,1,0:T(8,128)(2,1)} %extend.2), channel_id=1, source_target_pairs={{0,16},{16,32},{32,48},{48,64},{64,80},{80,96},{96,112},{1,17},{17... | collective-permute-start | bytes 786440 | tf_op jit(solution)/shard_map/ppermute | solution.py:53
  119.7 4.7 %collective-permute-start.11 = (bf16[2,4,128,128]{3,2,1,0:T(8,128)(2,1)}, bf16[2,4,128,128]{3,2,1,0:T(8,128)(2,1)S(1)}, u32[]{:S(2)}, u32[]{:S(2)}) collective-permute-start(bf16[2,4,128,128]{3,2,1,0:T(8,128)(2,1)} %extend.2), channel_id=1, source_target_pairs={{0,48},{16,64},{32,80},{48,96},{64,112},{1,49},{17,65},{33,81},{49... | collective-permute-start | bytes 786440 | tf_op jit(solution)/shard_map/ppermute | solution.py:53
  125.7 9.0 %project_kv.3 = (bf16[512,512]{1,0:T(8,128)(2,1)S(1)}, bf16[512,512]{1,0:T(8,128)(2,1)S(1)}, f32[2,4,128,128]{3,2,1,0:T(8,128)S(1)}, bf16[2,4,128,128]{3,2,1,0:T(8,128)(2,1)S(1)}) custom-call(s32[8]{0:T(128)S(1)} %stack.133.refs_0_, s32[2]{0:T(128)S(1)} %pad_add_fusion.1.refs_1_.place, s32[4,4]{1,0:T(4,128)S(1)} %copy-done.27, f32[4]{0:T(128)S(1)} %copy-done.30, ...), custom_call_target="tpu_custom_call" | custom-call | flops 3221225472 | bytes 11534336 | tf_op jit(solution)/shard_map/project_kv/pallas_call | solution.py:176
  136.4 2.9 %collective-permute-start.24 = (bf16[2,4,128,128]{3,2,1,0:T(8,128)(2,1)S(1)}, bf16[2,4,128,128]{3,2,1,0:T(8,128)(2,1)}, u32[]{:S(2)}, u32[]{:S(2)}) collective-permute-start(bf16[2,4,128,128]{3,2,1,0:T(8,128)(2,1)S(1)} %get-tuple-element.53), channel_id=1, source_target_pairs={{0,16},{16,32},{32,48},{48,64},{64,80},{80,96},{96,112},{1,17},{17... | collective-permute-start | bytes 786440 | tf_op jit(solution)/shard_map/ppermute | solution.py:53
  139.3 8.9 %project_qg.2 = (bf16[512,512]{1,0:T(8,128)(2,1)S(1)}, f32[512,512]{1,0:T(8,128)S(1)}, f32[512,512]{1,0:T(8,128)}) custom-call(s32[8]{0:T(128)S(1)} %stack.117.refs_0_, s32[2]{0:T(128)S(1)} %copy-done.35, s32[4,4]{1,0:T(4,128)S(1)} %copy-done.27, f32[4]{0:T(128)S(1)} %copy-done.30, bf16[2,512,384]{2,1,0:T(8,128)(2,1)S(1)} %collective-permute-done.1.refs_4_, ...), custom_call_target="tpu_custom_call" | custom-call | flops 3221225472 | bytes 11534336 | tf_op jit(solution)/shard_map/project_qg/pallas_call | solution.py:176
  151.5 3.1 %combine.2 = (f32[512,512]{1,0:T(8,128)}, f32[8,512]{1,0:T(8,128)}) custom-call(s32[2]{0:T(128)} %copy-done.34, s32[4,4]{1,0:T(4,128)} %lengths.7, f32[4]{0:T(128)} %decay.7, bf16[512,512]{1,0:T(8,128)(2,1)} %copy-done.22, f32[512,512]{1,0:T(8,128)} %copy-done.10, bf16[2,4,128,128]{3,2,1,0:T(8,128)(2,1)} %copy-done.37, bf16[2,4,128,128]{3,2,1,0:T(8,128)(2,1)} %copy-done.38), custom_call_target="tpu_custom_call" | custom-call | tf_op jit(solution)/shard_map/combine/pallas_call | solution.py:251
  163.8 10.1 %project_qg.3 = (bf16[512,512]{1,0:T(8,128)(2,1)S(1)}, f32[512,512]{1,0:T(8,128)S(1)}, f32[512,512]{1,0:T(8,128)}) custom-call(s32[8]{0:T(128)S(1)} %stack.133.refs_0_, s32[2]{0:T(128)S(1)} %copy-done.33, s32[4,4]{1,0:T(4,128)S(1)} %copy-done.28, f32[4]{0:T(128)S(1)} %copy-done.31, bf16[2,512,384]{2,1,0:T(8,128)(2,1)S(1)} %collective-permute-done.18.refs_4_, ...), custom_call_target="tpu_custom_call" | custom-call | flops 3221225472 | bytes 11534336 | tf_op jit(solution)/shard_map/project_qg/pallas_call | solution.py:176
  176.5 3.1 %combine.3 = (f32[512,512]{1,0:T(8,128)}, f32[8,512]{1,0:T(8,128)}) custom-call(s32[2]{0:T(128)} %copy-done.32, s32[4,4]{1,0:T(4,128)} %lengths.7, f32[4]{0:T(128)} %decay.7, bf16[512,512]{1,0:T(8,128)(2,1)} %copy-done.23, f32[512,512]{1,0:T(8,128)} %copy-done.11, bf16[2,4,128,128]{3,2,1,0:T(8,128)(2,1)} %copy-done.39, bf16[2,4,128,128]{3,2,1,0:T(8,128)(2,1)} %copy-done.40), custom_call_target="tpu_custom_call" | custom-call | tf_op jit(solution)/shard_map/combine/pallas_call | solution.py:251
  179.6 3.0 %collective-permute-start.13 = (f32[8,512]{1,0:T(8,128)S(1)}, f32[8,512]{1,0:T(8,128)S(1)}, u32[]{:S(2)}, u32[]{:S(2)}) collective-permute-start(f32[8,512]{1,0:T(8,128)S(1)} %add.453), channel_id=1, source_target_pairs={{0,8},{1,9},{2,10},{3,11},{4,12},{5,13},{6,14},{7,15},{8,0},{9,1},... | collective-permute-start | bytes 49160 | tf_op jit(solution)/shard_map/ppermute | solution.py:297
  184.9 3.6 %collective-permute-done.28 = f32[8,512]{1,0:T(8,128)S(1)} collective-permute-done((f32[8,512]{1,0:T(8,128)S(1)}, f32[8,512]{1,0:T(8,128)S(1)}, u32[]{:S(2)}, u32[]{:S(2)}) %collective-permute-start.28) | collective-permute-done | bytes 16416 | tf_op jit(solution)/shard_map/ppermute | solution.py:297
  189.0 3.3 %collective-permute-done.29 = f32[8,512]{1,0:T(8,128)S(1)} collective-permute-done((f32[8,512]{1,0:T(8,128)S(1)}, f32[8,512]{1,0:T(8,128)S(1)}, u32[]{:S(2)}, u32[]{:S(2)}) %collective-permute-start.29) | collective-permute-done | bytes 16416 | tf_op jit(solution)/shard_map/ppermute | solution.py:297
  194.2 3.0 %collective-permute-done.30 = f32[8,512]{1,0:T(8,128)S(1)} collective-permute-done((f32[8,512]{1,0:T(8,128)S(1)}, f32[8,512]{1,0:T(8,128)S(1)}, u32[]{:S(2)}, u32[]{:S(2)}) %collective-permute-start.30) | collective-permute-done | bytes 16416 | tf_op jit(solution)/shard_map/ppermute | solution.py:297
  (154 shorter events, 49.2 us)
Async XLA Ops:
  1.2 12.5 %collective-permute-start.16 = (bf16[512,384]{1,0:T(8,128)(2,1)S(1)}, bf16[512,384]{1,0:T(8,128)(2,1)S(1)}, u32[]{:S(2)}, u32[]{:S(2)}) collective-permute-start(bf16[512,384]{1,0:T(8,128)(2,1)S(1)} %bitcast.30), channel_id=1, source_target_pairs={{0,8},{1,9},{2,10},{3,11},{4,12},{5,13},{6,14},{7,15},{8,0},{9,1},... | collective-permute-start | bytes 1179656 | tf_op jit(solution)/shard_map/ppermute | solution.py:44
  4.6 11.3 %collective-permute-start = (bf16[512,384]{1,0:T(8,128)(2,1)S(1)}, bf16[512,384]{1,0:T(8,128)(2,1)S(1)}, u32[]{:S(2)}, u32[]{:S(2)}) collective-permute-start(bf16[512,384]{1,0:T(8,128)(2,1)S(1)} %bitcast.28), channel_id=1, source_target_pairs={{0,2},{1,7},{2,4},{3,1},{4,6},{5,3},{6,0},{7,5},{8,10},{9,15},{10,... | collective-permute-start | bytes 1179656 | tf_op jit(solution)/shard_map/ppermute | solution.py:40
  13.8 22.6 %collective-permute-start.17 = (bf16[2,512,384]{2,1,0:T(8,128)(2,1)S(1)}, bf16[2,512,384]{2,1,0:T(8,128)(2,1)S(1)}, u32[]{:S(2)}, u32[]{:S(2)}) collective-permute-start(bf16[2,512,384]{2,1,0:T(8,128)(2,1)S(1)} %pad_maximum_fusion.2.refs_4_), channel_id=1, source_target_pairs={{0,2},{1,7},{2,4},{3,1},{4,6},{5,3},{6,0},{7,5},{8,10},{9,15},{10,... | collective-permute-start | bytes 2359304 | tf_op jit(solution)/shard_map/ppermute | solution.py:40
  15.8 16.3 %collective-permute-start.2 = (bf16[512,384]{1,0:T(8,128)(2,1)S(1)}, bf16[512,384]{1,0:T(8,128)(2,1)S(1)}, u32[]{:S(2)}, u32[]{:S(2)}) collective-permute-start(bf16[512,384]{1,0:T(8,128)(2,1)S(1)} %collective-permute-done), channel_id=1, source_target_pairs={{0,2},{1,7},{2,4},{3,1},{4,6},{5,3},{6,0},{7,5},{8,10},{9,15},{10,... | collective-permute-start | bytes 1179656 | tf_op jit(solution)/shard_map/ppermute | solution.py:40
  32.1 9.0 %collective-permute-start.3 = (bf16[512,384]{1,0:T(8,128)(2,1)S(1)}, bf16[512,384]{1,0:T(8,128)(2,1)S(1)}, u32[]{:S(2)}, u32[]{:S(2)}) collective-permute-start(bf16[512,384]{1,0:T(8,128)(2,1)S(1)} %collective-permute-done.2), channel_id=1, source_target_pairs={{0,2},{1,7},{2,4},{3,1},{4,6},{5,3},{6,0},{7,5},{8,10},{9,15},{10,... | collective-permute-start | bytes 1179656 | tf_op jit(solution)/shard_map/ppermute | solution.py:40
  33.2 22.1 %collective-permute-start.1 = (bf16[2,512,384]{2,1,0:T(8,128)(2,1)}, bf16[2,512,384]{2,1,0:T(8,128)(2,1)S(1)}, u32[]{:S(2)}, u32[]{:S(2)}) collective-permute-start(bf16[2,512,384]{2,1,0:T(8,128)(2,1)} %pad_maximum_fusion.refs_4_), channel_id=1, source_target_pairs={{0,8},{1,9},{2,10},{3,11},{4,12},{5,13},{6,14},{7,15},{8,0},{9,1},... | collective-permute-start | bytes 2359304 | tf_op jit(solution)/shard_map/ppermute | solution.py:44
  36.4 18.9 %collective-permute-start.18 = (bf16[2,512,384]{2,1,0:T(8,128)(2,1)S(1)}, bf16[2,512,384]{2,1,0:T(8,128)(2,1)S(1)}, u32[]{:S(2)}, u32[]{:S(2)}) collective-permute-start(bf16[2,512,384]{2,1,0:T(8,128)(2,1)S(1)} %collective-permute-done.17.refs_5_), channel_id=1, source_target_pairs={{0,2},{1,7},{2,4},{3,1},{4,6},{5,3},{6,0},{7,5},{8,10},{9,15},{10,... | collective-permute-start | bytes 2359304 | tf_op jit(solution)/shard_map/ppermute | solution.py:40
  42.1 29.8 %collective-permute-start.4 = (bf16[2,512,384]{2,1,0:T(8,128)(2,1)}, bf16[2,512,384]{2,1,0:T(8,128)(2,1)S(1)}, u32[]{:S(2)}, u32[]{:S(2)}) collective-permute-start(bf16[2,512,384]{2,1,0:T(8,128)(2,1)} %pad_maximum_fusion.1.refs_5_), channel_id=1, source_target_pairs={{0,8},{1,9},{2,10},{3,11},{4,12},{5,13},{6,14},{7,15},{8,0},{9,1},... | collective-permute-start | bytes 2359304 | tf_op jit(solution)/shard_map/ppermute | solution.py:44
  45.3 26.8 %collective-permute-start.7 = (bf16[2,512,384]{2,1,0:T(8,128)(2,1)}, bf16[2,512,384]{2,1,0:T(8,128)(2,1)}, u32[]{:S(2)}, u32[]{:S(2)}) collective-permute-start(bf16[2,512,384]{2,1,0:T(8,128)(2,1)} %pad_maximum_fusion.refs_4_), channel_id=1, source_target_pairs={{0,1},{1,0},{2,3},{3,2},{4,5},{5,4},{6,7},{7,6},{8,9},{9,8},{10,11... | collective-permute-start | bytes 2359304 | tf_op jit(solution)/shard_map/ppermute | solution.py:48
  45.3 27.3 %collective-permute-start.8 = (bf16[2,512,384]{2,1,0:T(8,128)(2,1)}, bf16[2,512,384]{2,1,0:T(8,128)(2,1)}, u32[]{:S(2)}, u32[]{:S(2)}) collective-permute-start(bf16[2,512,384]{2,1,0:T(8,128)(2,1)} %pad_maximum_fusion.1.refs_5_), channel_id=1, source_target_pairs={{0,1},{1,0},{2,3},{3,2},{4,5},{5,4},{6,7},{7,6},{8,9},{9,8},{10,11... | collective-permute-start | bytes 2359304 | tf_op jit(solution)/shard_map/ppermute | solution.py:48
  55.3 32.9 %collective-permute-start.5 = (bf16[2,512,384]{2,1,0:T(8,128)(2,1)S(1)}, bf16[2,512,384]{2,1,0:T(8,128)(2,1)S(1)}, u32[]{:S(2)}, u32[]{:S(2)}) collective-permute-start(bf16[2,512,384]{2,1,0:T(8,128)(2,1)S(1)} %collective-permute-done.1.refs_4_), channel_id=1, source_target_pairs={{0,1},{1,0},{2,3},{3,2},{4,5},{5,4},{6,7},{7,6},{8,9},{9,8},{10,11... | collective-permute-start | bytes 2359304 | tf_op jit(solution)/shard_map/ppermute | solution.py:48
  55.3 33.3 %collective-permute-start.19 = (bf16[2,512,384]{2,1,0:T(8,128)(2,1)S(1)}, bf16[2,512,384]{2,1,0:T(8,128)(2,1)S(1)}, u32[]{:S(2)}, u32[]{:S(2)}) collective-permute-start(bf16[2,512,384]{2,1,0:T(8,128)(2,1)S(1)} %collective-permute-done.18.refs_4_), channel_id=1, source_target_pairs={{0,2},{1,7},{2,4},{3,1},{4,6},{5,3},{6,0},{7,5},{8,10},{9,15},{10,... | collective-permute-start | bytes 2359304 | tf_op jit(solution)/shard_map/ppermute | solution.py:40
  71.9 17.0 %collective-permute-start.6 = (bf16[2,512,384]{2,1,0:T(8,128)(2,1)S(1)}, bf16[2,512,384]{2,1,0:T(8,128)(2,1)S(1)}, u32[]{:S(2)}, u32[]{:S(2)}) collective-permute-start(bf16[2,512,384]{2,1,0:T(8,128)(2,1)S(1)} %collective-permute-done.4.refs_5_), channel_id=1, source_target_pairs={{0,1},{1,0},{2,3},{3,2},{4,5},{5,4},{6,7},{7,6},{8,9},{9,8},{10,11... | collective-permute-start | bytes 2359304 | tf_op jit(solution)/shard_map/ppermute | solution.py:48
  72.1 28.4 %collective-permute-start.22 = (bf16[2,512,384]{2,1,0:T(8,128)(2,1)}, bf16[2,512,384]{2,1,0:T(8,128)(2,1)S(1)}, u32[]{:S(2)}, u32[]{:S(2)}) collective-permute-start(bf16[2,512,384]{2,1,0:T(8,128)(2,1)} %copy-done.4), channel_id=1, source_target_pairs={{0,1},{1,0},{2,3},{3,2},{4,5},{5,4},{6,7},{7,6},{8,9},{9,8},{10,11... | collective-permute-start | bytes 2359304 | tf_op jit(solution)/shard_map/ppermute | solution.py:48
  72.6 27.9 %collective-permute-start.23 = (bf16[2,512,384]{2,1,0:T(8,128)(2,1)}, bf16[2,512,384]{2,1,0:T(8,128)(2,1)S(1)}, u32[]{:S(2)}, u32[]{:S(2)}) collective-permute-start(bf16[2,512,384]{2,1,0:T(8,128)(2,1)} %copy-done.12), channel_id=1, source_target_pairs={{0,1},{1,0},{2,3},{3,2},{4,5},{5,4},{6,7},{7,6},{8,9},{9,8},{10,11... | collective-permute-start | bytes 2359304 | tf_op jit(solution)/shard_map/ppermute | solution.py:48
  88.2 36.2 %collective-permute-start.20 = (bf16[2,512,384]{2,1,0:T(8,128)(2,1)S(1)}, bf16[2,512,384]{2,1,0:T(8,128)(2,1)}, u32[]{:S(2)}, u32[]{:S(2)}) collective-permute-start(bf16[2,512,384]{2,1,0:T(8,128)(2,1)S(1)} %collective-permute-done.18.refs_4_), channel_id=1, source_target_pairs={{0,1},{1,0},{2,3},{3,2},{4,5},{5,4},{6,7},{7,6},{8,9},{9,8},{10,11... | collective-permute-start | bytes 2359304 | tf_op jit(solution)/shard_map/ppermute | solution.py:48
  88.6 35.8 %collective-permute-start.21 = (bf16[2,512,384]{2,1,0:T(8,128)(2,1)S(1)}, bf16[2,512,384]{2,1,0:T(8,128)(2,1)}, u32[]{:S(2)}, u32[]{:S(2)}) collective-permute-start(bf16[2,512,384]{2,1,0:T(8,128)(2,1)S(1)} %collective-permute-done.19.refs_5_), channel_id=1, source_target_pairs={{0,1},{1,0},{2,3},{3,2},{4,5},{5,4},{6,7},{7,6},{8,9},{9,8},{10,11... | collective-permute-start | bytes 2359304 | tf_op jit(solution)/shard_map/ppermute | solution.py:48
  97.0 16.8 %collective-permute-start.9 = (bf16[2,4,128,128]{3,2,1,0:T(8,128)(2,1)S(1)}, bf16[2,4,128,128]{3,2,1,0:T(8,128)(2,1)S(1)}, u32[]{:S(2)}, u32[]{:S(2)}) collective-permute-start(bf16[2,4,128,128]{3,2,1,0:T(8,128)(2,1)S(1)} %get-tuple-element.40), channel_id=1, source_target_pairs={{0,16},{16,32},{32,48},{48,64},{64,80},{80,96},{96,112},{1,17},{17... | collective-permute-start | bytes 786440 | tf_op jit(solution)/shard_map/ppermute | solution.py:53
  116.3 33.7 %collective-permute-start.10 = (bf16[2,4,128,128]{3,2,1,0:T(8,128)(2,1)}, bf16[2,4,128,128]{3,2,1,0:T(8,128)(2,1)S(1)}, u32[]{:S(2)}, u32[]{:S(2)}) collective-permute-start(bf16[2,4,128,128]{3,2,1,0:T(8,128)(2,1)} %extend.2), channel_id=1, source_target_pairs={{0,16},{16,32},{32,48},{48,64},{64,80},{80,96},{96,112},{1,17},{17... | collective-permute-start | bytes 786440 | tf_op jit(solution)/shard_map/ppermute | solution.py:53
  119.7 31.0 %collective-permute-start.11 = (bf16[2,4,128,128]{3,2,1,0:T(8,128)(2,1)}, bf16[2,4,128,128]{3,2,1,0:T(8,128)(2,1)S(1)}, u32[]{:S(2)}, u32[]{:S(2)}) collective-permute-start(bf16[2,4,128,128]{3,2,1,0:T(8,128)(2,1)} %extend.2), channel_id=1, source_target_pairs={{0,48},{16,64},{32,80},{48,96},{64,112},{1,49},{17,65},{33,81},{49... | collective-permute-start | bytes 786440 | tf_op jit(solution)/shard_map/ppermute | solution.py:53
  136.4 18.2 %collective-permute-start.24 = (bf16[2,4,128,128]{3,2,1,0:T(8,128)(2,1)S(1)}, bf16[2,4,128,128]{3,2,1,0:T(8,128)(2,1)}, u32[]{:S(2)}, u32[]{:S(2)}) collective-permute-start(bf16[2,4,128,128]{3,2,1,0:T(8,128)(2,1)S(1)} %get-tuple-element.53), channel_id=1, source_target_pairs={{0,16},{16,32},{32,48},{48,64},{64,80},{80,96},{96,112},{1,17},{17... | collective-permute-start | bytes 786440 | tf_op jit(solution)/shard_map/ppermute | solution.py:53
  154.6 25.0 %collective-permute-start.12 = (f32[8,512]{1,0:T(8,128)}, f32[8,512]{1,0:T(8,128)S(1)}, u32[]{:S(2)}, u32[]{:S(2)}) collective-permute-start(f32[8,512]{1,0:T(8,128)} %get-tuple-element.43), channel_id=1, source_target_pairs={{0,1},{1,0},{2,3},{3,2},{4,5},{5,4},{6,7},{7,6},{8,9},{9,8},{10,11... | collective-permute-start | bytes 49160 | tf_op jit(solution)/shard_map/ppermute | solution.py:297
  156.5 19.1 %collective-permute-start.25 = (bf16[2,4,128,128]{3,2,1,0:T(8,128)(2,1)}, bf16[2,4,128,128]{3,2,1,0:T(8,128)(2,1)S(1)}, u32[]{:S(2)}, u32[]{:S(2)}) collective-permute-start(bf16[2,4,128,128]{3,2,1,0:T(8,128)(2,1)} %extend.3), channel_id=1, source_target_pairs={{0,16},{16,32},{32,48},{48,64},{64,80},{80,96},{96,112},{1,17},{17... | collective-permute-start | bytes 786440 | tf_op jit(solution)/shard_map/ppermute | solution.py:53
  159.2 16.5 %collective-permute-start.26 = (bf16[2,4,128,128]{3,2,1,0:T(8,128)(2,1)}, bf16[2,4,128,128]{3,2,1,0:T(8,128)(2,1)S(1)}, u32[]{:S(2)}, u32[]{:S(2)}) collective-permute-start(bf16[2,4,128,128]{3,2,1,0:T(8,128)(2,1)} %extend.3), channel_id=1, source_target_pairs={{0,48},{16,64},{32,80},{48,96},{64,112},{1,49},{17,65},{33,81},{49... | collective-permute-start | bytes 786440 | tf_op jit(solution)/shard_map/ppermute | solution.py:53
  (50 other events, 617.9 us)

commit v2 on v1

v2 whole, which is shorter than its diff:
```python
import functools

import jax
import jax.numpy as jnp
from jax import lax
from jax.experimental import pallas as pl
from jax.experimental.pallas import tpu as pltpu
from jax.sharding import PartitionSpec as P

EPSILON = 1e-06
BLOCK = 256
HEAD = 128
SHARD = 384
WIDTH = 512
LIMIT = 16
F32 = jnp.float32
BF16 = jnp.bfloat16
ANY = pl.BlockSpec(memory_space=pl.ANY)
HBM = pl.BlockSpec(memory_space=pltpu.HBM)
SMEM = pl.BlockSpec(memory_space=pltpu.SMEM)
VMEM = pl.BlockSpec(memory_space=pltpu.VMEM)
PIECES = [(0, 0), (0, 1), (1, 0), (0, 2), (1, 1), (0, 3), (1, 2), (1, 3)]
PIECE = 2 * SHARD


def tp_route(step):
    route = []
    for y in range(2):
        for z in range(4):
            for c in range(2):
                y2, z2, c2 = step(y, z, c)
                route.append((y * 8 + z * 2 + c, (y2 % 2) * 8 + (z2 % 4) * 2 + c2 % 2))
    return route


RING = tp_route(lambda y, z, c: (y, z + 1 - 2 * c, c))
ACROSS = tp_route(lambda y, z, c: (y + 1, z, c))
CORE = tp_route(lambda y, z, c: (y, z, c + 1))
PAIR_A = tp_route(lambda y, z, c: (y, z ^ 1, c))
PAIR_B = tp_route(lambda y, z, c: (y, 3 - z, c))


def ring(x):
    return lax.ppermute(x, "tp", RING)


def across(x):
    return lax.ppermute(x, "tp", ACROSS)


def other_core(x):
    return lax.ppermute(x, "tp", CORE)


def ahead(x, distance):
    n = lax.axis_size("ctx")
    return lax.ppermute(x, "ctx", [(i, i + distance) for i in range(n - distance)])


def doc_ends(lengths, seq):
    first = lengths[seq, 0]
    second = first + lengths[seq, 1]
    return first, second, second + lengths[seq, 2]


def doc_of(position, ends):
    return sum((position >= end).astype(jnp.int32) for end in ends)


def decay_of(rate, steps):
    return jnp.exp(-rate * steps.astype(F32))


def project_kernel(mode, first_seq, plan, *refs):
    n_x, parts, loads, n_held, n_w, n_acc = plan
    refs = list(refs)
    take = lambda n: [refs.pop(0) for _ in range(n)]
    meta, lengths, decay = take(3)
    xs = take(n_x)
    held = take(n_held)
    weights = take(4) if loads else []
    accs = take(n_acc)
    if mode == "qg":
        k_in, v_in, gain = take(3)
    outs = take({"first": 8, "more": n_acc, "kv": 3, "qg": 3}[mode])
    loaded = take(len(loads))
    xbuf, xsem, wsem = take(3)
    held = held + loaded

    def x_copies(p, i):
        return [
            pltpu.make_async_copy(
                xs[array] if index is None else xs[array].at[index],
                xbuf.at[p, :, pl.ds((2 * i + core) * SHARD, SHARD)],
                xsem.at[p, 2 * i + core],
            )
            for core, (array, index) in enumerate(parts[p][i][0])
        ]

    def w_copies(i, n):
        return [
            pltpu.make_async_copy(
                weights[n].at[pl.ds(pl.multiple_of(meta[1 + 2 * loads[i] + core] * SHARD, SHARD), SHARD), :],
                loaded[i].at[n, pl.ds(core * SHARD, SHARD), :],
                wsem.at[i, n, core],
            )
            for core in (0, 1)
        ]

    for p in range(len(parts)):
        for i in range(len(parts[p])):
            for copy in x_copies(p, i):
                copy.start()
    for i in range(len(loads)):
        for n in range(4):
            for copy in w_copies(i, n):
                copy.start()

    def product(p, n, acc):
        total = None if acc is None else acc[...]
        for i, (_, w) in enumerate(parts[p]):
            if n in (0, 2 if mode == "qg" else 0):
                for copy in x_copies(p, i):
                    copy.wait()
            if mode == "first":
                for copy in w_copies(0, n):
                    copy.wait()
            got = jnp.dot(
                xbuf[p, :, pl.ds(i * PIECE, PIECE)], held[w][n], preferred_element_type=F32
            )
            total = got if total is None else total + got
        return total

    offset = meta[0]

    def part(s, h):
        return pl.ds(s * BLOCK, BLOCK), pl.ds(h * HEAD, HEAD)

    heads = WIDTH // HEAD
    if mode == "first":
        half = xbuf.shape[1] // 2
        for n in range(4):
            got = product(0, n, None)
            outs[n][...] = got[:half]
            outs[4 + n][...] = got[half:]
    if mode == "more":
        for p in range(len(parts)):
            for n in range(4):
                outs[4 * p + n][...] = product(p, n, accs[4 * p + n])
    if mode == "kv":
        k_out, v_out, s_out = outs
        k_out[...] = jax.nn.silu(product(0, 0, accs[0])).astype(BF16)
        v_out[...] = jax.nn.silu(product(0, 1, accs[1])).astype(BF16)
        local = lax.broadcasted_iota(jnp.int32, (BLOCK, HEAD), 0)
        for s in range(s_out.shape[0]):
            ends = doc_ends(lengths, first_seq + s)
            keep = doc_of(local + offset, ends) == doc_of(offset + BLOCK - 1, ends)
            for h in range(heads):
                scale = jnp.where(keep, decay_of(decay[h], BLOCK - 1 - local), 0.0)
                weighted = (k_out[part(s, h)].astype(F32) * scale).astype(BF16)
                s_out[s, h] = lax.dot_general(
                    weighted, v_out[part(s, h)], (((0,), (0,)), ((), ())), preferred_element_type=F32
                )
    if mode == "qg":
        q_out, inner_out, gate_out = outs
        q_out[...] = jax.nn.silu(product(0, 2, accs[0])).astype(BF16)
        gate_out[...] = gain[...] * jax.nn.sigmoid(product(0, 3, accs[1]))
        row = lax.broadcasted_iota(jnp.int32, (BLOCK, BLOCK), 0)
        column = lax.broadcasted_iota(jnp.int32, (BLOCK, BLOCK), 1)
        causal = row >= column
        for h in range(heads):
            pair_decay = decay_of(decay[h], jnp.maximum(row - column, 0))
            for s in range(q_out.shape[0] // BLOCK):
                ends = doc_ends(lengths, first_seq + s)
                same = doc_of(row + offset, ends) == doc_of(column + offset, ends)
                scores = lax.dot_general(
                    q_out[part(s, h)],
                    k_in[part(s, h)],
                    (((1,), (1,)), ((), ())),
                    preferred_element_type=F32,
                )
                allowed = jnp.logical_and(causal, same)
                mixed = jnp.where(allowed, scores * pair_decay, 0.0).astype(BF16)
                inner_out[part(s, h)] = jnp.dot(
                    mixed, v_in[part(s, h)], preferred_element_type=F32
                )
    done = 1 if mode == "first" else 0
    for i in range(done, len(loads)):
        for n in range(4):
            for copy in w_copies(i, n):
                copy.wait()


def project(mode, scalars, parts, held, weights=(), loads=(), accs=(), extra=(), first_seq=0):
    arrays, plan_parts, used = [], [], []
    for pieces in parts:
        plan = []
        for (mine, other, index), number in pieces:
            for x in (mine, other):
                if all(x is not y for y in arrays):
                    arrays.append(x)
            where = [
                ([x is y for y in arrays].index(True), index) for x in (mine, other)
            ]
            if number in held and number not in used:
                used.append(number)
            plan.append((where, number))
        plan_parts.append(plan)
    numbers = used + list(loads)
    plan_parts = [[(where, numbers.index(number)) for where, number in plan] for plan in plan_parts]
    rows = arrays[0].shape[-2]
    half = jax.ShapeDtypeStruct((rows, WIDTH), BF16)
    wide = pltpu.VMEM((rows, WIDTH), F32)
    state = jax.ShapeDtypeStruct((rows // BLOCK, WIDTH // HEAD, HEAD, HEAD), F32)
    outs = {
        "first": [pltpu.VMEM((rows // 2, WIDTH), F32)] * 8,
        "more": [wide] * len(accs),
        "kv": [half, half, state],
        "qg": [half, wide, wide],
    }[mode]
    n_outs = len(outs)
    outs = outs + [pltpu.VMEM((4, PIECE, WIDTH), BF16)] * len(loads)
    most = max(len(p) for p in plan_parts)
    loading = [pltpu.with_memory_space_constraint(w, pltpu.HBM) for w in weights] if loads else []
    before = 3 + len(arrays) + len(used) + len(loading)
    aliases = {before + n: n for n in range(len(accs))} if mode == "more" else {}
    plan = (len(arrays), plan_parts, list(loads), len(used), 4, len(accs))
    got = pl.pallas_call(
        functools.partial(project_kernel, mode, first_seq, plan),
        out_shape=outs,
        in_specs=[SMEM] * 3
        + [ANY] * len(arrays)
        + [VMEM] * len(used)
        + [HBM] * len(loading)
        + [VMEM] * (len(accs) + len(extra)),
        out_specs=[VMEM] * len(outs),
        scratch_shapes=[
            pltpu.VMEM((len(parts), rows, most * PIECE), BF16),
            pltpu.SemaphoreType.DMA((len(parts), 2 * most)),
            pltpu.SemaphoreType.DMA((max(1, len(loads)), 4, 2)),
        ],
        input_output_aliases=aliases,
        compiler_params=pltpu.CompilerParams(vmem_limit_bytes=LIMIT * 2**20),
        cost_estimate=pl.CostEstimate(
            flops=2 * rows * PIECE * sum(len(p) for p in parts) * (4 if mode in ("first", "more") else 2) * WIDTH,
            bytes_accessed=2 * rows * PIECE,
            transcendentals=0,
        ),
        name="project_" + mode,
    )(*scalars, *arrays, *[held[n] for n in used], *loading, *accs, *extra)
    held.update(zip(loads, got[n_outs:]))
    return got[:n_outs]


def carried_share(meta, lengths, decay, s, h, block):
    ends = doc_ends(lengths, s)
    start = meta[0] - block * BLOCK
    keep = doc_of(start + BLOCK - 1, ends) == doc_of(start - 1, ends)
    rate = jnp.full((8, HEAD), decay[h] * (-1.0 * BLOCK), F32)
    return jnp.where(keep, jnp.exp(rate), 0.0)[0:1, :]


def extend_kernel(first_seq, meta, lengths, decay, state, before, out):
    for s in range(state.shape[0]):
        for h in range(state.shape[1]):
            share = carried_share(meta, lengths, decay, first_seq + s, h, 0)
            out[s, h] = (state[s, h] + share * before[s, h].astype(F32)).astype(BF16)


def extend(scalars, state, before, first_seq):
    return pl.pallas_call(
        functools.partial(extend_kernel, first_seq),
        out_shape=jax.ShapeDtypeStruct(state.shape, BF16),
        in_specs=[SMEM] * 3 + [VMEM] * 2,
        out_specs=VMEM,
        compiler_params=pltpu.CompilerParams(vmem_limit_bytes=LIMIT * 2**20),
        name="extend",
    )(*scalars, state, before)


def round_kernel(x, out):
    out[...] = x[...].astype(BF16)


def rounded(x):
    return pl.pallas_call(
        round_kernel,
        out_shape=jax.ShapeDtypeStruct(x.shape, BF16),
        in_specs=[VMEM],
        out_specs=VMEM,
        compiler_params=pltpu.CompilerParams(vmem_limit_bytes=LIMIT * 2**20),
        name="round",
    )(x)


def combine_kernel(first_seq, meta, lengths, decay, query, inner, near, far, attn_out, squares_out):
    seqs, heads = near.shape[:2]
    offset = meta[0]
    local = lax.broadcasted_iota(jnp.int32, (BLOCK, HEAD), 0)
    for s in range(seqs):
        ends = doc_ends(lengths, first_seq + s)
        inside = doc_of(local + offset, ends) == doc_of(offset - 1, ends)
        total = jnp.zeros((BLOCK, HEAD), F32)
        rows = pl.ds(s * BLOCK, BLOCK)
        for h in range(heads):
            columns = pl.ds(h * HEAD, HEAD)
            share = carried_share(meta, lengths, decay, first_seq + s, h, 1)
            share = share * carried_share(meta, lengths, decay, first_seq + s, h, 2)
            incoming = near[s, h].astype(F32) + share * far[s, h].astype(F32)
            high = incoming.astype(BF16)
            low = (incoming - high.astype(F32)).astype(BF16)
            q = query[rows, columns]
            carried = jnp.dot(q, high, preferred_element_type=F32)
            carried = carried + jnp.dot(q, low, preferred_element_type=F32)
            scale = jnp.where(inside, decay_of(decay[h], local + 1), 0.0)
            attn = inner[rows, columns] + carried * scale
            attn_out[rows, columns] = attn
            total = total + attn * attn
        line = jnp.sum(jnp.transpose(total), axis=0, keepdims=True)
        for i in range(BLOCK // HEAD):
            squares_out[pl.ds(s * (BLOCK // HEAD) + i, 1), :] = line[:, i * HEAD : (i + 1) * HEAD]


def combine(scalars, query, inner, near, far, first_seq):
    rows = query.shape[0]
    return pl.pallas_call(
        functools.partial(combine_kernel, first_seq),
        out_shape=[
            pltpu.VMEM((rows, WIDTH), F32),
            jax.ShapeDtypeStruct((rows // HEAD, HEAD), F32),
        ],
        in_specs=[SMEM] * 3 + [VMEM] * 4,
        out_specs=[VMEM] * 2,
        compiler_params=pltpu.CompilerParams(vmem_limit_bytes=LIMIT * 2**20),
        name="combine",
    )(*scalars, query, inner, near, far)


def finish_kernel(width_all, attn_y, attn_z, gate_y, gate_z, squares, out):
    attns, gates = (attn_y, attn_z), (gate_y, gate_z)
    half = out.shape[0] // 2
    per = BLOCK // HEAD
    scales = lax.rsqrt(squares[...] * (1.0 / width_all) + EPSILON)
    for i in range(scales.shape[0]):
        scale = jnp.transpose(jnp.broadcast_to(scales[i : i + 1, :], (HEAD, HEAD)))
        s, r = i // per, i % per
        rows = pl.ds((s % half) * BLOCK + r * HEAD, HEAD)
        for h in range(WIDTH // HEAD):
            columns = pl.ds(h * HEAD, HEAD)
            got = attns[s // half][rows, columns] * scale * gates[s // half][rows, columns]
            out[s, pl.ds(r * HEAD, HEAD), columns] = got.astype(BF16)


def finish(attns, gates, squares):
    width_all = WIDTH * lax.axis_size("tp")
    seqs = 2 * attns[0].shape[0] // BLOCK
    return pl.pallas_call(
        functools.partial(finish_kernel, width_all),
        out_shape=jax.ShapeDtypeStruct((seqs, BLOCK, WIDTH), BF16),
        in_specs=[VMEM] * 5,
        out_specs=VMEM,
        compiler_params=pltpu.CompilerParams(vmem_limit_bytes=LIMIT * 2**20),
        name="finish",
    )(*attns, *gates, squares)


def stack_kernel(first, second, out, sems):
    copies = [pltpu.make_async_copy(x, out.at[i], sems.at[i]) for i, x in enumerate((first, second))]
    for copy in copies:
        copy.start()
    for copy in copies:
        copy.wait()


def stack(first, second):
    return pl.pallas_call(
        stack_kernel,
        out_shape=pltpu.HBM((2, *first.shape), first.dtype),
        in_specs=[ANY] * 2,
        out_specs=HBM,
        scratch_shapes=[pltpu.SemaphoreType.DMA((2,))],
        compiler_params=pltpu.CompilerParams(vmem_limit_bytes=2**20),
        name="stack",
    )(first, second)


def add_kernel(first, second, out):
    out[...] = first[...] + second[...]


def add(first, second):
    return pl.pallas_call(
        add_kernel,
        out_shape=jax.ShapeDtypeStruct(first.shape, first.dtype),
        in_specs=[VMEM] * 2,
        out_specs=VMEM,
        compiler_params=pltpu.CompilerParams(vmem_limit_bytes=2**20),
        name="add",
    )(first, second)


def join_kernel(first, second, out):
    half = first.shape[0]
    out[pl.ds(0, half), :] = first[...]
    out[pl.ds(half, half), :] = second[...]


def join(first, second):
    return pl.pallas_call(
        join_kernel,
        out_shape=jax.ShapeDtypeStruct((2 * first.shape[0], first.shape[1]), first.dtype),
        in_specs=[VMEM] * 2,
        out_specs=VMEM,
        compiler_params=pltpu.CompilerParams(vmem_limit_bytes=2**20),
        name="join",
    )(first, second)


def all_sum(x):
    for route in (CORE, ACROSS, PAIR_A, PAIR_B):
        x = add(x, lax.ppermute(x, "tp", route))
    return x


def in_order(*groups):
    return lax.optimization_barrier(groups)


def on_device(hidden, w_query, w_key, w_value, w_gate, decay_rate, norm_gain, doc_lengths):
    seqs = hidden.shape[0]
    me = lax.axis_index("tp")
    my_y, my_z, my_c = me // 8, (me // 2) % 4, me % 2
    meta = [lax.axis_index("ctx") * BLOCK]
    gain = norm_gain.reshape(1, WIDTH)
    for flip, j in PIECES:
        for core in (0, 1):
            c = (my_c + core) % 2
            z = (my_z + j * (2 * c - 1) + 4) % 4
            meta.append((my_y + flip) % 2 * 8 + z * 2 + c)
    scalars = (jnp.stack(meta), doc_lengths, decay_rate)
    half = seqs // 2
    rows = hidden.reshape(seqs * BLOCK, SHARD)
    part_y, part_z = rows[: half * BLOCK], rows[half * BLOCK :]
    weights = [w_key, w_value, w_query, w_gate]
    held = {}

    def at(flip, j):
        return PIECES.index((flip, j))

    def one(x, flip, j):
        return [((x, other_core(x), None), at(flip, j))]

    def two(x, j):
        other = other_core(x)
        return [((x, other, flip), at(flip, j)) for flip in (0, 1)]

    y0, r1 = across(part_y), ring(part_z)
    acc = project("first", scalars, [one(rows, 0, 0)], held, weights, [0, 1, 2])
    acc, y0, r1, part_z = in_order(acc, y0, r1, part_z)

    a1, r2, far0 = ring(stack(part_y, y0)), ring(r1), across(part_z)
    acc = project("more", scalars, [one(y0, 1, 0), one(r1, 0, 1)], held, weights, [3, 4], acc)
    acc, a1, r2, far0, r1 = in_order(acc, a1, r2, far0, r1)

    a2, r3, far1 = ring(a1), ring(r2), across(r1)
    acc = project(
        "more", scalars, [two(a1, 1), one(r2, 0, 2) + one(far0, 1, 0)], held, weights, [5, 6], acc
    )
    acc, a2, r3, far1, r2 = in_order(acc, a2, r3, far1, r2)

    a3, far2 = ring(a2), across(r2)
    acc = project(
        "more", scalars, [two(a2, 2), one(r3, 0, 3) + one(far1, 1, 1)], held, weights, [7], acc
    )
    acc, a3, far2, r3 = in_order(acc, a3, far2, r3)

    far3 = across(r3)
    last_y = [two(a3, 3)]
    keys_y, values_y, state_y = project("kv", scalars, last_y, held, accs=acc[:2])
    before_y = ahead(rounded(state_y), 1)
    acc_z = project("more", scalars, [one(far2, 1, 2)], held, accs=in_order(acc[4:], state_y)[0])
    acc_z, far3 = in_order(acc_z, far3)

    last_z = [one(far3, 1, 3)]
    keys_z, values_z, state_z = project("kv", scalars, last_z, held, accs=acc_z[:2], first_seq=half)
    before_z = ahead(rounded(state_z), 1)
    acc_y, before_y, state_z = in_order(acc[2:4], before_y, state_z)
    longer_y = extend(scalars, state_y, before_y, 0)
    near_y, far_y = ahead(longer_y, 1), ahead(longer_y, 3)
    query_y, inner_y, gate_y = project(
        "qg", scalars, last_y, held, accs=acc_y, extra=(keys_y, values_y, gain)
    )
    query_y, before_z, acc_q = in_order(query_y, before_z, acc_z[2:])
    longer_z = extend(scalars, state_z, before_z, half)
    near_z, far_z = ahead(longer_z, 1), ahead(longer_z, 3)
    query_z, inner_z, gate_z = project(
        "qg", scalars, last_z, held, accs=acc_q, extra=(keys_z, values_z, gain), first_seq=half
    )
    query_z, near_y, far_y = in_order(query_z, near_y, far_y)
    attn_y, squares_y = combine(scalars, query_y, inner_y, near_y, far_y, 0)
    squares_y, near_z, far_z = in_order(squares_y, near_z, far_z)
    attn_z, squares_z = combine(scalars, query_z, inner_z, near_z, far_z, half)
    squares = all_sum(join(squares_y, squares_z))
    return finish((attn_y, attn_z), (gate_y, gate_z), squares)


def solution(mesh):
    in_specs = (
        P(None, "ctx", "tp"),
        P(None, "tp"),
        P(None, "tp"),
        P(None, "tp"),
        P(None, "tp"),
        P("tp"),
        P("tp"),
        P(),
    )
    out_specs = P(None, "ctx", "tp")
    return jax.shard_map(
        on_device, mesh=mesh, in_specs=in_specs, out_specs=out_specs, check_vma=False
    )
```

time: 204 us -> 139 us (0.68)
  the two profiles are of different devices: /device:TPU:0 before, /device:TPU:8 now
where the time goes in v2:
time: 139 us
  Pallas kernels  50.2 us (36%)
  waiting for transfers between devices  46 us (33%)
  starting transfers between devices  38.6 us (28%)
  local copies, waits for them, and re-layouts  3.76 us (3%)
    pallas_call x9, Pallas kernels, project(): pl.pallas_call(functools.partial(project_kernel, mode, first_seq, plan),...  44.1 us
    ppermute x6, waiting for transfers between devices, ahead(): lax.ppermute(x, 'ctx', [(i, i + distance) for i in range(n - distance)])  16.1 us
    ppermute x6, starting transfers between devices, ahead(): lax.ppermute(x, 'ctx', [(i, i + distance) for i in range(n - distance)])  15 us
    ppermute x6, waiting for transfers between devices, ring(): return lax.ppermute(x, 'tp', RING)  12.4 us
    ppermute x4, waiting for transfers between devices, all_sum(): x = add(x, lax.ppermute(x, 'tp', route))  10 us
    ppermute x5, starting transfers between devices, across(): return lax.ppermute(x, 'tp', ACROSS)  8.77 us
    ppermute x6, starting transfers between devices, ring(): return lax.ppermute(x, 'tp', RING)  7.86 us
    ppermute x5, waiting for transfers between devices, across(): return lax.ppermute(x, 'tp', ACROSS)  6.32 us
  transfers between devices with their start and end apart: 33, of which 15 were waited for; matrix products, arithmetic and copies ran while one was open for 1% of the time, Pallas kernels for 34%

profile of v2, /device:TPU:8, one launch (start us, length us, event | category | flops | bytes accessed | tf_op | source)
XLA Modules:
  0.0 138.9 jit_solution(9747386944209782069)
XLA Ops:
  1.2 2.4 %collective-permute-start.1 = (bf16[512,384]{1,0:T(8,128)(2,1)S(1)}, bf16[512,384]{1,0:T(8,128)(2,1)S(1)}, u32[]{:S(2)}, u32[]{:S(2)}) collective-permute-start(bf16[512,384]{1,0:T(8,128)(2,1)S(1)} %bitcast.23), channel_id=1, source_target_pairs={{0,8},{1,9},{2,10},{3,11},{4,12},{5,13},{6,14},{7,15},{8,0},{9,1},... | collective-permute-start | bytes 1179656 | tf_op jit(solution)/shard_map/ppermute | solution.py:48
  8.1 7.6 %project_first.1 = (f32[512,512]{1,0:T(8,128)S(1)}, f32[512,512]{1,0:T(8,128)S(1)}, f32[512,512]{1,0:T(8,128)S(1)}, f32[512,512]{1,0:T(8,128)S(1)}, f32[512,512]...) custom-call(s32[17]{0:T(128)S(1)} %stack.72.refs_0_.meta, ...), custom_call_target="tpu_custom_call" | custom-call | flops 3221225472 | bytes 1572864 | tf_op jit(solution)/shard_map/project_first/pallas_call | solution.py:228
  22.0 5.1 %project_more.4 = (f32[512,512]{1,0:T(8,128)S(1)}, f32[512,512]{1,0:T(8,128)S(1)}, f32[512,512]{1,0:T(8,128)S(1)}, f32[512,512]{1,0:T(8,128)S(1)}, f32[512,512]{...) custom-call(s32[17]{0:T(128)S(1)} %stack.72.refs_0_.meta, ...), custom_call_target="tpu_custom_call", output_to_operand_aliasing={{0}: (13, {}), {1}: (14, {}), {2}: (15, {}), {3}: (16, {}),... | custom-call | flops 3221225472 | bytes 786432 | tf_op jit(solution)/shard_map/project_more/pallas_call | solution.py:228
  27.1 7.2 %collective-permute-done.6.refs_5_ = bf16[512,384]{1,0:T(8,128)(2,1)S(1)} collective-permute-done((bf16[512,384]{1,0:T(8,128)(2,1)S(1)}, bf16[512,384]{1,0:T(8,128)(2,1)S(1)}, u32[]{:S(2)}, u32[]{:S(2)}) %collective-permute-start.6) | collective-permute-done | bytes 393248 | tf_op jit(solution)/shard_map/ppermute | solution.py:44
  38.9 8.6 %project_more.5 = (f32[512,512]{1,0:T(8,128)S(1)}, f32[512,512]{1,0:T(8,128)S(1)}, f32[512,512]{1,0:T(8,128)S(1)}, f32[512,512]{1,0:T(8,128)S(1)}, f32[512,512]{...) custom-call(s32[17]{0:T(128)S(1)} %stack.72.refs_0_.meta, ...), custom_call_target="tpu_custom_call", output_to_operand_aliasing={{0}: (17, {}), {1}: (18, {}), {2}: (19, {}), {3}: (20, {}),... | custom-call | flops 6442450944 | bytes 786432 | tf_op jit(solution)/shard_map/project_more/pallas_call | solution.py:228
  47.5 4.9 %collective-permute-done.12.refs_5_ = bf16[512,384]{1,0:T(8,128)(2,1)S(1)} collective-permute-done((bf16[512,384]{1,0:T(8,128)(2,1)S(1)}, bf16[512,384]{1,0:T(8,128)(2,1)S(1)}, u32[]{:S(2)}, u32[]{:S(2)}) %collective-permute-start.12) | collective-permute-done | bytes 393248 | tf_op jit(solution)/shard_map/ppermute | solution.py:44
  55.8 8.5 %project_more.6 = (f32[512,512]{1,0:T(8,128)S(1)}, f32[512,512]{1,0:T(8,128)S(1)}, f32[512,512]{1,0:T(8,128)S(1)}, f32[512,512]{1,0:T(8,128)S(1)}, f32[512,512]{...) custom-call(s32[17]{0:T(128)S(1)} %stack.72.refs_0_.meta, ...), custom_call_target="tpu_custom_call", output_to_operand_aliasing={{0}: (17, {}), {1}: (18, {}), {2}: (19, {}), {3}: (20, {}),... | custom-call | flops 6442450944 | bytes 786432 | tf_op jit(solution)/shard_map/project_more/pallas_call | solution.py:228
  68.6 3.2 %project_kv.2 = (bf16[512,512]{1,0:T(8,128)(2,1)S(1)}, bf16[512,512]{1,0:T(8,128)(2,1)S(1)}, f32[2,4,128,128]{3,2,1,0:T(8,128)S(1)}) custom-call(s32[17]{0:T(128)S(1)} %stack.72.refs_0_.meta, s32[4,4]{1,0:T(4,128)S(1)} %copy-done.2, f32[4]{0:T(128)S(1)} %copy-done.4, bf16[2,512,384]{2,1,0:T(8,128)(2,1)S(1)} %collective-permute-done.17.refs_3_, ...), custom_call_target="tpu_custom_call" | custom-call | flops 1610612736 | bytes 786432 | tf_op jit(solution)/shard_map/project_kv/pallas_call | solution.py:228
  71.9 2.7 %project_more.7 = (f32[512,512]{1,0:T(8,128)S(1)}, f32[512,512]{1,0:T(8,128)S(1)}, f32[512,512]{1,0:T(8,128)S(1)}, f32[512,512]{1,0:T(8,128)S(1)}) custom-call(s32[17]{0:T(128)S(1)} %stack.72.refs_0_.meta, s32[4,4]{1,0:T(4,128)S(1)} %copy-done.2, f32[4]{0:T(128)S(1)} %copy-done.4, ...), custom_call_target="tpu_custom_call", output_to_operand_aliasing={{0}: (6, {}), {1}: (7, {}), {2}: (8, {}), {3}: (9, {})} | custom-call | flops 1610612736 | bytes 786432 | tf_op jit(solution)/shard_map/project_more/pallas_call | solution.py:228
  74.6 4.7 %collective-permute-done.22.refs_3_ = bf16[512,384]{1,0:T(8,128)(2,1)S(1)} collective-permute-done((bf16[512,384]{1,0:T(8,128)(2,1)S(1)}, bf16[512,384]{1,0:T(8,128)(2,1)S(1)}, u32[]{:S(2)}, u32[]{:S(2)}) %collective-permute-start.22) | collective-permute-done | bytes 393248 | tf_op jit(solution)/shard_map/ppermute | solution.py:48
  79.3 3.4 %collective-permute-start.20 = (bf16[2,4,128,128]{3,2,1,0:T(8,128)(2,1)S(1)}, bf16[2,4,128,128]{3,2,1,0:T(8,128)(2,1)S(1)}, u32[]{:S(2)}, u32[]{:S(2)}) collective-permute-start(bf16[2,4,128,128]{3,2,1,0:T(8,128)(2,1)S(1)} %round.2), channel_id=1, source_target_pairs={{0,16},{16,32},{32,48},{48,64},{64,80},{80,96},{96,112},{1,17},{17... | collective-permute-start | bytes 786440 | tf_op jit(solution)/shard_map/ppermute | solution.py:57
  82.7 2.3 %project_kv.3 = (bf16[512,512]{1,0:T(8,128)(2,1)S(1)}, bf16[512,512]{1,0:T(8,128)(2,1)S(1)}, f32[2,4,128,128]{3,2,1,0:T(8,128)S(1)}) custom-call(s32[17]{0:T(128)S(1)} %stack.72.refs_0_.meta, s32[4,4]{1,0:T(4,128)S(1)} %copy-done.2, f32[4]{0:T(128)S(1)} %copy-done.4, bf16[512,384]{1,0:T(8,128)(2,1)S(1)} %collective-permute-done.22.refs_3_, ...), custom_call_target="tpu_custom_call" | custom-call | flops 805306368 | bytes 786432 | tf_op jit(solution)/shard_map/project_kv/pallas_call | solution.py:228
  85.0 3.4 %collective-permute-start.24 = (bf16[2,4,128,128]{3,2,1,0:T(8,128)(2,1)S(1)}, bf16[2,4,128,128]{3,2,1,0:T(8,128)(2,1)S(1)}, u32[]{:S(2)}, u32[]{:S(2)}) collective-permute-start(bf16[2,4,128,128]{3,2,1,0:T(8,128)(2,1)S(1)} %round.3), channel_id=1, source_target_pairs={{0,16},{16,32},{32,48},{48,64},{64,80},{80,96},{96,112},{1,17},{17... | collective-permute-start | bytes 786440 | tf_op jit(solution)/shard_map/ppermute | solution.py:57
  88.4 3.6 %collective-permute-done.20.before = bf16[2,4,128,128]{3,2,1,0:T(8,128)(2,1)S(1)} collective-permute-done((bf16[2,4,128,128]{3,2,1,0:T(8,128)(2,1)S(1)}, bf16[2,4,128,128]{3,2,1,0:T(8,128)(2,1)S(1)}, u32[]{:S(2)}, u32[]{:S(2)}) %collective-permute-start.20) | collective-permute-done | bytes 262176 | tf_op jit(solution)/shard_map/ppermute | solution.py:57
  94.6 2.3 %collective-permute-start.26 = (bf16[2,4,128,128]{3,2,1,0:T(8,128)(2,1)S(1)}, bf16[2,4,128,128]{3,2,1,0:T(8,128)(2,1)S(1)}, u32[]{:S(2)}, u32[]{:S(2)}) collective-permute-start(bf16[2,4,128,128]{3,2,1,0:T(8,128)(2,1)S(1)} %extend.2), channel_id=1, source_target_pairs={{0,48},{16,64},{32,80},{48,96},{64,112},{1,49},{17,65},{33,81},{49... | collective-permute-start | bytes 786440 | tf_op jit(solution)/shard_map/ppermute | solution.py:57
  96.9 3.5 %project_qg.2 = (bf16[512,512]{1,0:T(8,128)(2,1)S(1)}, f32[512,512]{1,0:T(8,128)S(1)}, f32[512,512]{1,0:T(8,128)S(1)}) custom-call(s32[17]{0:T(128)S(1)} %stack.72.refs_0_.meta, s32[4,4]{1,0:T(4,128)S(1)} %copy-done.2, f32[4]{0:T(128)S(1)} %copy-done.4, bf16[2,512,384]{2,1,0:T(8,128)(2,1)S(1)} %collective-permute-done.17.refs_3_, ...), custom_call_target="tpu_custom_call" | custom-call | flops 1610612736 | bytes 786432 | tf_op jit(solution)/shard_map/project_qg/pallas_call | solution.py:228
  101.1 2.1 %collective-permute-start.27 = (bf16[2,4,128,128]{3,2,1,0:T(8,128)(2,1)S(1)}, bf16[2,4,128,128]{3,2,1,0:T(8,128)(2,1)S(1)}, u32[]{:S(2)}, u32[]{:S(2)}) collective-permute-start(bf16[2,4,128,128]{3,2,1,0:T(8,128)(2,1)S(1)} %extend.3), channel_id=1, source_target_pairs={{0,16},{16,32},{32,48},{48,64},{64,80},{80,96},{96,112},{1,17},{17... | collective-permute-start | bytes 786440 | tf_op jit(solution)/shard_map/ppermute | solution.py:57
  105.2 2.6 %project_qg.3 = (bf16[512,512]{1,0:T(8,128)(2,1)S(1)}, f32[512,512]{1,0:T(8,128)S(1)}, f32[512,512]{1,0:T(8,128)S(1)}) custom-call(s32[17]{0:T(128)S(1)} %stack.72.refs_0_.meta, s32[4,4]{1,0:T(4,128)S(1)} %copy-done.2, f32[4]{0:T(128)S(1)} %copy-done.4, bf16[512,384]{1,0:T(8,128)(2,1)S(1)} %collective-permute-done.22.refs_3_, ...), custom_call_target="tpu_custom_call" | custom-call | flops 805306368 | bytes 786432 | tf_op jit(solution)/shard_map/project_qg/pallas_call | solution.py:228
  108.1 8.3 %collective-permute-done.26.far = bf16[2,4,128,128]{3,2,1,0:T(8,128)(2,1)S(1)} collective-permute-done((bf16[2,4,128,128]{3,2,1,0:T(8,128)(2,1)S(1)}, bf16[2,4,128,128]{3,2,1,0:T(8,128)(2,1)S(1)}, u32[]{:S(2)}, u32[]{:S(2)}) %collective-permute-start.26) | collective-permute-done | bytes 262176 | tf_op jit(solution)/shard_map/ppermute | solution.py:57
  117.7 3.8 %collective-permute-done.28.far = bf16[2,4,128,128]{3,2,1,0:T(8,128)(2,1)S(1)} collective-permute-done((bf16[2,4,128,128]{3,2,1,0:T(8,128)(2,1)S(1)}, bf16[2,4,128,128]{3,2,1,0:T(8,128)(2,1)S(1)}, u32[]{:S(2)}, u32[]{:S(2)}) %collective-permute-start.28) | collective-permute-done | bytes 262176 | tf_op jit(solution)/shard_map/ppermute | solution.py:57
  124.0 2.0 %collective-permute-start.30 = (f32[8,128]{1,0:T(8,128)S(1)}, f32[8,128]{1,0:T(8,128)S(1)}, u32[]{:S(2)}, u32[]{:S(2)}) collective-permute-start(f32[8,128]{1,0:T(8,128)S(1)} %add.309.first), channel_id=1, source_target_pairs={{0,8},{1,9},{2,10},{3,11},{4,12},{5,13},{6,14},{7,15},{8,0},{9,1},... | collective-permute-start | bytes 12296 | tf_op jit(solution)/shard_map/ppermute | solution.py:421
  126.1 3.1 %collective-permute-done.30.second = f32[8,128]{1,0:T(8,128)S(1)} collective-permute-done((f32[8,128]{1,0:T(8,128)S(1)}, f32[8,128]{1,0:T(8,128)S(1)}, u32[]{:S(2)}, u32[]{:S(2)}) %collective-permute-start.30) | collective-permute-done | bytes 4128 | tf_op jit(solution)/shard_map/ppermute | solution.py:421
  130.6 2.2 %collective-permute-done.31.second = f32[8,128]{1,0:T(8,128)S(1)} collective-permute-done((f32[8,128]{1,0:T(8,128)S(1)}, f32[8,128]{1,0:T(8,128)S(1)}, u32[]{:S(2)}, u32[]{:S(2)}) %collective-permute-start.31) | collective-permute-done | bytes 4128 | tf_op jit(solution)/shard_map/ppermute | solution.py:421
  134.0 3.6 %collective-permute-done.32.second = f32[8,128]{1,0:T(8,128)S(1)} collective-permute-done((f32[8,128]{1,0:T(8,128)S(1)}, f32[8,128]{1,0:T(8,128)S(1)}, u32[]{:S(2)}, u32[]{:S(2)}) %collective-permute-start.32) | collective-permute-done | bytes 4128 | tf_op jit(solution)/shard_map/ppermute | solution.py:421
  (78 shorter events, 37.5 us)
Async XLA Ops:
  0.0 5.6 %collective-permute-start = (bf16[1024,384]{1,0:T(8,128)(2,1)}, bf16[1024,384]{1,0:T(8,128)(2,1)S(1)}, u32[]{:S(2)}, u32[]{:S(2)}) collective-permute-start(bf16[1024,384]{1,0:T(8,128)(2,1)} %bitcast.21), channel_id=1, source_target_pairs={{0,1},{1,0},{2,3},{3,2},{4,5},{5,4},{6,7},{7,6},{8,9},{9,8},{10,11... | collective-permute-start | bytes 2359304 | tf_op jit(solution)/shard_map/ppermute | solution.py:52
  1.2 14.5 %collective-permute-start.1 = (bf16[512,384]{1,0:T(8,128)(2,1)S(1)}, bf16[512,384]{1,0:T(8,128)(2,1)S(1)}, u32[]{:S(2)}, u32[]{:S(2)}) collective-permute-start(bf16[512,384]{1,0:T(8,128)(2,1)S(1)} %bitcast.23), channel_id=1, source_target_pairs={{0,8},{1,9},{2,10},{3,11},{4,12},{5,13},{6,14},{7,15},{8,0},{9,1},... | collective-permute-start | bytes 1179656 | tf_op jit(solution)/shard_map/ppermute | solution.py:48
  3.6 12.2 %collective-permute-start.2 = (bf16[512,384]{1,0:T(8,128)(2,1)S(1)}, bf16[512,384]{1,0:T(8,128)(2,1)S(1)}, u32[]{:S(2)}, u32[]{:S(2)}) collective-permute-start(bf16[512,384]{1,0:T(8,128)(2,1)S(1)} %bitcast.27), channel_id=1, source_target_pairs={{0,2},{1,7},{2,4},{3,1},{4,6},{5,3},{6,0},{7,5},{8,10},{9,15},{10,... | collective-permute-start | bytes 1179656 | tf_op jit(solution)/shard_map/ppermute | solution.py:44
  16.7 17.7 %collective-permute-start.5 = (bf16[2,512,384]{2,1,0:T(8,128)(2,1)}, bf16[2,512,384]{2,1,0:T(8,128)(2,1)S(1)}, u32[]{:S(2)}, u32[]{:S(2)}) collective-permute-start(bf16[2,512,384]{2,1,0:T(8,128)(2,1)} %stack.73), channel_id=1, source_target_pairs={{0,2},{1,7},{2,4},{3,1},{4,6},{5,3},{6,0},{7,5},{8,10},{9,15},{10,... | collective-permute-start | bytes 2359304 | tf_op jit(solution)/shard_map/ppermute | solution.py:44
  19.1 15.2 %collective-permute-start.6 = (bf16[512,384]{1,0:T(8,128)(2,1)S(1)}, bf16[512,384]{1,0:T(8,128)(2,1)S(1)}, u32[]{:S(2)}, u32[]{:S(2)}) collective-permute-start(bf16[512,384]{1,0:T(8,128)(2,1)S(1)} %collective-permute-done.2.refs_5_), channel_id=1, source_target_pairs={{0,2},{1,7},{2,4},{3,1},{4,6},{5,3},{6,0},{7,5},{8,10},{9,15},{10,... | collective-permute-start | bytes 1179656 | tf_op jit(solution)/shard_map/ppermute | solution.py:44
  20.8 13.6 %collective-permute-start.7 = (bf16[512,384]{1,0:T(8,128)(2,1)S(1)}, bf16[512,384]{1,0:T(8,128)(2,1)S(1)}, u32[]{:S(2)}, u32[]{:S(2)}) collective-permute-start(bf16[512,384]{1,0:T(8,128)(2,1)S(1)} %bitcast.28), channel_id=1, source_target_pairs={{0,8},{1,9},{2,10},{3,11},{4,12},{5,13},{6,14},{7,15},{8,0},{9,1},... | collective-permute-start | bytes 1179656 | tf_op jit(solution)/shard_map/ppermute | solution.py:48
  34.4 4.5 %collective-permute-start.8 = (bf16[2,512,384]{2,1,0:T(8,128)(2,1)S(1)}, bf16[2,512,384]{2,1,0:T(8,128)(2,1)S(1)}, u32[]{:S(2)}, u32[]{:S(2)}) collective-permute-start(bf16[2,512,384]{2,1,0:T(8,128)(2,1)S(1)} %collective-permute-done.5.refs_3_), channel_id=1, source_target_pairs={{0,1},{1,0},{2,3},{3,2},{4,5},{5,4},{6,7},{7,6},{8,9},{9,8},{10,11... | collective-permute-start | bytes 2359304 | tf_op jit(solution)/shard_map/ppermute | solution.py:52
  34.9 4.0 %collective-permute-start.9 = (bf16[512,384]{1,0:T(8,128)(2,1)S(1)}, bf16[512,384]{1,0:T(8,128)(2,1)S(1)}, u32[]{:S(2)}, u32[]{:S(2)}) collective-permute-start(bf16[512,384]{1,0:T(8,128)(2,1)S(1)} %collective-permute-done.6.refs_5_), channel_id=1, source_target_pairs={{0,1},{1,0},{2,3},{3,2},{4,5},{5,4},{6,7},{7,6},{8,9},{9,8},{10,11... | collective-permute-start | bytes 1179656 | tf_op jit(solution)/shard_map/ppermute | solution.py:52
  35.0 17.4 %collective-permute-start.11 = (bf16[2,512,384]{2,1,0:T(8,128)(2,1)S(1)}, bf16[2,512,384]{2,1,0:T(8,128)(2,1)S(1)}, u32[]{:S(2)}, u32[]{:S(2)}) collective-permute-start(bf16[2,512,384]{2,1,0:T(8,128)(2,1)S(1)} %collective-permute-done.5.refs_3_), channel_id=1, source_target_pairs={{0,2},{1,7},{2,4},{3,1},{4,6},{5,3},{6,0},{7,5},{8,10},{9,15},{10,... | collective-permute-start | bytes 2359304 | tf_op jit(solution)/shard_map/ppermute | solution.py:44
  35.7 16.7 %collective-permute-start.12 = (bf16[512,384]{1,0:T(8,128)(2,1)S(1)}, bf16[512,384]{1,0:T(8,128)(2,1)S(1)}, u32[]{:S(2)}, u32[]{:S(2)}) collective-permute-start(bf16[512,384]{1,0:T(8,128)(2,1)S(1)} %collective-permute-done.6.refs_5_), channel_id=1, source_target_pairs={{0,2},{1,7},{2,4},{3,1},{4,6},{5,3},{6,0},{7,5},{8,10},{9,15},{10,... | collective-permute-start | bytes 1179656 | tf_op jit(solution)/shard_map/ppermute | solution.py:44
  37.3 15.1 %collective-permute-start.13 = (bf16[512,384]{1,0:T(8,128)(2,1)S(1)}, bf16[512,384]{1,0:T(8,128)(2,1)S(1)}, u32[]{:S(2)}, u32[]{:S(2)}) collective-permute-start(bf16[512,384]{1,0:T(8,128)(2,1)S(1)} %collective-permute-done.2.refs_5_), channel_id=1, source_target_pairs={{0,8},{1,9},{2,10},{3,11},{4,12},{5,13},{6,14},{7,15},{8,0},{9,1},... | collective-permute-start | bytes 1179656 | tf_op jit(solution)/shard_map/ppermute | solution.py:48
  53.0 13.2 %collective-permute-start.17 = (bf16[2,512,384]{2,1,0:T(8,128)(2,1)S(1)}, bf16[2,512,384]{2,1,0:T(8,128)(2,1)S(1)}, u32[]{:S(2)}, u32[]{:S(2)}) collective-permute-start(bf16[2,512,384]{2,1,0:T(8,128)(2,1)S(1)} %collective-permute-done.11.refs_3_), channel_id=1, source_target_pairs={{0,2},{1,7},{2,4},{3,1},{4,6},{5,3},{6,0},{7,5},{8,10},{9,15},{10,... | collective-permute-start | bytes 2359304 | tf_op jit(solution)/shard_map/ppermute | solution.py:44
  53.0 13.0 %collective-permute-start.18 = (bf16[512,384]{1,0:T(8,128)(2,1)S(1)}, bf16[512,384]{1,0:T(8,128)(2,1)S(1)}, u32[]{:S(2)}, u32[]{:S(2)}) collective-permute-start(bf16[512,384]{1,0:T(8,128)(2,1)S(1)} %collective-permute-done.6.refs_5_), channel_id=1, source_target_pairs={{0,8},{1,9},{2,10},{3,11},{4,12},{5,13},{6,14},{7,15},{8,0},{9,1},... | collective-permute-start | bytes 1179656 | tf_op jit(solution)/shard_map/ppermute | solution.py:48
  66.2 5.7 %collective-permute-start.21 = (bf16[512,384]{1,0:T(8,128)(2,1)S(1)}, bf16[512,384]{1,0:T(8,128)(2,1)S(1)}, u32[]{:S(2)}, u32[]{:S(2)}) collective-permute-start(bf16[512,384]{1,0:T(8,128)(2,1)S(1)} %collective-permute-done.18.refs_3_), channel_id=1, source_target_pairs={{0,1},{1,0},{2,3},{3,2},{4,5},{5,4},{6,7},{7,6},{8,9},{9,8},{10,11... | collective-permute-start | bytes 1179656 | tf_op jit(solution)/shard_map/ppermute | solution.py:52
  66.7 12.5 %collective-permute-start.22 = (bf16[512,384]{1,0:T(8,128)(2,1)S(1)}, bf16[512,384]{1,0:T(8,128)(2,1)S(1)}, u32[]{:S(2)}, u32[]{:S(2)}) collective-permute-start(bf16[512,384]{1,0:T(8,128)(2,1)S(1)} %collective-permute-done.12.refs_5_), channel_id=1, source_target_pairs={{0,8},{1,9},{2,10},{3,11},{4,12},{5,13},{6,14},{7,15},{8,0},{9,1},... | collective-permute-start | bytes 1179656 | tf_op jit(solution)/shard_map/ppermute | solution.py:48
  79.3 12.8 %collective-permute-start.20 = (bf16[2,4,128,128]{3,2,1,0:T(8,128)(2,1)S(1)}, bf16[2,4,128,128]{3,2,1,0:T(8,128)(2,1)S(1)}, u32[]{:S(2)}, u32[]{:S(2)}) collective-permute-start(bf16[2,4,128,128]{3,2,1,0:T(8,128)(2,1)S(1)} %round.2), channel_id=1, source_target_pairs={{0,16},{16,32},{32,48},{48,64},{64,80},{80,96},{96,112},{1,17},{17... | collective-permute-start | bytes 786440 | tf_op jit(solution)/shard_map/ppermute | solution.py:57
  85.0 15.4 %collective-permute-start.24 = (bf16[2,4,128,128]{3,2,1,0:T(8,128)(2,1)S(1)}, bf16[2,4,128,128]{3,2,1,0:T(8,128)(2,1)S(1)}, u32[]{:S(2)}, u32[]{:S(2)}) collective-permute-start(bf16[2,4,128,128]{3,2,1,0:T(8,128)(2,1)S(1)} %round.3), channel_id=1, source_target_pairs={{0,16},{16,32},{32,48},{48,64},{64,80},{80,96},{96,112},{1,17},{17... | collective-permute-start | bytes 786440 | tf_op jit(solution)/shard_map/ppermute | solution.py:57
  92.7 15.4 %collective-permute-start.25 = (bf16[2,4,128,128]{3,2,1,0:T(8,128)(2,1)S(1)}, bf16[2,4,128,128]{3,2,1,0:T(8,128)(2,1)S(1)}, u32[]{:S(2)}, u32[]{:S(2)}) collective-permute-start(bf16[2,4,128,128]{3,2,1,0:T(8,128)(2,1)S(1)} %extend.2), channel_id=1, source_target_pairs={{0,16},{16,32},{32,48},{48,64},{64,80},{80,96},{96,112},{1,17},{17... | collective-permute-start | bytes 786440 | tf_op jit(solution)/shard_map/ppermute | solution.py:57
  94.6 21.8 %collective-permute-start.26 = (bf16[2,4,128,128]{3,2,1,0:T(8,128)(2,1)S(1)}, bf16[2,4,128,128]{3,2,1,0:T(8,128)(2,1)S(1)}, u32[]{:S(2)}, u32[]{:S(2)}) collective-permute-start(bf16[2,4,128,128]{3,2,1,0:T(8,128)(2,1)S(1)} %extend.2), channel_id=1, source_target_pairs={{0,48},{16,64},{32,80},{48,96},{64,112},{1,49},{17,65},{33,81},{49... | collective-permute-start | bytes 786440 | tf_op jit(solution)/shard_map/ppermute | solution.py:57
  101.1 16.6 %collective-permute-start.27 = (bf16[2,4,128,128]{3,2,1,0:T(8,128)(2,1)S(1)}, bf16[2,4,128,128]{3,2,1,0:T(8,128)(2,1)S(1)}, u32[]{:S(2)}, u32[]{:S(2)}) collective-permute-start(bf16[2,4,128,128]{3,2,1,0:T(8,128)(2,1)S(1)} %extend.3), channel_id=1, source_target_pairs={{0,16},{16,32},{32,48},{48,64},{64,80},{80,96},{96,112},{1,17},{17... | collective-permute-start | bytes 786440 | tf_op jit(solution)/shard_map/ppermute | solution.py:57
  103.2 18.3 %collective-permute-start.28 = (bf16[2,4,128,128]{3,2,1,0:T(8,128)(2,1)S(1)}, bf16[2,4,128,128]{3,2,1,0:T(8,128)(2,1)S(1)}, u32[]{:S(2)}, u32[]{:S(2)}) collective-permute-start(bf16[2,4,128,128]{3,2,1,0:T(8,128)(2,1)S(1)} %extend.3), channel_id=1, source_target_pairs={{0,48},{16,64},{32,80},{48,96},{64,112},{1,49},{17,65},{33,81},{49... | collective-permute-start | bytes 786440 | tf_op jit(solution)/shard_map/ppermute | solution.py:57
  124.0 5.1 %collective-permute-start.30 = (f32[8,128]{1,0:T(8,128)S(1)}, f32[8,128]{1,0:T(8,128)S(1)}, u32[]{:S(2)}, u32[]{:S(2)}) collective-permute-start(f32[8,128]{1,0:T(8,128)S(1)} %add.309.first), channel_id=1, source_target_pairs={{0,8},{1,9},{2,10},{3,11},{4,12},{5,13},{6,14},{7,15},{8,0},{9,1},... | collective-permute-start | bytes 12296 | tf_op jit(solution)/shard_map/ppermute | solution.py:421
  129.2 3.6 %collective-permute-start.31 = (f32[8,128]{1,0:T(8,128)S(1)}, f32[8,128]{1,0:T(8,128)S(1)}, u32[]{:S(2)}, u32[]{:S(2)}) collective-permute-start(f32[8,128]{1,0:T(8,128)S(1)} %add.310.first), channel_id=1, source_target_pairs={{0,2},{1,3},{2,0},{3,1},{4,6},{5,7},{6,4},{7,5},{8,10},{9,11},{10,... | collective-permute-start | bytes 12296 | tf_op jit(solution)/shard_map/ppermute | solution.py:421
  132.8 4.8 %collective-permute-start.32 = (f32[8,128]{1,0:T(8,128)S(1)}, f32[8,128]{1,0:T(8,128)S(1)}, u32[]{:S(2)}, u32[]{:S(2)}) collective-permute-start(f32[8,128]{1,0:T(8,128)S(1)} %add.311.first), channel_id=1, source_target_pairs={{0,6},{1,7},{2,4},{3,5},{4,2},{5,3},{6,0},{7,1},{8,14},{9,15},{10,... | collective-permute-start | bytes 12296 | tf_op jit(solution)/shard_map/ppermute | solution.py:421
  (15 other events, 73.7 us)

commit v3 on v2

--- a/solution.py
+++ b/solution.py
@@ -19,8 +19,9 @@
 HBM = pl.BlockSpec(memory_space=pltpu.HBM)
 SMEM = pl.BlockSpec(memory_space=pltpu.SMEM)
 VMEM = pl.BlockSpec(memory_space=pltpu.VMEM)
-PIECES = [(0, 0), (0, 1), (1, 0), (0, 2), (1, 1), (0, 3), (1, 2), (1, 3)]
+PIECES = [(0, 0), (1, 0), (0, 1), (0, 2), (1, 1), (0, 3), (1, 2), (1, 3)]
 PIECE = 2 * SHARD
+CTX = 1 + 2 * len(PIECES)
 
 
 def tp_route(step):
@@ -57,6 +58,10 @@
     return lax.ppermute(x, "ctx", [(i, i + distance) for i in range(n - distance)])
 
 
+def swapped(x, bit):
+    return lax.ppermute(x, "ctx", [(i, i ^ bit) for i in range(lax.axis_size("ctx"))])
+
+
 def doc_ends(lengths, seq):
     first = lengths[seq, 0]
     second = first + lengths[seq, 1]
@@ -75,14 +80,14 @@
     n_x, parts, loads, n_held, n_w, n_acc = plan
     refs = list(refs)
     take = lambda n: [refs.pop(0) for _ in range(n)]
-    meta, lengths, decay = take(3)
+    meta, lengths, decay = take(3) if mode in ("kv", "qg") else (take(1)[0], None, None)
     xs = take(n_x)
     held = take(n_held)
     weights = take(4) if loads else []
     accs = take(n_acc)
     if mode == "qg":
         k_in, v_in, gain = take(3)
-    outs = take({"first": 8, "more": n_acc, "kv": 3, "qg": 3}[mode])
+    outs = take({"first": 4, "more": len(parts) * 4, "kv": 4, "qg": 3}[mode])
     loaded = take(len(loads))
     xbuf, xsem, wsem = take(3)
     held = held + loaded
@@ -111,10 +116,21 @@
         for i in range(len(parts[p])):
             for copy in x_copies(p, i):
                 copy.start()
-    for i in range(len(loads)):
-        for n in range(4):
+    def start_loads(chosen):
+        for i in chosen:
+            for n in range(4):
+                for copy in w_copies(i, n):
+                    copy.start()
+
+    now = len({w for pieces in parts for _, w in pieces if w >= n_held})
+    waited = set()
+    start_loads(range(now))
+
+    def load(i, n):
+        if i >= 0 and (i, n) not in waited:
+            waited.add((i, n))
             for copy in w_copies(i, n):
-                copy.start()
+                copy.wait()
 
     def product(p, n, acc):
         total = None if acc is None else acc[...]
@@ -122,9 +138,9 @@
             if n in (0, 2 if mode == "qg" else 0):
                 for copy in x_copies(p, i):
                     copy.wait()
-            if mode == "first":
-                for copy in w_copies(0, n):
-                    copy.wait()
+            load(w - n_held, n)
+            if (p, n, i) == (0, 0, 0):
+                start_loads(range(now, len(loads)))
             got = jnp.dot(
                 xbuf[p, :, pl.ds(i * PIECE, PIECE)], held[w][n], preferred_element_type=F32
             )
@@ -138,17 +154,15 @@
 
     heads = WIDTH // HEAD
     if mode == "first":
-        half = xbuf.shape[1] // 2
         for n in range(4):
-            got = product(0, n, None)
-            outs[n][...] = got[:half]
-            outs[4 + n][...] = got[half:]
+            outs[n][...] = product(0, n, None)
     if mode == "more":
         for p in range(len(parts)):
             for n in range(4):
-                outs[4 * p + n][...] = product(p, n, accs[4 * p + n])
+                k = 4 * p + n
+                outs[k][...] = product(p, n, accs[k] if k < n_acc else None)
     if mode == "kv":
-        k_out, v_out, s_out = outs
+        k_out, v_out, s_out, s_half = outs
         k_out[...] = jax.nn.silu(product(0, 0, accs[0])).astype(BF16)
         v_out[...] = jax.nn.silu(product(0, 1, accs[1])).astype(BF16)
         local = lax.broadcasted_iota(jnp.int32, (BLOCK, HEAD), 0)
@@ -158,9 +172,11 @@
             for h in range(heads):
                 scale = jnp.where(keep, decay_of(decay[h], BLOCK - 1 - local), 0.0)
                 weighted = (k_out[part(s, h)].astype(F32) * scale).astype(BF16)
-                s_out[s, h] = lax.dot_general(
+                state = lax.dot_general(
                     weighted, v_out[part(s, h)], (((0,), (0,)), ((), ())), preferred_element_type=F32
                 )
+                s_out[s, h] = state
+                s_half[s, h] = state.astype(BF16)
     if mode == "qg":
         q_out, inner_out, gate_out = outs
         q_out[...] = jax.nn.silu(product(0, 2, accs[0])).astype(BF16)
@@ -184,11 +200,9 @@
                 inner_out[part(s, h)] = jnp.dot(
                     mixed, v_in[part(s, h)], preferred_element_type=F32
                 )
-    done = 1 if mode == "first" else 0
-    for i in range(done, len(loads)):
+    for i in range(len(loads)):
         for n in range(4):
-            for copy in w_copies(i, n):
-                copy.wait()
+            load(i, n)
 
 
 def project(mode, scalars, parts, held, weights=(), loads=(), accs=(), extra=(), first_seq=0):
@@ -208,28 +222,35 @@
         plan_parts.append(plan)
     numbers = used + list(loads)
     plan_parts = [[(where, numbers.index(number)) for where, number in plan] for plan in plan_parts]
-    rows = arrays[0].shape[-2]
+    index = parts[0][0][0][2]
+    rows = index.size if isinstance(index, pl.Slice) else arrays[0].shape[-2]
     half = jax.ShapeDtypeStruct((rows, WIDTH), BF16)
     wide = pltpu.VMEM((rows, WIDTH), F32)
-    state = jax.ShapeDtypeStruct((rows // BLOCK, WIDTH // HEAD, HEAD, HEAD), F32)
+    state = [
+        jax.ShapeDtypeStruct((rows // BLOCK, WIDTH // HEAD, HEAD, HEAD), t) for t in (F32, BF16)
+    ]
     outs = {
-        "first": [pltpu.VMEM((rows // 2, WIDTH), F32)] * 8,
-        "more": [wide] * len(accs),
-        "kv": [half, half, state],
+        "first": [wide] * 4,
+        "more": [wide] * (4 * len(parts)),
+        "kv": [half, half, *state],
         "qg": [half, wide, wide],
     }[mode]
     n_outs = len(outs)
+    if mode in ("first", "more"):
+        scalars = scalars[:1]
     outs = outs + [pltpu.VMEM((4, PIECE, WIDTH), BF16)] * len(loads)
     most = max(len(p) for p in plan_parts)
+    if mode == "first":
+        arrays = [pltpu.with_memory_space_constraint(x, pltpu.HBM) for x in arrays]
     loading = [pltpu.with_memory_space_constraint(w, pltpu.HBM) for w in weights] if loads else []
-    before = 3 + len(arrays) + len(used) + len(loading)
+    before = len(scalars) + len(arrays) + len(used) + len(loading)
     aliases = {before + n: n for n in range(len(accs))} if mode == "more" else {}
     plan = (len(arrays), plan_parts, list(loads), len(used), 4, len(accs))
     got = pl.pallas_call(
         functools.partial(project_kernel, mode, first_seq, plan),
         out_shape=outs,
-        in_specs=[SMEM] * 3
-        + [ANY] * len(arrays)
+        in_specs=[SMEM] * len(scalars)
+        + [HBM if mode == "first" else ANY] * len(arrays)
         + [VMEM] * len(used)
         + [HBM] * len(loading)
         + [VMEM] * (len(accs) + len(extra)),
@@ -260,6 +281,30 @@
     return jnp.where(keep, jnp.exp(rate), 0.0)[0:1, :]
 
 
+def one_or(condition, share):
+    return jnp.where(condition, 1.0, share)
+
+
+def pair_kernel(first_seq, meta, lengths, decay, state, before, out):
+    odd = meta[CTX] % 2 == 1
+    for s in range(state.shape[0]):
+        for h in range(state.shape[1]):
+            share = functools.partial(carried_share, meta, lengths, decay, first_seq + s, h)
+            mine, other = one_or(odd, share(-1)), one_or(jnp.logical_not(odd), share(0))
+            out[s, h] = (mine * state[s, h] + other * before[s, h].astype(F32)).astype(BF16)
+
+
+def quad_kernel(first_seq, meta, lengths, decay, state, before, out):
+    odd, high = meta[CTX] % 2, meta[CTX] // 2 % 2 == 1
+    for s in range(state.shape[0]):
+        for h in range(state.shape[1]):
+            share = functools.partial(carried_share, meta, lengths, decay, first_seq + s, h)
+            mine = one_or(high, share(odd - 2) * share(odd - 3))
+            other = one_or(jnp.logical_not(high), share(odd) * share(odd - 1))
+            got = mine * state[s, h].astype(F32) + other * before[s, h].astype(F32)
+            out[s, h] = got.astype(BF16)
+
+
 def extend_kernel(first_seq, meta, lengths, decay, state, before, out):
     for s in range(state.shape[0]):
         for h in range(state.shape[1]):
@@ -267,9 +312,9 @@
             out[s, h] = (state[s, h] + share * before[s, h].astype(F32)).astype(BF16)
 
 
-def extend(scalars, state, before, first_seq):
+def extend(kernel, scalars, state, before, first_seq):
     return pl.pallas_call(
-        functools.partial(extend_kernel, first_seq),
+        functools.partial(kernel, first_seq),
         out_shape=jax.ShapeDtypeStruct(state.shape, BF16),
         in_specs=[SMEM] * 3 + [VMEM] * 2,
         out_specs=VMEM,
@@ -278,23 +323,20 @@
     )(*scalars, state, before)
 
 
-def round_kernel(x, out):
-    out[...] = x[...].astype(BF16)
-
-
-def rounded(x):
-    return pl.pallas_call(
-        round_kernel,
-        out_shape=jax.ShapeDtypeStruct(x.shape, BF16),
-        in_specs=[VMEM],
-        out_specs=VMEM,
-        compiler_params=pltpu.CompilerParams(vmem_limit_bytes=LIMIT * 2**20),
-        name="round",
-    )(x)
-
-
-def combine_kernel(first_seq, meta, lengths, decay, query, inner, near, far, attn_out, squares_out):
-    seqs, heads = near.shape[:2]
+def shares(scan, meta, share):
+    if not scan:
+        return [1.0, share(1) * share(2)]
+    place = meta[CTX] % 4
+    odd, high = place % 2 == 1, place >= 2
+    first = jnp.where(odd, 1.0, jnp.zeros((1, HEAD), F32))
+    second = jnp.where(high, one_or(jnp.logical_not(odd), share(1)), 0.0)
+    third = one_or(place < 1, share(1)) * one_or(place < 2, share(2)) * one_or(place < 3, share(3))
+    return [first, second, third]
+
+
+def combine_kernel(scan, first_seq, meta, lengths, decay, query, inner, *refs):
+    arrived, (attn_out, squares_out) = refs[:-2], refs[-2:]
+    seqs, heads = arrived[0].shape[:2]
     offset = meta[0]
     local = lax.broadcasted_iota(jnp.int32, (BLOCK, HEAD), 0)
     for s in range(seqs):
@@ -304,9 +346,10 @@
         rows = pl.ds(s * BLOCK, BLOCK)
         for h in range(heads):
             columns = pl.ds(h * HEAD, HEAD)
-            share = carried_share(meta, lengths, decay, first_seq + s, h, 1)
-            share = share * carried_share(meta, lengths, decay, first_seq + s, h, 2)
-            incoming = near[s, h].astype(F32) + share * far[s, h].astype(F32)
+            share = functools.partial(carried_share, meta, lengths, decay, first_seq + s, h)
+            incoming = sum(
+                weight * x[s, h].astype(F32) for weight, x in zip(shares(scan, meta, share), arrived)
+            )
             high = incoming.astype(BF16)
             low = (incoming - high.astype(F32)).astype(BF16)
             q = query[rows, columns]
@@ -321,19 +364,19 @@
             squares_out[pl.ds(s * (BLOCK // HEAD) + i, 1), :] = line[:, i * HEAD : (i + 1) * HEAD]
 
 
-def combine(scalars, query, inner, near, far, first_seq):
+def combine(scan, scalars, query, inner, arrived, first_seq):
     rows = query.shape[0]
     return pl.pallas_call(
-        functools.partial(combine_kernel, first_seq),
+        functools.partial(combine_kernel, scan, first_seq),
         out_shape=[
             pltpu.VMEM((rows, WIDTH), F32),
             jax.ShapeDtypeStruct((rows // HEAD, HEAD), F32),
         ],
-        in_specs=[SMEM] * 3 + [VMEM] * 4,
+        in_specs=[SMEM] * 3 + [VMEM] * (2 + len(arrived)),
         out_specs=[VMEM] * 2,
         compiler_params=pltpu.CompilerParams(vmem_limit_bytes=LIMIT * 2**20),
         name="combine",
-    )(*scalars, query, inner, near, far)
+    )(*scalars, query, inner, *arrived)
 
 
 def finish_kernel(width_all, attn_y, attn_z, gate_y, gate_z, squares, out):
@@ -437,6 +480,7 @@
             c = (my_c + core) % 2
             z = (my_z + j * (2 * c - 1) + 4) % 4
             meta.append((my_y + flip) % 2 * 8 + z * 2 + c)
+    meta.append(lax.axis_index("ctx"))
     scalars = (jnp.stack(meta), doc_lengths, decay_rate)
     half = seqs // 2
     rows = hidden.reshape(seqs * BLOCK, SHARD)
@@ -455,51 +499,56 @@
         return [((x, other, flip), at(flip, j)) for flip in (0, 1)]
 
     y0, r1 = across(part_y), ring(part_z)
-    acc = project("first", scalars, [one(rows, 0, 0)], held, weights, [0, 1, 2])
+    rows_other = other_core(rows)
+    own_y, own_z = [
+        ((rows, rows_other, pl.ds(p * half * BLOCK, half * BLOCK)), at(0, 0)) for p in (0, 1)
+    ]
+    acc = project("first", scalars, [[own_y]], held, weights, [0, 1])
     acc, y0, r1, part_z = in_order(acc, y0, r1, part_z)
 
-    a1, r2, far0 = ring(stack(part_y, y0)), ring(r1), across(part_z)
-    acc = project("more", scalars, [one(y0, 1, 0), one(r1, 0, 1)], held, weights, [3, 4], acc)
-    acc, a1, r2, far0, r1 = in_order(acc, a1, r2, far0, r1)
-
-    a2, r3, far1 = ring(a1), ring(r2), across(r1)
-    acc = project(
-        "more", scalars, [two(a1, 1), one(r2, 0, 2) + one(far0, 1, 0)], held, weights, [5, 6], acc
+    a1, r2, far_a = ring(stack(part_y, y0)), ring(r1), across(stack(part_z, r1))
+    parts = [one(y0, 1, 0), [own_z] + one(r1, 0, 1)]
+    acc = project("more", scalars, parts, held, weights, [2, 3, 4], acc)
+    acc, a1, r2, far_a = in_order(acc, a1, r2, far_a)
+
+    a2, r3, far2 = ring(a1), ring(r2), across(r2)
+    parts = [two(a1, 1), one(r2, 0, 2) + [(x, at(1, i)) for i, (x, _) in enumerate(two(far_a, 0))]]
+    acc = project("more", scalars, parts, held, weights, [5, 6], acc)
+    acc, a2, r3, far2 = in_order(acc, a2, r3, far2)
+
+    a3, far3 = ring(a2), across(r3)
+    parts = [two(a2, 2), one(r3, 0, 3) + one(far2, 1, 2)]
+    acc = project("more", scalars, parts, held, weights, [7], acc)
+    acc, a3, far3 = in_order(acc, a3, far3)
+
+    last_y, last_z = [two(a3, 3)], [one(far3, 1, 3)]
+    keys_y, values_y, state_y, sent_y = project("kv", scalars, last_y, held, accs=acc[:2])
+    one_y = swapped(sent_y, 1)
+    acc, state_y = in_order(acc, state_y)
+    keys_z, values_z, state_z, sent_z = project(
+        "kv", scalars, last_z, held, accs=acc[4:6], first_seq=half
     )
-    acc, a2, r3, far1, r2 = in_order(acc, a2, r3, far1, r2)
-
-    a3, far2 = ring(a2), across(r2)
-    acc = project(
-        "more", scalars, [two(a2, 2), one(r3, 0, 3) + one(far1, 1, 1)], held, weights, [7], acc
+    before_z = ahead(sent_z, 1)
+    acc, state_z = in_order(acc, state_z)
+    query_y, inner_y, gate_y = project(
+        "qg", scalars, last_y, held, accs=acc[2:4], extra=(keys_y, values_y, gain)
     )
-    acc, a3, far2, r3 = in_order(acc, a3, far2, r3)
-
-    far3 = across(r3)
-    last_y = [two(a3, 3)]
-    keys_y, values_y, state_y = project("kv", scalars, last_y, held, accs=acc[:2])
-    before_y = ahead(rounded(state_y), 1)
-    acc_z = project("more", scalars, [one(far2, 1, 2)], held, accs=in_order(acc[4:], state_y)[0])
-    acc_z, far3 = in_order(acc_z, far3)
-
-    last_z = [one(far3, 1, 3)]
-    keys_z, values_z, state_z = project("kv", scalars, last_z, held, accs=acc_z[:2], first_seq=half)
-    before_z = ahead(rounded(state_z), 1)
-    acc_y, before_y, state_z = in_order(acc[2:4], before_y, state_z)
-    longer_y = extend(scalars, state_y, before_y, 0)
-    near_y, far_y = ahead(longer_y, 1), ahead(longer_y, 3)
-    query_y, inner_y, gate_y = project(
-        "qg", scalars, last_y, held, accs=acc_y, extra=(keys_y, values_y, gain)
+    query_y, one_y, acc = in_order(query_y, one_y, acc)
+    pair_y = extend(pair_kernel, scalars, state_y, one_y, 0)
+    two_y = swapped(pair_y, 2)
+    before_z, pair_y = in_order(before_z, pair_y)
+    longer_z = extend(extend_kernel, scalars, state_z, before_z, half)
+    near_z, far_z = ahead(longer_z, 1), ahead(longer_z, 3)
+    acc, longer_z = in_order(acc, longer_z)
+    query_z, inner_z, gate_z = project(
+        "qg", scalars, last_z, held, accs=acc[6:], extra=(keys_z, values_z, gain), first_seq=half
     )
-    query_y, before_z, acc_q = in_order(query_y, before_z, acc_z[2:])
-    longer_z = extend(scalars, state_z, before_z, half)
-    near_z, far_z = ahead(longer_z, 1), ahead(longer_z, 3)
-    query_z, inner_z, gate_z = project(
-        "qg", scalars, last_z, held, accs=acc_q, extra=(keys_z, values_z, gain), first_seq=half
-    )
-    query_z, near_y, far_y = in_order(query_z, near_y, far_y)
-    attn_y, squares_y = combine(scalars, query_y, inner_y, near_y, far_y, 0)
-    squares_y, near_z, far_z = in_order(squares_y, near_z, far_z)
-    attn_z, squares_z = combine(scalars, query_z, inner_z, near_z, far_z, half)
+    query_z, two_y = in_order(query_z, two_y)
+    four_y = ahead(extend(quad_kernel, scalars, pair_y, two_y, 0), 4)
+    query_z, near_z, far_z = in_order(query_z, near_z, far_z)
+    attn_z, squares_z = combine(False, scalars, query_z, inner_z, (near_z, far_z), half)
+    squares_z, four_y = in_order(squares_z, four_y)
+    attn_y, squares_y = combine(True, scalars, query_y, inner_y, (one_y, two_y, four_y), 0)
     squares = all_sum(join(squares_y, squares_z))
     return finish((attn_y, attn_z), (gate_y, gate_z), squares)
 

time: 139 us -> 133 us (0.957)
  the two profiles are of different devices: /device:TPU:8 before, /device:TPU:0 now
where the time goes in v3:
time: 133 us; the launch traced here: 132 us
  Pallas kernels  50.5 us (38%)
  starting transfers between devices  48.1 us (36%)
  waiting for transfers between devices  31.3 us (24%)
  local copies, waits for them, and re-layouts  2.2 us (2%)
    pallas_call x8, Pallas kernels, project(): pl.pallas_call(functools.partial(project_kernel, mode, first_seq, plan),...  42.7 us
    ppermute x4, starting transfers between devices, ahead(): lax.ppermute(x, 'ctx', [(i, i + distance) for i in range(n - distance)])  13.5 us
    ppermute x4, starting transfers between devices, across(): return lax.ppermute(x, 'tp', ACROSS)  12.2 us
    ppermute x6, starting transfers between devices, ring(): return lax.ppermute(x, 'tp', RING)  10.1 us
    ppermute x4, waiting for transfers between devices, all_sum(): x = add(x, lax.ppermute(x, 'tp', route))  9.66 us
    ppermute x4, waiting for transfers between devices, ahead(): lax.ppermute(x, 'ctx', [(i, i + distance) for i in range(n - distance)])  8.1 us
    ppermute x6, waiting for transfers between devices, ring(): return lax.ppermute(x, 'tp', RING)  8.06 us
    ppermute x4, starting transfers between devices, all_sum(): x = add(x, lax.ppermute(x, 'tp', route))  5.12 us
  transfers between devices with their start and end apart: 31, of which 11 were waited for; matrix products, arithmetic and copies ran while one was open for 1% of the time, Pallas kernels for 36%

profile of v3, /device:TPU:0, one launch (start us, length us, event | category | flops | bytes accessed | tf_op | source)
XLA Modules:
  0.0 132.5 jit_solution(6942489509843671098)
XLA Ops:
  1.2 3.4 %collective-permute-start.1 = (bf16[512,384]{1,0:T(8,128)(2,1)S(1)}, bf16[512,384]{1,0:T(8,128)(2,1)S(1)}, u32[]{:S(2)}, u32[]{:S(2)}) collective-permute-start(bf16[512,384]{1,0:T(8,128)(2,1)S(1)} %bitcast.27), channel_id=1, source_target_pairs={{0,8},{1,9},{2,10},{3,11},{4,12},{5,13},{6,14},{7,15},{8,0},{9,1},... | collective-permute-start | bytes 1179656 | tf_op jit(solution)/shard_map/ppermute | solution.py:49
  7.5 5.0 %project_first.1 = (f32[512,512]{1,0:T(8,128)S(1)}, f32[512,512]{1,0:T(8,128)S(1)}, f32[512,512]{1,0:T(8,128)S(1)}, f32[512,512]{1,0:T(8,128)S(1)}, bf16[4,768,5...) custom-call(s32[18]{0:T(128)S(1)} %stack.77.refs_0_.meta, bf16[1024,384]{1,0:T(8,128)(2,1)} %bitcast.23, ...), custom_call_target="tpu_custom_call" | custom-call | flops 1610612736 | bytes 786432 | tf_op jit(solution)/shard_map/project_first/pallas_call | solution.py:249
  16.7 3.3 %collective-permute-start.7 = (bf16[2,512,384]{2,1,0:T(8,128)(2,1)}, bf16[2,512,384]{2,1,0:T(8,128)(2,1)S(1)}, u32[]{:S(2)}, u32[]{:S(2)}) collective-permute-start(bf16[2,512,384]{2,1,0:T(8,128)(2,1)} %stack.79), channel_id=1, source_target_pairs={{0,8},{1,9},{2,10},{3,11},{4,12},{5,13},{6,14},{7,15},{8,0},{9,1},... | collective-permute-start | bytes 2359304 | tf_op jit(solution)/shard_map/ppermute | solution.py:49
  21.9 1.9 %collective-permute-start.6 = (bf16[512,384]{1,0:T(8,128)(2,1)S(1)}, bf16[512,384]{1,0:T(8,128)(2,1)S(1)}, u32[]{:S(2)}, u32[]{:S(2)}) collective-permute-start(bf16[512,384]{1,0:T(8,128)(2,1)S(1)} %collective-permute-done.2.refs_5_.second), channel_id=1, source_target_pairs={{0,2},{1,7},{2,4},{3,1},{4,6},{5,3},{6,0},{7,5},{8,10},{9,15},{10,... | collective-permute-start | bytes 1179656 | tf_op jit(solution)/shard_map/ppermute | solution.py:45
  23.9 7.4 %project_more.3 = (f32[512,512]{1,0:T(8,128)S(1)}, f32[512,512]{1,0:T(8,128)S(1)}, f32[512,512]{1,0:T(8,128)S(1)}, f32[512,512]{1,0:T(8,128)S(1)}, f32[512,512]{...) custom-call(s32[18]{0:T(128)S(1)} %stack.77.refs_0_.meta, ...), custom_call_target="tpu_custom_call", output_to_operand_aliasing={{0}: (13, {}), {1}: (14, {}), {2}: (15, {}), {3}: (16, {})} | custom-call | flops 4831838208 | bytes 786432 | tf_op jit(solution)/shard_map/project_more/pallas_call | solution.py:249
  31.2 7.2 %collective-permute-done.6.refs_3_ = bf16[512,384]{1,0:T(8,128)(2,1)S(1)} collective-permute-done((bf16[512,384]{1,0:T(8,128)(2,1)S(1)}, bf16[512,384]{1,0:T(8,128)(2,1)S(1)}, u32[]{:S(2)}, u32[]{:S(2)}) %collective-permute-start.6) | collective-permute-done | bytes 393248 | tf_op jit(solution)/shard_map/ppermute | solution.py:45
  40.4 1.9 %collective-permute-start.12 = (bf16[512,384]{1,0:T(8,128)(2,1)S(1)}, bf16[512,384]{1,0:T(8,128)(2,1)S(1)}, u32[]{:S(2)}, u32[]{:S(2)}) collective-permute-start(bf16[512,384]{1,0:T(8,128)(2,1)S(1)} %collective-permute-done.6.refs_3_), channel_id=1, source_target_pairs={{0,2},{1,7},{2,4},{3,1},{4,6},{5,3},{6,0},{7,5},{8,10},{9,15},{10,... | collective-permute-start | bytes 1179656 | tf_op jit(solution)/shard_map/ppermute | solution.py:45
  42.4 3.1 %collective-permute-start.13 = (bf16[512,384]{1,0:T(8,128)(2,1)S(1)}, bf16[512,384]{1,0:T(8,128)(2,1)S(1)}, u32[]{:S(2)}, u32[]{:S(2)}) collective-permute-start(bf16[512,384]{1,0:T(8,128)(2,1)S(1)} %collective-permute-done.6.refs_3_), channel_id=1, source_target_pairs={{0,8},{1,9},{2,10},{3,11},{4,12},{5,13},{6,14},{7,15},{8,0},{9,1},... | collective-permute-start | bytes 1179656 | tf_op jit(solution)/shard_map/ppermute | solution.py:49
  45.5 10.3 %project_more.4 = (f32[512,512]{1,0:T(8,128)S(1)}, f32[512,512]{1,0:T(8,128)S(1)}, f32[512,512]{1,0:T(8,128)S(1)}, f32[512,512]{1,0:T(8,128)S(1)}, f32[512,512]{...) custom-call(s32[18]{0:T(128)S(1)} %stack.77.refs_0_.meta, ...), custom_call_target="tpu_custom_call", output_to_operand_aliasing={{0}: (15, {}), {1}: (16, {}), {2}: (17, {}), {3}: (18, {}),... | custom-call | flops 8053063680 | bytes 786432 | tf_op jit(solution)/shard_map/project_more/pallas_call | solution.py:249
  58.4 2.4 %collective-permute-start.18 = (bf16[512,384]{1,0:T(8,128)(2,1)S(1)}, bf16[512,384]{1,0:T(8,128)(2,1)S(1)}, u32[]{:S(2)}, u32[]{:S(2)}) collective-permute-start(bf16[512,384]{1,0:T(8,128)(2,1)S(1)} %collective-permute-done.12.refs_3_), channel_id=1, source_target_pairs={{0,8},{1,9},{2,10},{3,11},{4,12},{5,13},{6,14},{7,15},{8,0},{9,1},... | collective-permute-start | bytes 1179656 | tf_op jit(solution)/shard_map/ppermute | solution.py:49
  60.8 8.5 %project_more.5 = (f32[512,512]{1,0:T(8,128)S(1)}, f32[512,512]{1,0:T(8,128)S(1)}, f32[512,512]{1,0:T(8,128)S(1)}, f32[512,512]{1,0:T(8,128)S(1)}, f32[512,512]{...) custom-call(s32[18]{0:T(128)S(1)} %stack.77.refs_0_.meta, ...), custom_call_target="tpu_custom_call", output_to_operand_aliasing={{0}: (14, {}), {1}: (15, {}), {2}: (16, {}), {3}: (17, {}),... | custom-call | flops 6442450944 | bytes 786432 | tf_op jit(solution)/shard_map/project_more/pallas_call | solution.py:249
  73.6 3.2 %project_kv.2 = (bf16[512,512]{1,0:T(8,128)(2,1)S(1)}, bf16[512,512]{1,0:T(8,128)(2,1)S(1)}, f32[2,4,128,128]{3,2,1,0:T(8,128)S(1)}, bf16[2,4,128,128]{3,2,1,0:T(8,128)(2,1)S(1)}) custom-call(s32[18]{0:T(128)S(1)} %stack.77.refs_0_.meta, s32[4,4]{1,0:T(4,128)S(1)} %copy-done.3, f32[4]{0:T(128)S(1)} %copy-done.4, ...), custom_call_target="tpu_custom_call" | custom-call | flops 1610612736 | bytes 786432 | tf_op jit(solution)/shard_map/project_kv/pallas_call | solution.py:249
  78.5 2.3 %project_kv.3 = (bf16[512,512]{1,0:T(8,128)(2,1)S(1)}, bf16[512,512]{1,0:T(8,128)(2,1)S(1)}, f32[2,4,128,128]{3,2,1,0:T(8,128)S(1)}, bf16[2,4,128,128]{3,2,1,0:T(8,128)(2,1)S(1)}) custom-call(s32[18]{0:T(128)S(1)} %stack.77.refs_0_.meta, s32[4,4]{1,0:T(4,128)S(1)} %copy-done.3, f32[4]{0:T(128)S(1)} %copy-done.4, ...), custom_call_target="tpu_custom_call" | custom-call | flops 805306368 | bytes 786432 | tf_op jit(solution)/shard_map/project_kv/pallas_call | solution.py:249
  80.8 2.5 %collective-permute-start.22 = (bf16[2,4,128,128]{3,2,1,0:T(8,128)(2,1)S(1)}, bf16[2,4,128,128]{3,2,1,0:T(8,128)(2,1)S(1)}, u32[]{:S(2)}, u32[]{:S(2)}) collective-permute-start(bf16[2,4,128,128]{3,2,1,0:T(8,128)(2,1)S(1)} %get-tuple-element.222), channel_id=1, source_target_pairs={{0,16},{16,32},{32,48},{48,64},{64,80},{80,96},{96,112},{1,17},{17... | collective-permute-start | bytes 786440 | tf_op jit(solution)/shard_map/ppermute | solution.py:58
  83.3 3.5 %project_qg.2 = (bf16[512,512]{1,0:T(8,128)(2,1)S(1)}, f32[512,512]{1,0:T(8,128)S(1)}, f32[512,512]{1,0:T(8,128)S(1)}) custom-call(s32[18]{0:T(128)S(1)} %stack.77.refs_0_.meta, s32[4,4]{1,0:T(4,128)S(1)} %copy-done.3, f32[4]{0:T(128)S(1)} %copy-done.4, bf16[2,512,384]{2,1,0:T(8,128)(2,1)S(1)} %collective-permute-done.17.refs_3_, ...), custom_call_target="tpu_custom_call" | custom-call | flops 1610612736 | bytes 786432 | tf_op jit(solution)/shard_map/project_qg/pallas_call | solution.py:249
  87.5 3.1 %collective-permute-start.23 = (bf16[2,4,128,128]{3,2,1,0:T(8,128)(2,1)S(1)}, bf16[2,4,128,128]{3,2,1,0:T(8,128)(2,1)S(1)}, u32[]{:S(2)}, u32[]{:S(2)}) collective-permute-start(bf16[2,4,128,128]{3,2,1,0:T(8,128)(2,1)S(1)} %extend.3.state), channel_id=1, source_target_pairs={{0,32},{16,48},{32,0},{48,16},{64,96},{80,112},{96,64},{112,80},{1... | collective-permute-start | bytes 786440 | tf_op jit(solution)/shard_map/ppermute | solution.py:62
  91.2 4.0 %collective-permute-start.24 = (bf16[2,4,128,128]{3,2,1,0:T(8,128)(2,1)S(1)}, bf16[2,4,128,128]{3,2,1,0:T(8,128)(2,1)S(1)}, u32[]{:S(2)}, u32[]{:S(2)}) collective-permute-start(bf16[2,4,128,128]{3,2,1,0:T(8,128)(2,1)S(1)} %extend.4), channel_id=1, source_target_pairs={{0,16},{16,32},{32,48},{48,64},{64,80},{80,96},{96,112},{1,17},{17... | collective-permute-start | bytes 786440 | tf_op jit(solution)/shard_map/ppermute | solution.py:58
  95.3 5.7 %collective-permute-start.25 = (bf16[2,4,128,128]{3,2,1,0:T(8,128)(2,1)S(1)}, bf16[2,4,128,128]{3,2,1,0:T(8,128)(2,1)S(1)}, u32[]{:S(2)}, u32[]{:S(2)}) collective-permute-start(bf16[2,4,128,128]{3,2,1,0:T(8,128)(2,1)S(1)} %extend.4), channel_id=1, source_target_pairs={{0,48},{16,64},{32,80},{48,96},{64,112},{1,49},{17,65},{33,81},{49... | collective-permute-start | bytes 786440 | tf_op jit(solution)/shard_map/ppermute | solution.py:58
  101.0 2.6 %project_qg.3 = (bf16[512,512]{1,0:T(8,128)(2,1)S(1)}, f32[512,512]{1,0:T(8,128)S(1)}, f32[512,512]{1,0:T(8,128)S(1)}) custom-call(s32[18]{0:T(128)S(1)} %stack.77.refs_0_.meta, s32[4,4]{1,0:T(4,128)S(1)} %copy-done.3, f32[4]{0:T(128)S(1)} %copy-done.4, bf16[512,384]{1,0:T(8,128)(2,1)S(1)} %collective-permute-done.18.refs_3_, ...), custom_call_target="tpu_custom_call" | custom-call | flops 805306368 | bytes 786432 | tf_op jit(solution)/shard_map/project_qg/pallas_call | solution.py:249
  106.9 8.1 %collective-permute-done.26.refs_2_ = bf16[2,4,128,128]{3,2,1,0:T(8,128)(2,1)S(1)} collective-permute-done((bf16[2,4,128,128]{3,2,1,0:T(8,128)(2,1)S(1)}, bf16[2,4,128,128]{3,2,1,0:T(8,128)(2,1)S(1)}, u32[]{:S(2)}, u32[]{:S(2)}) %collective-permute-start.26) | collective-permute-done | bytes 262176 | tf_op jit(solution)/shard_map/ppermute | solution.py:58
  117.6 2.6 %collective-permute-start.28 = (f32[8,128]{1,0:T(8,128)S(1)}, f32[8,128]{1,0:T(8,128)S(1)}, u32[]{:S(2)}, u32[]{:S(2)}) collective-permute-start(f32[8,128]{1,0:T(8,128)S(1)} %add.309.first), channel_id=1, source_target_pairs={{0,8},{1,9},{2,10},{3,11},{4,12},{5,13},{6,14},{7,15},{8,0},{9,1},... | collective-permute-start | bytes 12296 | tf_op jit(solution)/shard_map/ppermute | solution.py:464
  120.2 2.5 %collective-permute-done.28.second = f32[8,128]{1,0:T(8,128)S(1)} collective-permute-done((f32[8,128]{1,0:T(8,128)S(1)}, f32[8,128]{1,0:T(8,128)S(1)}, u32[]{:S(2)}, u32[]{:S(2)}) %collective-permute-start.28) | collective-permute-done | bytes 4128 | tf_op jit(solution)/shard_map/ppermute | solution.py:464
  123.6 2.7 %collective-permute-done.29.second = f32[8,128]{1,0:T(8,128)S(1)} collective-permute-done((f32[8,128]{1,0:T(8,128)S(1)}, f32[8,128]{1,0:T(8,128)S(1)}, u32[]{:S(2)}, u32[]{:S(2)}) %collective-permute-start.29) | collective-permute-done | bytes 4128 | tf_op jit(solution)/shard_map/ppermute | solution.py:464
  127.8 3.3 %collective-permute-done.30.second = f32[8,128]{1,0:T(8,128)S(1)} collective-permute-done((f32[8,128]{1,0:T(8,128)S(1)}, f32[8,128]{1,0:T(8,128)S(1)}, u32[]{:S(2)}, u32[]{:S(2)}) %collective-permute-start.30) | collective-permute-done | bytes 4128 | tf_op jit(solution)/shard_map/ppermute | solution.py:464
  (73 shorter events, 31.7 us)
Async XLA Ops:
  0.0 6.6 %collective-permute-start = (bf16[1024,384]{1,0:T(8,128)(2,1)}, bf16[1024,384]{1,0:T(8,128)(2,1)S(1)}, u32[]{:S(2)}, u32[]{:S(2)}) collective-permute-start(bf16[1024,384]{1,0:T(8,128)(2,1)} %bitcast.22), channel_id=1, source_target_pairs={{0,1},{1,0},{2,3},{3,2},{4,5},{5,4},{6,7},{7,6},{8,9},{9,8},{10,11... | collective-permute-start | bytes 2359304 | tf_op jit(solution)/shard_map/ppermute | solution.py:53
  1.2 13.1 %collective-permute-start.1 = (bf16[512,384]{1,0:T(8,128)(2,1)S(1)}, bf16[512,384]{1,0:T(8,128)(2,1)S(1)}, u32[]{:S(2)}, u32[]{:S(2)}) collective-permute-start(bf16[512,384]{1,0:T(8,128)(2,1)S(1)} %bitcast.27), channel_id=1, source_target_pairs={{0,8},{1,9},{2,10},{3,11},{4,12},{5,13},{6,14},{7,15},{8,0},{9,1},... | collective-permute-start | bytes 1179656 | tf_op jit(solution)/shard_map/ppermute | solution.py:49
  4.6 9.8 %collective-permute-start.2 = (bf16[512,384]{1,0:T(8,128)(2,1)S(1)}, bf16[512,384]{1,0:T(8,128)(2,1)S(1)}, u32[]{:S(2)}, u32[]{:S(2)}) collective-permute-start(bf16[512,384]{1,0:T(8,128)(2,1)S(1)} %bitcast.25), channel_id=1, source_target_pairs={{0,2},{1,7},{2,4},{3,1},{4,6},{5,3},{6,0},{7,5},{8,10},{9,15},{10,... | collective-permute-start | bytes 1179656 | tf_op jit(solution)/shard_map/ppermute | solution.py:45
  14.3 9.5 %collective-permute-start.3 = (bf16[512,384]{1,0:T(8,128)(2,1)S(1)}, bf16[512,384]{1,0:T(8,128)(2,1)S(1)}, u32[]{:S(2)}, u32[]{:S(2)}) collective-permute-start(bf16[512,384]{1,0:T(8,128)(2,1)S(1)} %collective-permute-done.1.refs_1_.second), channel_id=1, source_target_pairs={{0,1},{1,0},{2,3},{3,2},{4,5},{5,4},{6,7},{7,6},{8,9},{9,8},{10,11... | collective-permute-start | bytes 1179656 | tf_op jit(solution)/shard_map/ppermute | solution.py:53
  14.6 9.2 %collective-permute-start.4 = (bf16[512,384]{1,0:T(8,128)(2,1)S(1)}, bf16[512,384]{1,0:T(8,128)(2,1)S(1)}, u32[]{:S(2)}, u32[]{:S(2)}) collective-permute-start(bf16[512,384]{1,0:T(8,128)(2,1)S(1)} %collective-permute-done.2.refs_5_.second), channel_id=1, source_target_pairs={{0,1},{1,0},{2,3},{3,2},{4,5},{5,4},{6,7},{7,6},{8,9},{9,8},{10,11... | collective-permute-start | bytes 1179656 | tf_op jit(solution)/shard_map/ppermute | solution.py:53
  16.7 21.8 %collective-permute-start.7 = (bf16[2,512,384]{2,1,0:T(8,128)(2,1)}, bf16[2,512,384]{2,1,0:T(8,128)(2,1)S(1)}, u32[]{:S(2)}, u32[]{:S(2)}) collective-permute-start(bf16[2,512,384]{2,1,0:T(8,128)(2,1)} %stack.79), channel_id=1, source_target_pairs={{0,8},{1,9},{2,10},{3,11},{4,12},{5,13},{6,14},{7,15},{8,0},{9,1},... | collective-permute-start | bytes 2359304 | tf_op jit(solution)/shard_map/ppermute | solution.py:49
  20.0 18.4 %collective-permute-start.5 = (bf16[2,512,384]{2,1,0:T(8,128)(2,1)}, bf16[2,512,384]{2,1,0:T(8,128)(2,1)S(1)}, u32[]{:S(2)}, u32[]{:S(2)}) collective-permute-start(bf16[2,512,384]{2,1,0:T(8,128)(2,1)} %stack.78), channel_id=1, source_target_pairs={{0,2},{1,7},{2,4},{3,1},{4,6},{5,3},{6,0},{7,5},{8,10},{9,15},{10,... | collective-permute-start | bytes 2359304 | tf_op jit(solution)/shard_map/ppermute | solution.py:45
  21.9 16.5 %collective-permute-start.6 = (bf16[512,384]{1,0:T(8,128)(2,1)S(1)}, bf16[512,384]{1,0:T(8,128)(2,1)S(1)}, u32[]{:S(2)}, u32[]{:S(2)}) collective-permute-start(bf16[512,384]{1,0:T(8,128)(2,1)S(1)} %collective-permute-done.2.refs_5_.second), channel_id=1, source_target_pairs={{0,2},{1,7},{2,4},{3,1},{4,6},{5,3},{6,0},{7,5},{8,10},{9,15},{10,... | collective-permute-start | bytes 1179656 | tf_op jit(solution)/shard_map/ppermute | solution.py:45
  38.5 7.1 %collective-permute-start.10 = (bf16[2,512,384]{2,1,0:T(8,128)(2,1)S(1)}, bf16[2,512,384]{2,1,0:T(8,128)(2,1)S(1)}, u32[]{:S(2)}, u32[]{:S(2)}) collective-permute-start(bf16[2,512,384]{2,1,0:T(8,128)(2,1)S(1)} %collective-permute-done.7.refs_5_), channel_id=1, source_target_pairs={{0,1},{1,0},{2,3},{3,2},{4,5},{5,4},{6,7},{7,6},{8,9},{9,8},{10,11... | collective-permute-start | bytes 2359304 | tf_op jit(solution)/shard_map/ppermute | solution.py:53
  38.5 7.1 %collective-permute-start.8 = (bf16[2,512,384]{2,1,0:T(8,128)(2,1)S(1)}, bf16[2,512,384]{2,1,0:T(8,128)(2,1)S(1)}, u32[]{:S(2)}, u32[]{:S(2)}) collective-permute-start(bf16[2,512,384]{2,1,0:T(8,128)(2,1)S(1)} %collective-permute-done.5.refs_1_), channel_id=1, source_target_pairs={{0,1},{1,0},{2,3},{3,2},{4,5},{5,4},{6,7},{7,6},{8,9},{9,8},{10,11... | collective-permute-start | bytes 2359304 | tf_op jit(solution)/shard_map/ppermute | solution.py:53
  39.0 17.7 %collective-permute-start.11 = (bf16[2,512,384]{2,1,0:T(8,128)(2,1)S(1)}, bf16[2,512,384]{2,1,0:T(8,128)(2,1)S(1)}, u32[]{:S(2)}, u32[]{:S(2)}) collective-permute-start(bf16[2,512,384]{2,1,0:T(8,128)(2,1)S(1)} %collective-permute-done.5.refs_1_), channel_id=1, source_target_pairs={{0,2},{1,7},{2,4},{3,1},{4,6},{5,3},{6,0},{7,5},{8,10},{9,15},{10,... | collective-permute-start | bytes 2359304 | tf_op jit(solution)/shard_map/ppermute | solution.py:45
  40.4 16.3 %collective-permute-start.12 = (bf16[512,384]{1,0:T(8,128)(2,1)S(1)}, bf16[512,384]{1,0:T(8,128)(2,1)S(1)}, u32[]{:S(2)}, u32[]{:S(2)}) collective-permute-start(bf16[512,384]{1,0:T(8,128)(2,1)S(1)} %collective-permute-done.6.refs_3_), channel_id=1, source_target_pairs={{0,2},{1,7},{2,4},{3,1},{4,6},{5,3},{6,0},{7,5},{8,10},{9,15},{10,... | collective-permute-start | bytes 1179656 | tf_op jit(solution)/shard_map/ppermute | solution.py:45
  42.4 14.3 %collective-permute-start.13 = (bf16[512,384]{1,0:T(8,128)(2,1)S(1)}, bf16[512,384]{1,0:T(8,128)(2,1)S(1)}, u32[]{:S(2)}, u32[]{:S(2)}) collective-permute-start(bf16[512,384]{1,0:T(8,128)(2,1)S(1)} %collective-permute-done.6.refs_3_), channel_id=1, source_target_pairs={{0,8},{1,9},{2,10},{3,11},{4,12},{5,13},{6,14},{7,15},{8,0},{9,1},... | collective-permute-start | bytes 1179656 | tf_op jit(solution)/shard_map/ppermute | solution.py:49
  57.3 13.5 %collective-permute-start.17 = (bf16[2,512,384]{2,1,0:T(8,128)(2,1)S(1)}, bf16[2,512,384]{2,1,0:T(8,128)(2,1)S(1)}, u32[]{:S(2)}, u32[]{:S(2)}) collective-permute-start(bf16[2,512,384]{2,1,0:T(8,128)(2,1)S(1)} %collective-permute-done.11.refs_1_), channel_id=1, source_target_pairs={{0,2},{1,7},{2,4},{3,1},{4,6},{5,3},{6,0},{7,5},{8,10},{9,15},{10,... | collective-permute-start | bytes 2359304 | tf_op jit(solution)/shard_map/ppermute | solution.py:45
  58.4 12.5 %collective-permute-start.18 = (bf16[512,384]{1,0:T(8,128)(2,1)S(1)}, bf16[512,384]{1,0:T(8,128)(2,1)S(1)}, u32[]{:S(2)}, u32[]{:S(2)}) collective-permute-start(bf16[512,384]{1,0:T(8,128)(2,1)S(1)} %collective-permute-done.12.refs_3_), channel_id=1, source_target_pairs={{0,8},{1,9},{2,10},{3,11},{4,12},{5,13},{6,14},{7,15},{8,0},{9,1},... | collective-permute-start | bytes 1179656 | tf_op jit(solution)/shard_map/ppermute | solution.py:49
  71.7 6.8 %collective-permute-start.20 = (bf16[512,384]{1,0:T(8,128)(2,1)S(1)}, bf16[512,384]{1,0:T(8,128)(2,1)S(1)}, u32[]{:S(2)}, u32[]{:S(2)}) collective-permute-start(bf16[512,384]{1,0:T(8,128)(2,1)S(1)} %collective-permute-done.18.refs_3_), channel_id=1, source_target_pairs={{0,1},{1,0},{2,3},{3,2},{4,5},{5,4},{6,7},{7,6},{8,9},{9,8},{10,11... | collective-permute-start | bytes 1179656 | tf_op jit(solution)/shard_map/ppermute | solution.py:53
  76.9 9.9 %collective-permute-start.21 = (bf16[2,4,128,128]{3,2,1,0:T(8,128)(2,1)S(1)}, bf16[2,4,128,128]{3,2,1,0:T(8,128)(2,1)S(1)}, u32[]{:S(2)}, u32[]{:S(2)}) collective-permute-start(bf16[2,4,128,128]{3,2,1,0:T(8,128)(2,1)S(1)} %get-tuple-element.213), channel_id=1, source_target_pairs={{0,16},{16,0},{32,48},{48,32},{64,80},{80,64},{96,112},{112,96},{1... | collective-permute-start | bytes 786440 | tf_op jit(solution)/shard_map/ppermute | solution.py:62
  80.8 9.8 %collective-permute-start.22 = (bf16[2,4,128,128]{3,2,1,0:T(8,128)(2,1)S(1)}, bf16[2,4,128,128]{3,2,1,0:T(8,128)(2,1)S(1)}, u32[]{:S(2)}, u32[]{:S(2)}) collective-permute-start(bf16[2,4,128,128]{3,2,1,0:T(8,128)(2,1)S(1)} %get-tuple-element.222), channel_id=1, source_target_pairs={{0,16},{16,32},{32,48},{48,64},{64,80},{80,96},{96,112},{1,17},{17... | collective-permute-start | bytes 786440 | tf_op jit(solution)/shard_map/ppermute | solution.py:58
  87.5 16.1 %collective-permute-start.23 = (bf16[2,4,128,128]{3,2,1,0:T(8,128)(2,1)S(1)}, bf16[2,4,128,128]{3,2,1,0:T(8,128)(2,1)S(1)}, u32[]{:S(2)}, u32[]{:S(2)}) collective-permute-start(bf16[2,4,128,128]{3,2,1,0:T(8,128)(2,1)S(1)} %extend.3.state), channel_id=1, source_target_pairs={{0,32},{16,48},{32,0},{48,16},{64,96},{80,112},{96,64},{112,80},{1... | collective-permute-start | bytes 786440 | tf_op jit(solution)/shard_map/ppermute | solution.py:62
  91.2 14.4 %collective-permute-start.24 = (bf16[2,4,128,128]{3,2,1,0:T(8,128)(2,1)S(1)}, bf16[2,4,128,128]{3,2,1,0:T(8,128)(2,1)S(1)}, u32[]{:S(2)}, u32[]{:S(2)}) collective-permute-start(bf16[2,4,128,128]{3,2,1,0:T(8,128)(2,1)S(1)} %extend.4), channel_id=1, source_target_pairs={{0,16},{16,32},{32,48},{48,64},{64,80},{80,96},{96,112},{1,17},{17... | collective-permute-start | bytes 786440 | tf_op jit(solution)/shard_map/ppermute | solution.py:58
  95.3 10.4 %collective-permute-start.25 = (bf16[2,4,128,128]{3,2,1,0:T(8,128)(2,1)S(1)}, bf16[2,4,128,128]{3,2,1,0:T(8,128)(2,1)S(1)}, u32[]{:S(2)}, u32[]{:S(2)}) collective-permute-start(bf16[2,4,128,128]{3,2,1,0:T(8,128)(2,1)S(1)} %extend.4), channel_id=1, source_target_pairs={{0,48},{16,64},{32,80},{48,96},{64,112},{1,49},{17,65},{33,81},{49... | collective-permute-start | bytes 786440 | tf_op jit(solution)/shard_map/ppermute | solution.py:58
  104.3 10.7 %collective-permute-start.26 = (bf16[2,4,128,128]{3,2,1,0:T(8,128)(2,1)S(1)}, bf16[2,4,128,128]{3,2,1,0:T(8,128)(2,1)S(1)}, u32[]{:S(2)}, u32[]{:S(2)}) collective-permute-start(bf16[2,4,128,128]{3,2,1,0:T(8,128)(2,1)S(1)} %extend.5), channel_id=1, source_target_pairs={{0,64},{16,80},{32,96},{48,112},{1,65},{17,81},{33,97},{49,113},{2... | collective-permute-start | bytes 786440 | tf_op jit(solution)/shard_map/ppermute | solution.py:58
  117.6 5.1 %collective-permute-start.28 = (f32[8,128]{1,0:T(8,128)S(1)}, f32[8,128]{1,0:T(8,128)S(1)}, u32[]{:S(2)}, u32[]{:S(2)}) collective-permute-start(f32[8,128]{1,0:T(8,128)S(1)} %add.309.first), channel_id=1, source_target_pairs={{0,8},{1,9},{2,10},{3,11},{4,12},{5,13},{6,14},{7,15},{8,0},{9,1},... | collective-permute-start | bytes 12296 | tf_op jit(solution)/shard_map/ppermute | solution.py:464
  126.3 4.8 %collective-permute-start.30 = (f32[8,128]{1,0:T(8,128)S(1)}, f32[8,128]{1,0:T(8,128)S(1)}, u32[]{:S(2)}, u32[]{:S(2)}) collective-permute-start(f32[8,128]{1,0:T(8,128)S(1)} %add.311.first), channel_id=1, source_target_pairs={{0,6},{1,7},{2,4},{3,5},{4,2},{5,3},{6,0},{7,1},{8,14},{9,15},{10,... | collective-permute-start | bytes 12296 | tf_op jit(solution)/shard_map/ppermute | solution.py:464
  (13 other events, 78.5 us)

commit v4 on v3

--- a/solution.py
+++ b/solution.py
@@ -60,6 +60,11 @@
 
 def swapped(x, bit):
     return lax.ppermute(x, "ctx", [(i, i ^ bit) for i in range(lax.axis_size("ctx"))])
+
+
+def round_x(x, distance):
+    n = lax.axis_size("ctx")
+    return lax.ppermute(x, "ctx", [(i, i // 4 * 4 + (i + distance) % 4) for i in range(n)])
 
 
 def doc_ends(lengths, seq):
@@ -305,11 +310,23 @@
             out[s, h] = got.astype(BF16)
 
 
-def extend_kernel(first_seq, meta, lengths, decay, state, before, out):
-    for s in range(state.shape[0]):
-        for h in range(state.shape[1]):
-            share = carried_share(meta, lengths, decay, first_seq + s, h, 0)
-            out[s, h] = (state[s, h] + share * before[s, h].astype(F32)).astype(BF16)
+def choose_kernel(meta, state, earlier, *outs):
+    for distance, out in enumerate(outs, 1):
+        wraps = meta[CTX] % 4 + distance >= 4
+        for s in range(state.shape[0]):
+            for h in range(state.shape[1]):
+                out[s, h] = jnp.where(wraps, earlier[s, h], state[s, h])
+
+
+def choose(scalars, state, earlier):
+    return pl.pallas_call(
+        choose_kernel,
+        out_shape=[jax.ShapeDtypeStruct(state.shape, BF16)] * 3,
+        in_specs=[SMEM] + [VMEM] * 2,
+        out_specs=[VMEM] * 3,
+        compiler_params=pltpu.CompilerParams(vmem_limit_bytes=LIMIT * 2**20),
+        name="choose",
+    )(scalars[0], state, earlier)
 
 
 def extend(kernel, scalars, state, before, first_seq):
@@ -325,7 +342,7 @@
 
 def shares(scan, meta, share):
     if not scan:
-        return [1.0, share(1) * share(2)]
+        return [1.0, share(1), share(1) * share(2), share(1) * share(2) * share(3)]
     place = meta[CTX] % 4
     odd, high = place % 2 == 1, place >= 2
     first = jnp.where(odd, 1.0, jnp.zeros((1, HEAD), F32))
@@ -528,7 +545,7 @@
     keys_z, values_z, state_z, sent_z = project(
         "kv", scalars, last_z, held, accs=acc[4:6], first_seq=half
     )
-    before_z = ahead(sent_z, 1)
+    above_z = ahead(sent_z, 4)
     acc, state_z = in_order(acc, state_z)
     query_y, inner_y, gate_y = project(
         "qg", scalars, last_y, held, accs=acc[2:4], extra=(keys_y, values_y, gain)
@@ -536,17 +553,17 @@
     query_y, one_y, acc = in_order(query_y, one_y, acc)
     pair_y = extend(pair_kernel, scalars, state_y, one_y, 0)
     two_y = swapped(pair_y, 2)
-    before_z, pair_y = in_order(before_z, pair_y)
-    longer_z = extend(extend_kernel, scalars, state_z, before_z, half)
-    near_z, far_z = ahead(longer_z, 1), ahead(longer_z, 3)
-    acc, longer_z = in_order(acc, longer_z)
+    above_z, pair_y = in_order(above_z, pair_y)
+    chosen = choose(scalars, sent_z, above_z)
+    around_z = [round_x(x, distance) for distance, x in enumerate(chosen, 1)]
+    acc, chosen = in_order(acc, chosen)
     query_z, inner_z, gate_z = project(
         "qg", scalars, last_z, held, accs=acc[6:], extra=(keys_z, values_z, gain), first_seq=half
     )
     query_z, two_y = in_order(query_z, two_y)
     four_y = ahead(extend(quad_kernel, scalars, pair_y, two_y, 0), 4)
-    query_z, near_z, far_z = in_order(query_z, near_z, far_z)
-    attn_z, squares_z = combine(False, scalars, query_z, inner_z, (near_z, far_z), half)
+    query_z, around_z = in_order(query_z, around_z)
+    attn_z, squares_z = combine(False, scalars, query_z, inner_z, (*around_z, above_z), half)
     squares_z, four_y = in_order(squares_z, four_y)
     attn_y, squares_y = combine(True, scalars, query_y, inner_y, (one_y, two_y, four_y), 0)
     squares = all_sum(join(squares_y, squares_z))

time: 133 us -> 128 us (0.962)
  waiting for transfers between devices: 31.3 us -> 28.2 us
  starting transfers between devices: 48.1 us -> 45.9 us
    ppermute x4 -> x2, waiting for transfers between devices: 8.1 us -> 0.01 us  [ahead(): lax.ppermute(x, 'ctx', [(i, i + distance) for i in range(n - distance)])]
    ppermute x4 -> x2, starting transfers between devices: 13.5 us -> 6.58 us  [ahead(): lax.ppermute(x, 'ctx', [(i, i + distance) for i in range(n - distance)])]
    ppermute x0 -> x3, waiting for transfers between devices: none -> 5.37 us  [round_x(): lax.ppermute(x, 'ctx', [(i, i // 4 * 4 + (i + distance) % 4) for i in ran...]
    ppermute x0 -> x3, starting transfers between devices: none -> 4.16 us  [round_x(): lax.ppermute(x, 'ctx', [(i, i // 4 * 4 + (i + distance) % 4) for i in ran...]
  transfers between devices with their start and end apart: 31 -> 32, of which waited for: 11 -> 13; matrix products, arithmetic and copies ran while one was open for 1% -> 1% of each run, Pallas kernels for 36% -> 38%
where the time goes in v4:
time: 128 us
  Pallas kernels  51.5 us (40%)
  starting transfers between devices  45.9 us (36%)
  waiting for transfers between devices  28.2 us (22%)
  local copies, waits for them, and re-layouts  2.21 us (2%)
    pallas_call x8, Pallas kernels, project(): pl.pallas_call(functools.partial(project_kernel, mode, first_seq, plan),...  43.5 us
    ppermute x4, starting transfers between devices, across(): return lax.ppermute(x, 'tp', ACROSS)  12.2 us
    ppermute x6, starting transfers between devices, ring(): return lax.ppermute(x, 'tp', RING)  10.1 us
    ppermute x4, waiting for transfers between devices, all_sum(): x = add(x, lax.ppermute(x, 'tp', route))  8.83 us
    ppermute x6, waiting for transfers between devices, ring(): return lax.ppermute(x, 'tp', RING)  8.06 us
    ppermute x2, starting transfers between devices, ahead(): lax.ppermute(x, 'ctx', [(i, i + distance) for i in range(n - distance)])  6.58 us
    ppermute x4, starting transfers between devices, all_sum(): x = add(x, lax.ppermute(x, 'tp', route))  5.95 us
    ppermute x3, waiting for transfers between devices, round_x(): lax.ppermute(x, 'ctx', [(i, i // 4 * 4 + (i + distance) % 4) for i in ran...  5.37 us
  transfers between devices with their start and end apart: 32, of which 13 were waited for; matrix products, arithmetic and copies ran while one was open for 1% of the time, Pallas kernels for 38%

profile of v4, /device:TPU:0, one launch (start us, length us, event | category | flops | bytes accessed | tf_op | source)
XLA Modules:
  0.0 128.1 jit_solution(9543766379745134503)
XLA Ops:
  1.2 3.4 %collective-permute-start.1 = (bf16[512,384]{1,0:T(8,128)(2,1)S(1)}, bf16[512,384]{1,0:T(8,128)(2,1)S(1)}, u32[]{:S(2)}, u32[]{:S(2)}) collective-permute-start(bf16[512,384]{1,0:T(8,128)(2,1)S(1)} %bitcast.27), channel_id=1, source_target_pairs={{0,8},{1,9},{2,10},{3,11},{4,12},{5,13},{6,14},{7,15},{8,0},{9,1},... | collective-permute-start | bytes 1179656 | tf_op jit(solution)/shard_map/ppermute | solution.py:49
  7.5 5.0 %project_first.1 = (f32[512,512]{1,0:T(8,128)S(1)}, f32[512,512]{1,0:T(8,128)S(1)}, f32[512,512]{1,0:T(8,128)S(1)}, f32[512,512]{1,0:T(8,128)S(1)}, bf16[4,768,5...) custom-call(s32[18]{0:T(128)S(1)} %stack.77.refs_0_.meta, bf16[1024,384]{1,0:T(8,128)(2,1)} %bitcast.23, ...), custom_call_target="tpu_custom_call" | custom-call | flops 1610612736 | bytes 786432 | tf_op jit(solution)/shard_map/project_first/pallas_call | solution.py:254
  16.7 3.3 %collective-permute-start.7 = (bf16[2,512,384]{2,1,0:T(8,128)(2,1)}, bf16[2,512,384]{2,1,0:T(8,128)(2,1)S(1)}, u32[]{:S(2)}, u32[]{:S(2)}) collective-permute-start(bf16[2,512,384]{2,1,0:T(8,128)(2,1)} %stack.79), channel_id=1, source_target_pairs={{0,8},{1,9},{2,10},{3,11},{4,12},{5,13},{6,14},{7,15},{8,0},{9,1},... | collective-permute-start | bytes 2359304 | tf_op jit(solution)/shard_map/ppermute | solution.py:49
  21.9 1.9 %collective-permute-start.6 = (bf16[512,384]{1,0:T(8,128)(2,1)S(1)}, bf16[512,384]{1,0:T(8,128)(2,1)S(1)}, u32[]{:S(2)}, u32[]{:S(2)}) collective-permute-start(bf16[512,384]{1,0:T(8,128)(2,1)S(1)} %collective-permute-done.2.refs_5_.second), channel_id=1, source_target_pairs={{0,2},{1,7},{2,4},{3,1},{4,6},{5,3},{6,0},{7,5},{8,10},{9,15},{10,... | collective-permute-start | bytes 1179656 | tf_op jit(solution)/shard_map/ppermute | solution.py:45
  23.9 7.4 %project_more.3 = (f32[512,512]{1,0:T(8,128)S(1)}, f32[512,512]{1,0:T(8,128)S(1)}, f32[512,512]{1,0:T(8,128)S(1)}, f32[512,512]{1,0:T(8,128)S(1)}, f32[512,512]{...) custom-call(s32[18]{0:T(128)S(1)} %stack.77.refs_0_.meta, ...), custom_call_target="tpu_custom_call", output_to_operand_aliasing={{0}: (13, {}), {1}: (14, {}), {2}: (15, {}), {3}: (16, {})} | custom-call | flops 4831838208 | bytes 786432 | tf_op jit(solution)/shard_map/project_more/pallas_call | solution.py:254
  31.2 7.2 %collective-permute-done.6.refs_3_ = bf16[512,384]{1,0:T(8,128)(2,1)S(1)} collective-permute-done((bf16[512,384]{1,0:T(8,128)(2,1)S(1)}, bf16[512,384]{1,0:T(8,128)(2,1)S(1)}, u32[]{:S(2)}, u32[]{:S(2)}) %collective-permute-start.6) | collective-permute-done | bytes 393248 | tf_op jit(solution)/shard_map/ppermute | solution.py:45
  40.4 1.9 %collective-permute-start.12 = (bf16[512,384]{1,0:T(8,128)(2,1)S(1)}, bf16[512,384]{1,0:T(8,128)(2,1)S(1)}, u32[]{:S(2)}, u32[]{:S(2)}) collective-permute-start(bf16[512,384]{1,0:T(8,128)(2,1)S(1)} %collective-permute-done.6.refs_3_), channel_id=1, source_target_pairs={{0,2},{1,7},{2,4},{3,1},{4,6},{5,3},{6,0},{7,5},{8,10},{9,15},{10,... | collective-permute-start | bytes 1179656 | tf_op jit(solution)/shard_map/ppermute | solution.py:45
  42.4 3.1 %collective-permute-start.13 = (bf16[512,384]{1,0:T(8,128)(2,1)S(1)}, bf16[512,384]{1,0:T(8,128)(2,1)S(1)}, u32[]{:S(2)}, u32[]{:S(2)}) collective-permute-start(bf16[512,384]{1,0:T(8,128)(2,1)S(1)} %collective-permute-done.6.refs_3_), channel_id=1, source_target_pairs={{0,8},{1,9},{2,10},{3,11},{4,12},{5,13},{6,14},{7,15},{8,0},{9,1},... | collective-permute-start | bytes 1179656 | tf_op jit(solution)/shard_map/ppermute | solution.py:49
  45.5 10.3 %project_more.4 = (f32[512,512]{1,0:T(8,128)S(1)}, f32[512,512]{1,0:T(8,128)S(1)}, f32[512,512]{1,0:T(8,128)S(1)}, f32[512,512]{1,0:T(8,128)S(1)}, f32[512,512]{...) custom-call(s32[18]{0:T(128)S(1)} %stack.77.refs_0_.meta, ...), custom_call_target="tpu_custom_call", output_to_operand_aliasing={{0}: (15, {}), {1}: (16, {}), {2}: (17, {}), {3}: (18, {}),... | custom-call | flops 8053063680 | bytes 786432 | tf_op jit(solution)/shard_map/project_more/pallas_call | solution.py:254
  58.4 2.4 %collective-permute-start.18 = (bf16[512,384]{1,0:T(8,128)(2,1)S(1)}, bf16[512,384]{1,0:T(8,128)(2,1)S(1)}, u32[]{:S(2)}, u32[]{:S(2)}) collective-permute-start(bf16[512,384]{1,0:T(8,128)(2,1)S(1)} %collective-permute-done.12.refs_3_), channel_id=1, source_target_pairs={{0,8},{1,9},{2,10},{3,11},{4,12},{5,13},{6,14},{7,15},{8,0},{9,1},... | collective-permute-start | bytes 1179656 | tf_op jit(solution)/shard_map/ppermute | solution.py:49
  60.8 8.5 %project_more.5 = (f32[512,512]{1,0:T(8,128)S(1)}, f32[512,512]{1,0:T(8,128)S(1)}, f32[512,512]{1,0:T(8,128)S(1)}, f32[512,512]{1,0:T(8,128)S(1)}, f32[512,512]{...) custom-call(s32[18]{0:T(128)S(1)} %stack.77.refs_0_.meta, ...), custom_call_target="tpu_custom_call", output_to_operand_aliasing={{0}: (14, {}), {1}: (15, {}), {2}: (16, {}), {3}: (17, {}),... | custom-call | flops 6442450944 | bytes 786432 | tf_op jit(solution)/shard_map/project_more/pallas_call | solution.py:254
  73.6 3.2 %project_kv.2 = (bf16[512,512]{1,0:T(8,128)(2,1)S(1)}, bf16[512,512]{1,0:T(8,128)(2,1)S(1)}, f32[2,4,128,128]{3,2,1,0:T(8,128)S(1)}, bf16[2,4,128,128]{3,2,1,0:T(8,128)(2,1)S(1)}) custom-call(s32[18]{0:T(128)S(1)} %stack.77.refs_0_.meta, s32[4,4]{1,0:T(4,128)S(1)} %copy-done.3, f32[4]{0:T(128)S(1)} %copy-done.4, ...), custom_call_target="tpu_custom_call" | custom-call | flops 1610612736 | bytes 786432 | tf_op jit(solution)/shard_map/project_kv/pallas_call | solution.py:254
  78.5 3.1 %project_kv.3 = (bf16[512,512]{1,0:T(8,128)(2,1)S(1)}, bf16[512,512]{1,0:T(8,128)(2,1)S(1)}, f32[2,4,128,128]{3,2,1,0:T(8,128)}, bf16[2,4,128,128]{3,2,1,0:T(8,128)(2,1)S(1)}) custom-call(s32[18]{0:T(128)S(1)} %stack.77.refs_0_.meta, s32[4,4]{1,0:T(4,128)S(1)} %copy-done.3, f32[4]{0:T(128)S(1)} %copy-done.4, ...), custom_call_target="tpu_custom_call" | custom-call | flops 805306368 | bytes 786432 | tf_op jit(solution)/shard_map/project_kv/pallas_call | solution.py:254
  81.6 2.7 %collective-permute-start.22 = (bf16[2,4,128,128]{3,2,1,0:T(8,128)(2,1)S(1)}, bf16[2,4,128,128]{3,2,1,0:T(8,128)(2,1)S(1)}, u32[]{:S(2)}, u32[]{:S(2)}) collective-permute-start(bf16[2,4,128,128]{3,2,1,0:T(8,128)(2,1)S(1)} %get-tuple-element.222.state), channel_id=1, source_target_pairs={{0,64},{16,80},{32,96},{48,112},{1,65},{17,81},{33,97},{49,113},{2... | collective-permute-start | bytes 786440 | tf_op jit(solution)/shard_map/ppermute | solution.py:58
  84.3 3.5 %project_qg.2 = (bf16[512,512]{1,0:T(8,128)(2,1)S(1)}, f32[512,512]{1,0:T(8,128)S(1)}, f32[512,512]{1,0:T(8,128)S(1)}) custom-call(s32[18]{0:T(128)S(1)} %stack.77.refs_0_.meta, s32[4,4]{1,0:T(4,128)S(1)} %copy-done.3, f32[4]{0:T(128)S(1)} %copy-done.4, bf16[2,512,384]{2,1,0:T(8,128)(2,1)S(1)} %collective-permute-done.17.refs_3_, ...), custom_call_target="tpu_custom_call" | custom-call | flops 1610612736 | bytes 786432 | tf_op jit(solution)/shard_map/project_qg/pallas_call | solution.py:254
  88.5 2.8 %collective-permute-start.23 = (bf16[2,4,128,128]{3,2,1,0:T(8,128)(2,1)S(1)}, bf16[2,4,128,128]{3,2,1,0:T(8,128)(2,1)S(1)}, u32[]{:S(2)}, u32[]{:S(2)}) collective-permute-start(bf16[2,4,128,128]{3,2,1,0:T(8,128)(2,1)S(1)} %extend.2.state), channel_id=1, source_target_pairs={{0,32},{16,48},{32,0},{48,16},{64,96},{80,112},{96,64},{112,80},{1... | collective-permute-start | bytes 786440 | tf_op jit(solution)/shard_map/ppermute | solution.py:62
  92.3 2.1 %collective-permute-start.25 = (bf16[2,4,128,128]{3,2,1,0:T(8,128)(2,1)S(1)}, bf16[2,4,128,128]{3,2,1,0:T(8,128)(2,1)S(1)}, u32[]{:S(2)}, u32[]{:S(2)}) collective-permute-start(bf16[2,4,128,128]{3,2,1,0:T(8,128)(2,1)S(1)} %get-tuple-element.226), channel_id=1, source_target_pairs={{0,32},{16,48},{32,0},{48,16},{64,96},{80,112},{96,64},{112,80},{1... | collective-permute-start | bytes 786440 | tf_op jit(solution)/shard_map/ppermute | solution.py:67
  96.2 2.5 %project_qg.3 = (bf16[512,512]{1,0:T(8,128)(2,1)S(1)}, f32[512,512]{1,0:T(8,128)S(1)}, f32[512,512]{1,0:T(8,128)S(1)}) custom-call(s32[18]{0:T(128)S(1)} %stack.77.refs_0_.meta, s32[4,4]{1,0:T(4,128)S(1)} %copy-done.3, f32[4]{0:T(128)S(1)} %copy-done.4, bf16[512,384]{1,0:T(8,128)(2,1)S(1)} %collective-permute-done.18.refs_3_, ...), custom_call_target="tpu_custom_call" | custom-call | flops 805306368 | bytes 786432 | tf_op jit(solution)/shard_map/project_qg/pallas_call | solution.py:254
  100.0 3.9 %collective-permute-start.27 = (bf16[2,4,128,128]{3,2,1,0:T(8,128)(2,1)S(1)}, bf16[2,4,128,128]{3,2,1,0:T(8,128)(2,1)S(1)}, u32[]{:S(2)}, u32[]{:S(2)}) collective-permute-start(bf16[2,4,128,128]{3,2,1,0:T(8,128)(2,1)S(1)} %extend.3), channel_id=1, source_target_pairs={{0,64},{16,80},{32,96},{48,112},{1,65},{17,81},{33,97},{49,113},{2... | collective-permute-start | bytes 786440 | tf_op jit(solution)/shard_map/ppermute | solution.py:58
  104.9 4.4 %collective-permute-done.25.refs_1_ = bf16[2,4,128,128]{3,2,1,0:T(8,128)(2,1)S(1)} collective-permute-done((bf16[2,4,128,128]{3,2,1,0:T(8,128)(2,1)S(1)}, bf16[2,4,128,128]{3,2,1,0:T(8,128)(2,1)S(1)}, u32[]{:S(2)}, u32[]{:S(2)}) %collective-permute-start.25) | collective-permute-done | bytes 262176 | tf_op jit(solution)/shard_map/ppermute | solution.py:67
  113.2 2.9 %collective-permute-start.29 = (f32[8,128]{1,0:T(8,128)S(1)}, f32[8,128]{1,0:T(8,128)S(1)}, u32[]{:S(2)}, u32[]{:S(2)}) collective-permute-start(f32[8,128]{1,0:T(8,128)S(1)} %add.309.first), channel_id=1, source_target_pairs={{0,8},{1,9},{2,10},{3,11},{4,12},{5,13},{6,14},{7,15},{8,0},{9,1},... | collective-permute-start | bytes 12296 | tf_op jit(solution)/shard_map/ppermute | solution.py:481
  116.1 2.2 %collective-permute-done.29.second = f32[8,128]{1,0:T(8,128)S(1)} collective-permute-done((f32[8,128]{1,0:T(8,128)S(1)}, f32[8,128]{1,0:T(8,128)S(1)}, u32[]{:S(2)}, u32[]{:S(2)}) %collective-permute-start.29) | collective-permute-done | bytes 4128 | tf_op jit(solution)/shard_map/ppermute | solution.py:481
  119.6 2.3 %collective-permute-done.30.second = f32[8,128]{1,0:T(8,128)S(1)} collective-permute-done((f32[8,128]{1,0:T(8,128)S(1)}, f32[8,128]{1,0:T(8,128)S(1)}, u32[]{:S(2)}, u32[]{:S(2)}) %collective-permute-start.30) | collective-permute-done | bytes 4128 | tf_op jit(solution)/shard_map/ppermute | solution.py:481
  123.7 3.1 %collective-permute-done.31.second = f32[8,128]{1,0:T(8,128)S(1)} collective-permute-done((f32[8,128]{1,0:T(8,128)S(1)}, f32[8,128]{1,0:T(8,128)S(1)}, u32[]{:S(2)}, u32[]{:S(2)}) %collective-permute-start.31) | collective-permute-done | bytes 4128 | tf_op jit(solution)/shard_map/ppermute | solution.py:481
  (75 shorter events, 34.6 us)
Async XLA Ops:
  0.0 6.6 %collective-permute-start = (bf16[1024,384]{1,0:T(8,128)(2,1)}, bf16[1024,384]{1,0:T(8,128)(2,1)S(1)}, u32[]{:S(2)}, u32[]{:S(2)}) collective-permute-start(bf16[1024,384]{1,0:T(8,128)(2,1)} %bitcast.22), channel_id=1, source_target_pairs={{0,1},{1,0},{2,3},{3,2},{4,5},{5,4},{6,7},{7,6},{8,9},{9,8},{10,11... | collective-permute-start | bytes 2359304 | tf_op jit(solution)/shard_map/ppermute | solution.py:53
  1.2 13.1 %collective-permute-start.1 = (bf16[512,384]{1,0:T(8,128)(2,1)S(1)}, bf16[512,384]{1,0:T(8,128)(2,1)S(1)}, u32[]{:S(2)}, u32[]{:S(2)}) collective-permute-start(bf16[512,384]{1,0:T(8,128)(2,1)S(1)} %bitcast.27), channel_id=1, source_target_pairs={{0,8},{1,9},{2,10},{3,11},{4,12},{5,13},{6,14},{7,15},{8,0},{9,1},... | collective-permute-start | bytes 1179656 | tf_op jit(solution)/shard_map/ppermute | solution.py:49
  4.6 9.8 %collective-permute-start.2 = (bf16[512,384]{1,0:T(8,128)(2,1)S(1)}, bf16[512,384]{1,0:T(8,128)(2,1)S(1)}, u32[]{:S(2)}, u32[]{:S(2)}) collective-permute-start(bf16[512,384]{1,0:T(8,128)(2,1)S(1)} %bitcast.25), channel_id=1, source_target_pairs={{0,2},{1,7},{2,4},{3,1},{4,6},{5,3},{6,0},{7,5},{8,10},{9,15},{10,... | collective-permute-start | bytes 1179656 | tf_op jit(solution)/shard_map/ppermute | solution.py:45
  14.3 9.5 %collective-permute-start.3 = (bf16[512,384]{1,0:T(8,128)(2,1)S(1)}, bf16[512,384]{1,0:T(8,128)(2,1)S(1)}, u32[]{:S(2)}, u32[]{:S(2)}) collective-permute-start(bf16[512,384]{1,0:T(8,128)(2,1)S(1)} %collective-permute-done.1.refs_1_.second), channel_id=1, source_target_pairs={{0,1},{1,0},{2,3},{3,2},{4,5},{5,4},{6,7},{7,6},{8,9},{9,8},{10,11... | collective-permute-start | bytes 1179656 | tf_op jit(solution)/shard_map/ppermute | solution.py:53
  14.6 9.2 %collective-permute-start.4 = (bf16[512,384]{1,0:T(8,128)(2,1)S(1)}, bf16[512,384]{1,0:T(8,128)(2,1)S(1)}, u32[]{:S(2)}, u32[]{:S(2)}) collective-permute-start(bf16[512,384]{1,0:T(8,128)(2,1)S(1)} %collective-permute-done.2.refs_5_.second), channel_id=1, source_target_pairs={{0,1},{1,0},{2,3},{3,2},{4,5},{5,4},{6,7},{7,6},{8,9},{9,8},{10,11... | collective-permute-start | bytes 1179656 | tf_op jit(solution)/shard_map/ppermute | solution.py:53
  16.7 21.8 %collective-permute-start.7 = (bf16[2,512,384]{2,1,0:T(8,128)(2,1)}, bf16[2,512,384]{2,1,0:T(8,128)(2,1)S(1)}, u32[]{:S(2)}, u32[]{:S(2)}) collective-permute-start(bf16[2,512,384]{2,1,0:T(8,128)(2,1)} %stack.79), channel_id=1, source_target_pairs={{0,8},{1,9},{2,10},{3,11},{4,12},{5,13},{6,14},{7,15},{8,0},{9,1},... | collective-permute-start | bytes 2359304 | tf_op jit(solution)/shard_map/ppermute | solution.py:49
  20.0 18.4 %collective-permute-start.5 = (bf16[2,512,384]{2,1,0:T(8,128)(2,1)}, bf16[2,512,384]{2,1,0:T(8,128)(2,1)S(1)}, u32[]{:S(2)}, u32[]{:S(2)}) collective-permute-start(bf16[2,512,384]{2,1,0:T(8,128)(2,1)} %stack.78), channel_id=1, source_target_pairs={{0,2},{1,7},{2,4},{3,1},{4,6},{5,3},{6,0},{7,5},{8,10},{9,15},{10,... | collective-permute-start | bytes 2359304 | tf_op jit(solution)/shard_map/ppermute | solution.py:45
  21.9 16.5 %collective-permute-start.6 = (bf16[512,384]{1,0:T(8,128)(2,1)S(1)}, bf16[512,384]{1,0:T(8,128)(2,1)S(1)}, u32[]{:S(2)}, u32[]{:S(2)}) collective-permute-start(bf16[512,384]{1,0:T(8,128)(2,1)S(1)} %collective-permute-done.2.refs_5_.second), channel_id=1, source_target_pairs={{0,2},{1,7},{2,4},{3,1},{4,6},{5,3},{6,0},{7,5},{8,10},{9,15},{10,... | collective-permute-start | bytes 1179656 | tf_op jit(solution)/shard_map/ppermute | solution.py:45
  38.4 7.1 %collective-permute-start.10 = (bf16[2,512,384]{2,1,0:T(8,128)(2,1)S(1)}, bf16[2,512,384]{2,1,0:T(8,128)(2,1)S(1)}, u32[]{:S(2)}, u32[]{:S(2)}) collective-permute-start(bf16[2,512,384]{2,1,0:T(8,128)(2,1)S(1)} %collective-permute-done.7.refs_5_), channel_id=1, source_target_pairs={{0,1},{1,0},{2,3},{3,2},{4,5},{5,4},{6,7},{7,6},{8,9},{9,8},{10,11... | collective-permute-start | bytes 2359304 | tf_op jit(solution)/shard_map/ppermute | solution.py:53
  38.4 7.1 %collective-permute-start.8 = (bf16[2,512,384]{2,1,0:T(8,128)(2,1)S(1)}, bf16[2,512,384]{2,1,0:T(8,128)(2,1)S(1)}, u32[]{:S(2)}, u32[]{:S(2)}) collective-permute-start(bf16[2,512,384]{2,1,0:T(8,128)(2,1)S(1)} %collective-permute-done.5.refs_1_), channel_id=1, source_target_pairs={{0,1},{1,0},{2,3},{3,2},{4,5},{5,4},{6,7},{7,6},{8,9},{9,8},{10,11... | collective-permute-start | bytes 2359304 | tf_op jit(solution)/shard_map/ppermute | solution.py:53
  39.0 17.7 %collective-permute-start.11 = (bf16[2,512,384]{2,1,0:T(8,128)(2,1)S(1)}, bf16[2,512,384]{2,1,0:T(8,128)(2,1)S(1)}, u32[]{:S(2)}, u32[]{:S(2)}) collective-permute-start(bf16[2,512,384]{2,1,0:T(8,128)(2,1)S(1)} %collective-permute-done.5.refs_1_), channel_id=1, source_target_pairs={{0,2},{1,7},{2,4},{3,1},{4,6},{5,3},{6,0},{7,5},{8,10},{9,15},{10,... | collective-permute-start | bytes 2359304 | tf_op jit(solution)/shard_map/ppermute | solution.py:45
  40.4 16.3 %collective-permute-start.12 = (bf16[512,384]{1,0:T(8,128)(2,1)S(1)}, bf16[512,384]{1,0:T(8,128)(2,1)S(1)}, u32[]{:S(2)}, u32[]{:S(2)}) collective-permute-start(bf16[512,384]{1,0:T(8,128)(2,1)S(1)} %collective-permute-done.6.refs_3_), channel_id=1, source_target_pairs={{0,2},{1,7},{2,4},{3,1},{4,6},{5,3},{6,0},{7,5},{8,10},{9,15},{10,... | collective-permute-start | bytes 1179656 | tf_op jit(solution)/shard_map/ppermute | solution.py:45
  42.4 14.3 %collective-permute-start.13 = (bf16[512,384]{1,0:T(8,128)(2,1)S(1)}, bf16[512,384]{1,0:T(8,128)(2,1)S(1)}, u32[]{:S(2)}, u32[]{:S(2)}) collective-permute-start(bf16[512,384]{1,0:T(8,128)(2,1)S(1)} %collective-permute-done.6.refs_3_), channel_id=1, source_target_pairs={{0,8},{1,9},{2,10},{3,11},{4,12},{5,13},{6,14},{7,15},{8,0},{9,1},... | collective-permute-start | bytes 1179656 | tf_op jit(solution)/shard_map/ppermute | solution.py:49
  57.3 13.5 %collective-permute-start.17 = (bf16[2,512,384]{2,1,0:T(8,128)(2,1)S(1)}, bf16[2,512,384]{2,1,0:T(8,128)(2,1)S(1)}, u32[]{:S(2)}, u32[]{:S(2)}) collective-permute-start(bf16[2,512,384]{2,1,0:T(8,128)(2,1)S(1)} %collective-permute-done.11.refs_1_), channel_id=1, source_target_pairs={{0,2},{1,7},{2,4},{3,1},{4,6},{5,3},{6,0},{7,5},{8,10},{9,15},{10,... | collective-permute-start | bytes 2359304 | tf_op jit(solution)/shard_map/ppermute | solution.py:45
  58.4 12.5 %collective-permute-start.18 = (bf16[512,384]{1,0:T(8,128)(2,1)S(1)}, bf16[512,384]{1,0:T(8,128)(2,1)S(1)}, u32[]{:S(2)}, u32[]{:S(2)}) collective-permute-start(bf16[512,384]{1,0:T(8,128)(2,1)S(1)} %collective-permute-done.12.refs_3_), channel_id=1, source_target_pairs={{0,8},{1,9},{2,10},{3,11},{4,12},{5,13},{6,14},{7,15},{8,0},{9,1},... | collective-permute-start | bytes 1179656 | tf_op jit(solution)/shard_map/ppermute | solution.py:49
  71.7 6.8 %collective-permute-start.21 = (bf16[512,384]{1,0:T(8,128)(2,1)S(1)}, bf16[512,384]{1,0:T(8,128)(2,1)S(1)}, u32[]{:S(2)}, u32[]{:S(2)}) collective-permute-start(bf16[512,384]{1,0:T(8,128)(2,1)S(1)} %collective-permute-done.18.refs_3_), channel_id=1, source_target_pairs={{0,1},{1,0},{2,3},{3,2},{4,5},{5,4},{6,7},{7,6},{8,9},{9,8},{10,11... | collective-permute-start | bytes 1179656 | tf_op jit(solution)/shard_map/ppermute | solution.py:53
  76.9 10.9 %collective-permute-start.20 = (bf16[2,4,128,128]{3,2,1,0:T(8,128)(2,1)S(1)}, bf16[2,4,128,128]{3,2,1,0:T(8,128)(2,1)S(1)}, u32[]{:S(2)}, u32[]{:S(2)}) collective-permute-start(bf16[2,4,128,128]{3,2,1,0:T(8,128)(2,1)S(1)} %get-tuple-element.213), channel_id=1, source_target_pairs={{0,16},{16,0},{32,48},{48,32},{64,80},{80,64},{96,112},{112,96},{1... | collective-permute-start | bytes 786440 | tf_op jit(solution)/shard_map/ppermute | solution.py:62
  81.6 9.7 %collective-permute-start.22 = (bf16[2,4,128,128]{3,2,1,0:T(8,128)(2,1)S(1)}, bf16[2,4,128,128]{3,2,1,0:T(8,128)(2,1)S(1)}, u32[]{:S(2)}, u32[]{:S(2)}) collective-permute-start(bf16[2,4,128,128]{3,2,1,0:T(8,128)(2,1)S(1)} %get-tuple-element.222.state), channel_id=1, source_target_pairs={{0,64},{16,80},{32,96},{48,112},{1,65},{17,81},{33,97},{49,113},{2... | collective-permute-start | bytes 786440 | tf_op jit(solution)/shard_map/ppermute | solution.py:58
  88.5 10.8 %collective-permute-start.23 = (bf16[2,4,128,128]{3,2,1,0:T(8,128)(2,1)S(1)}, bf16[2,4,128,128]{3,2,1,0:T(8,128)(2,1)S(1)}, u32[]{:S(2)}, u32[]{:S(2)}) collective-permute-start(bf16[2,4,128,128]{3,2,1,0:T(8,128)(2,1)S(1)} %extend.2.state), channel_id=1, source_target_pairs={{0,32},{16,48},{32,0},{48,16},{64,96},{80,112},{96,64},{112,80},{1... | collective-permute-start | bytes 786440 | tf_op jit(solution)/shard_map/ppermute | solution.py:62
  92.0 12.9 %collective-permute-start.24 = (bf16[2,4,128,128]{3,2,1,0:T(8,128)(2,1)S(1)}, bf16[2,4,128,128]{3,2,1,0:T(8,128)(2,1)S(1)}, u32[]{:S(2)}, u32[]{:S(2)}) collective-permute-start(bf16[2,4,128,128]{3,2,1,0:T(8,128)(2,1)S(1)} %get-tuple-element.225), channel_id=1, source_target_pairs={{0,16},{16,32},{32,48},{48,0},{64,80},{80,96},{96,112},{112,64},{1... | collective-permute-start | bytes 786440 | tf_op jit(solution)/shard_map/ppermute | solution.py:67
  92.3 17.0 %collective-permute-start.25 = (bf16[2,4,128,128]{3,2,1,0:T(8,128)(2,1)S(1)}, bf16[2,4,128,128]{3,2,1,0:T(8,128)(2,1)S(1)}, u32[]{:S(2)}, u32[]{:S(2)}) collective-permute-start(bf16[2,4,128,128]{3,2,1,0:T(8,128)(2,1)S(1)} %get-tuple-element.226), channel_id=1, source_target_pairs={{0,32},{16,48},{32,0},{48,16},{64,96},{80,112},{96,64},{112,80},{1... | collective-permute-start | bytes 786440 | tf_op jit(solution)/shard_map/ppermute | solution.py:67
  94.4 14.9 %collective-permute-start.26 = (bf16[2,4,128,128]{3,2,1,0:T(8,128)(2,1)S(1)}, bf16[2,4,128,128]{3,2,1,0:T(8,128)(2,1)S(1)}, u32[]{:S(2)}, u32[]{:S(2)}) collective-permute-start(bf16[2,4,128,128]{3,2,1,0:T(8,128)(2,1)S(1)} %get-tuple-element.227), channel_id=1, source_target_pairs={{0,48},{16,0},{32,16},{48,32},{64,112},{80,64},{96,80},{112,96},{1... | collective-permute-start | bytes 786440 | tf_op jit(solution)/shard_map/ppermute | solution.py:67
  100.0 10.6 %collective-permute-start.27 = (bf16[2,4,128,128]{3,2,1,0:T(8,128)(2,1)S(1)}, bf16[2,4,128,128]{3,2,1,0:T(8,128)(2,1)S(1)}, u32[]{:S(2)}, u32[]{:S(2)}) collective-permute-start(bf16[2,4,128,128]{3,2,1,0:T(8,128)(2,1)S(1)} %extend.3), channel_id=1, source_target_pairs={{0,64},{16,80},{32,96},{48,112},{1,65},{17,81},{33,97},{49,113},{2... | collective-permute-start | bytes 786440 | tf_op jit(solution)/shard_map/ppermute | solution.py:58
  113.2 5.1 %collective-permute-start.29 = (f32[8,128]{1,0:T(8,128)S(1)}, f32[8,128]{1,0:T(8,128)S(1)}, u32[]{:S(2)}, u32[]{:S(2)}) collective-permute-start(f32[8,128]{1,0:T(8,128)S(1)} %add.309.first), channel_id=1, source_target_pairs={{0,8},{1,9},{2,10},{3,11},{4,12},{5,13},{6,14},{7,15},{8,0},{9,1},... | collective-permute-start | bytes 12296 | tf_op jit(solution)/shard_map/ppermute | solution.py:481
  (14 other events, 84.3 us)

commit v5 on v4

--- a/solution.py
+++ b/solution.py
@@ -92,7 +92,7 @@
     accs = take(n_acc)
     if mode == "qg":
         k_in, v_in, gain = take(3)
-    outs = take({"first": 4, "more": len(parts) * 4, "kv": 4, "qg": 3}[mode])
+    outs = take({"first": 4, "more": len(parts) * 4, "kv": 3, "qg": 3}[mode])
     loaded = take(len(loads))
     xbuf, xsem, wsem = take(3)
     held = held + loaded
@@ -117,10 +117,14 @@
             for core in (0, 1)
         ]
 
-    for p in range(len(parts)):
-        for i in range(len(parts[p])):
+    order = [(p, i) for p in range(len(parts)) for i in range(len(parts[p]))]
+
+    def start_x(chosen):
+        for p, i in chosen:
             for copy in x_copies(p, i):
                 copy.start()
+
+    start_x(order[:2])
     def start_loads(chosen):
         for i in chosen:
             for n in range(4):
@@ -143,9 +147,11 @@
             if n in (0, 2 if mode == "qg" else 0):
                 for copy in x_copies(p, i):
                     copy.wait()
+                k = order.index((p, i)) + 2
+                start_x(order[k : k + 1])
+                if k == max(2, len(order) - 1):
+                    start_loads(range(now, len(loads)))
             load(w - n_held, n)
-            if (p, n, i) == (0, 0, 0):
-                start_loads(range(now, len(loads)))
             got = jnp.dot(
                 xbuf[p, :, pl.ds(i * PIECE, PIECE)], held[w][n], preferred_element_type=F32
             )
@@ -167,7 +173,7 @@
                 k = 4 * p + n
                 outs[k][...] = product(p, n, accs[k] if k < n_acc else None)
     if mode == "kv":
-        k_out, v_out, s_out, s_half = outs
+        k_out, v_out, s_out = outs
         k_out[...] = jax.nn.silu(product(0, 0, accs[0])).astype(BF16)
         v_out[...] = jax.nn.silu(product(0, 1, accs[1])).astype(BF16)
         local = lax.broadcasted_iota(jnp.int32, (BLOCK, HEAD), 0)
@@ -180,8 +186,7 @@
                 state = lax.dot_general(
                     weighted, v_out[part(s, h)], (((0,), (0,)), ((), ())), preferred_element_type=F32
                 )
-                s_out[s, h] = state
-                s_half[s, h] = state.astype(BF16)
+                s_out[s, h] = state.astype(BF16)
     if mode == "qg":
         q_out, inner_out, gate_out = outs
         q_out[...] = jax.nn.silu(product(0, 2, accs[0])).astype(BF16)
@@ -231,13 +236,11 @@
     rows = index.size if isinstance(index, pl.Slice) else arrays[0].shape[-2]
     half = jax.ShapeDtypeStruct((rows, WIDTH), BF16)
     wide = pltpu.VMEM((rows, WIDTH), F32)
-    state = [
-        jax.ShapeDtypeStruct((rows // BLOCK, WIDTH // HEAD, HEAD, HEAD), t) for t in (F32, BF16)
-    ]
+    state = jax.ShapeDtypeStruct((rows // BLOCK, WIDTH // HEAD, HEAD, HEAD), BF16)
     outs = {
         "first": [wide] * 4,
         "more": [wide] * (4 * len(parts)),
-        "kv": [half, half, *state],
+        "kv": [half, half, state],
         "qg": [half, wide, wide],
     }[mode]
     n_outs = len(outs)
@@ -296,7 +299,8 @@
         for h in range(state.shape[1]):
             share = functools.partial(carried_share, meta, lengths, decay, first_seq + s, h)
             mine, other = one_or(odd, share(-1)), one_or(jnp.logical_not(odd), share(0))
-            out[s, h] = (mine * state[s, h] + other * before[s, h].astype(F32)).astype(BF16)
+            got = mine * state[s, h].astype(F32) + other * before[s, h].astype(F32)
+            out[s, h] = got.astype(BF16)
 
 
 def quad_kernel(first_seq, meta, lengths, decay, state, before, out):
@@ -539,14 +543,14 @@
     acc, a3, far3 = in_order(acc, a3, far3)
 
     last_y, last_z = [two(a3, 3)], [one(far3, 1, 3)]
-    keys_y, values_y, state_y, sent_y = project("kv", scalars, last_y, held, accs=acc[:2])
+    keys_y, values_y, sent_y = project("kv", scalars, last_y, held, accs=acc[:2])
     one_y = swapped(sent_y, 1)
-    acc, state_y = in_order(acc, state_y)
-    keys_z, values_z, state_z, sent_z = project(
+    acc, state_y = in_order(acc, sent_y)
+    keys_z, values_z, sent_z = project(
         "kv", scalars, last_z, held, accs=acc[4:6], first_seq=half
     )
     above_z = ahead(sent_z, 4)
-    acc, state_z = in_order(acc, state_z)
+    acc, state_z = in_order(acc, sent_z)
     query_y, inner_y, gate_y = project(
         "qg", scalars, last_y, held, accs=acc[2:4], extra=(keys_y, values_y, gain)
     )
@@ -554,7 +558,7 @@
     pair_y = extend(pair_kernel, scalars, state_y, one_y, 0)
     two_y = swapped(pair_y, 2)
     above_z, pair_y = in_order(above_z, pair_y)
-    chosen = choose(scalars, sent_z, above_z)
+    chosen = choose(scalars, state_z, above_z)
     around_z = [round_x(x, distance) for distance, x in enumerate(chosen, 1)]
     acc, chosen = in_order(acc, chosen)
     query_z, inner_z, gate_z = project(

time: 128 us -> 127 us (level)
  no operation moved by 1% of the time
where the time goes in v5:
time: 127 us
  Pallas kernels  50.5 us (40%)
  starting transfers between devices  45.9 us (36%)
  waiting for transfers between devices  28.3 us (22%)
  local copies, waits for them, and re-layouts  2.21 us (2%)
    pallas_call x8, Pallas kernels, project(): pl.pallas_call(functools.partial(project_kernel, mode, first_seq, plan),...  42.6 us
    ppermute x4, starting transfers between devices, across(): return lax.ppermute(x, 'tp', ACROSS)  12.2 us
    ppermute x6, starting transfers between devices, ring(): return lax.ppermute(x, 'tp', RING)  10 us
    ppermute x4, waiting for transfers between devices, all_sum(): x = add(x, lax.ppermute(x, 'tp', route))  8.83 us
    ppermute x6, waiting for transfers between devices, ring(): return lax.ppermute(x, 'tp', RING)  8.15 us
    ppermute x2, starting transfers between devices, ahead(): lax.ppermute(x, 'ctx', [(i, i + distance) for i in range(n - distance)])  6.66 us
    ppermute x4, starting transfers between devices, all_sum(): x = add(x, lax.ppermute(x, 'tp', route))  5.95 us
    ppermute x3, waiting for transfers between devices, round_x(): lax.ppermute(x, 'ctx', [(i, i // 4 * 4 + (i + distance) % 4) for i in ran...  5.38 us
  transfers between devices with their start and end apart: 32, of which 13 were waited for; matrix products, arithmetic and copies ran while one was open for 1% of the time, Pallas kernels for 38%

profile of v5, /device:TPU:0, one launch (start us, length us, event | category | flops | bytes accessed | tf_op | source)
XLA Modules:
  0.0 127.3 jit_solution(4426577574174851244)
XLA Ops:
  1.2 3.4 %collective-permute-start.1 = (bf16[512,384]{1,0:T(8,128)(2,1)S(1)}, bf16[512,384]{1,0:T(8,128)(2,1)S(1)}, u32[]{:S(2)}, u32[]{:S(2)}) collective-permute-start(bf16[512,384]{1,0:T(8,128)(2,1)S(1)} %bitcast.27), channel_id=1, source_target_pairs={{0,8},{1,9},{2,10},{3,11},{4,12},{5,13},{6,14},{7,15},{8,0},{9,1},... | collective-permute-start | bytes 1179656 | tf_op jit(solution)/shard_map/ppermute | solution.py:49
  7.5 5.0 %project_first.1 = (f32[512,512]{1,0:T(8,128)S(1)}, f32[512,512]{1,0:T(8,128)S(1)}, f32[512,512]{1,0:T(8,128)S(1)}, f32[512,512]{1,0:T(8,128)S(1)}, bf16[4,768,5...) custom-call(s32[18]{0:T(128)S(1)} %stack.77.refs_0_.meta, bf16[1024,384]{1,0:T(8,128)(2,1)} %bitcast.23, ...), custom_call_target="tpu_custom_call" | custom-call | flops 1610612736 | bytes 786432 | tf_op jit(solution)/shard_map/project_first/pallas_call | solution.py:257
  16.7 3.3 %collective-permute-start.7 = (bf16[2,512,384]{2,1,0:T(8,128)(2,1)}, bf16[2,512,384]{2,1,0:T(8,128)(2,1)S(1)}, u32[]{:S(2)}, u32[]{:S(2)}) collective-permute-start(bf16[2,512,384]{2,1,0:T(8,128)(2,1)} %stack.79), channel_id=1, source_target_pairs={{0,8},{1,9},{2,10},{3,11},{4,12},{5,13},{6,14},{7,15},{8,0},{9,1},... | collective-permute-start | bytes 2359304 | tf_op jit(solution)/shard_map/ppermute | solution.py:49
  21.9 1.9 %collective-permute-start.6 = (bf16[512,384]{1,0:T(8,128)(2,1)S(1)}, bf16[512,384]{1,0:T(8,128)(2,1)S(1)}, u32[]{:S(2)}, u32[]{:S(2)}) collective-permute-start(bf16[512,384]{1,0:T(8,128)(2,1)S(1)} %collective-permute-done.2.refs_5_.second), channel_id=1, source_target_pairs={{0,2},{1,7},{2,4},{3,1},{4,6},{5,3},{6,0},{7,5},{8,10},{9,15},{10,... | collective-permute-start | bytes 1179656 | tf_op jit(solution)/shard_map/ppermute | solution.py:45
  23.9 7.3 %project_more.3 = (f32[512,512]{1,0:T(8,128)S(1)}, f32[512,512]{1,0:T(8,128)S(1)}, f32[512,512]{1,0:T(8,128)S(1)}, f32[512,512]{1,0:T(8,128)S(1)}, f32[512,512]{...) custom-call(s32[18]{0:T(128)S(1)} %stack.77.refs_0_.meta, ...), custom_call_target="tpu_custom_call", output_to_operand_aliasing={{0}: (13, {}), {1}: (14, {}), {2}: (15, {}), {3}: (16, {})} | custom-call | flops 4831838208 | bytes 786432 | tf_op jit(solution)/shard_map/project_more/pallas_call | solution.py:257
  31.2 7.2 %collective-permute-done.6.refs_3_ = bf16[512,384]{1,0:T(8,128)(2,1)S(1)} collective-permute-done((bf16[512,384]{1,0:T(8,128)(2,1)S(1)}, bf16[512,384]{1,0:T(8,128)(2,1)S(1)}, u32[]{:S(2)}, u32[]{:S(2)}) %collective-permute-start.6) | collective-permute-done | bytes 393248 | tf_op jit(solution)/shard_map/ppermute | solution.py:45
  40.4 1.9 %collective-permute-start.12 = (bf16[512,384]{1,0:T(8,128)(2,1)S(1)}, bf16[512,384]{1,0:T(8,128)(2,1)S(1)}, u32[]{:S(2)}, u32[]{:S(2)}) collective-permute-start(bf16[512,384]{1,0:T(8,128)(2,1)S(1)} %collective-permute-done.6.refs_3_), channel_id=1, source_target_pairs={{0,2},{1,7},{2,4},{3,1},{4,6},{5,3},{6,0},{7,5},{8,10},{9,15},{10,... | collective-permute-start | bytes 1179656 | tf_op jit(solution)/shard_map/ppermute | solution.py:45
  42.4 3.1 %collective-permute-start.13 = (bf16[512,384]{1,0:T(8,128)(2,1)S(1)}, bf16[512,384]{1,0:T(8,128)(2,1)S(1)}, u32[]{:S(2)}, u32[]{:S(2)}) collective-permute-start(bf16[512,384]{1,0:T(8,128)(2,1)S(1)} %collective-permute-done.6.refs_3_), channel_id=1, source_target_pairs={{0,8},{1,9},{2,10},{3,11},{4,12},{5,13},{6,14},{7,15},{8,0},{9,1},... | collective-permute-start | bytes 1179656 | tf_op jit(solution)/shard_map/ppermute | solution.py:49
  45.5 10.2 %project_more.4 = (f32[512,512]{1,0:T(8,128)S(1)}, f32[512,512]{1,0:T(8,128)S(1)}, f32[512,512]{1,0:T(8,128)S(1)}, f32[512,512]{1,0:T(8,128)S(1)}, f32[512,512]{...) custom-call(s32[18]{0:T(128)S(1)} %stack.77.refs_0_.meta, ...), custom_call_target="tpu_custom_call", output_to_operand_aliasing={{0}: (15, {}), {1}: (16, {}), {2}: (17, {}), {3}: (18, {}),... | custom-call | flops 8053063680 | bytes 786432 | tf_op jit(solution)/shard_map/project_more/pallas_call | solution.py:257
  58.3 2.4 %collective-permute-start.18 = (bf16[512,384]{1,0:T(8,128)(2,1)S(1)}, bf16[512,384]{1,0:T(8,128)(2,1)S(1)}, u32[]{:S(2)}, u32[]{:S(2)}) collective-permute-start(bf16[512,384]{1,0:T(8,128)(2,1)S(1)} %collective-permute-done.12.refs_3_), channel_id=1, source_target_pairs={{0,8},{1,9},{2,10},{3,11},{4,12},{5,13},{6,14},{7,15},{8,0},{9,1},... | collective-permute-start | bytes 1179656 | tf_op jit(solution)/shard_map/ppermute | solution.py:49
  60.8 8.4 %project_more.5 = (f32[512,512]{1,0:T(8,128)S(1)}, f32[512,512]{1,0:T(8,128)S(1)}, f32[512,512]{1,0:T(8,128)S(1)}, f32[512,512]{1,0:T(8,128)S(1)}, f32[512,512]{...) custom-call(s32[18]{0:T(128)S(1)} %stack.77.refs_0_.meta, ...), custom_call_target="tpu_custom_call", output_to_operand_aliasing={{0}: (14, {}), {1}: (15, {}), {2}: (16, {}), {3}: (17, {}),... | custom-call | flops 6442450944 | bytes 786432 | tf_op jit(solution)/shard_map/project_more/pallas_call | solution.py:257
  73.5 3.2 %project_kv.2 = (bf16[512,512]{1,0:T(8,128)(2,1)S(1)}, bf16[512,512]{1,0:T(8,128)(2,1)S(1)}, bf16[2,4,128,128]{3,2,1,0:T(8,128)(2,1)S(1)}) custom-call(s32[18]{0:T(128)S(1)} %stack.77.refs_0_.meta, s32[4,4]{1,0:T(4,128)S(1)} %copy-done.3, f32[4]{0:T(128)S(1)} %copy-done.4, bf16[2,512,384]{2,1,0:T(8,128)(2,1)S(1)} %collective-permute-done.17.refs_3_, ...), custom_call_target="tpu_custom_call" | custom-call | flops 1610612736 | bytes 786432 | tf_op jit(solution)/shard_map/project_kv/pallas_call | solution.py:257
  78.4 2.3 %project_kv.3 = (bf16[512,512]{1,0:T(8,128)(2,1)S(1)}, bf16[512,512]{1,0:T(8,128)(2,1)S(1)}, bf16[2,4,128,128]{3,2,1,0:T(8,128)(2,1)S(1)}) custom-call(s32[18]{0:T(128)S(1)} %stack.77.refs_0_.meta, s32[4,4]{1,0:T(4,128)S(1)} %copy-done.3, f32[4]{0:T(128)S(1)} %copy-done.4, bf16[512,384]{1,0:T(8,128)(2,1)S(1)} %collective-permute-done.18.refs_3_, ...), custom_call_target="tpu_custom_call" | custom-call | flops 805306368 | bytes 786432 | tf_op jit(solution)/shard_map/project_kv/pallas_call | solution.py:257
  80.7 2.8 %collective-permute-start.22 = (bf16[2,4,128,128]{3,2,1,0:T(8,128)(2,1)S(1)}, bf16[2,4,128,128]{3,2,1,0:T(8,128)(2,1)S(1)}, u32[]{:S(2)}, u32[]{:S(2)}) collective-permute-start(bf16[2,4,128,128]{3,2,1,0:T(8,128)(2,1)S(1)} %get-tuple-element.222.state), channel_id=1, source_target_pairs={{0,64},{16,80},{32,96},{48,112},{1,65},{17,81},{33,97},{49,113},{2... | collective-permute-start | bytes 786440 | tf_op jit(solution)/shard_map/ppermute | solution.py:58
  83.5 3.5 %project_qg.2 = (bf16[512,512]{1,0:T(8,128)(2,1)S(1)}, f32[512,512]{1,0:T(8,128)S(1)}, f32[512,512]{1,0:T(8,128)S(1)}) custom-call(s32[18]{0:T(128)S(1)} %stack.77.refs_0_.meta, s32[4,4]{1,0:T(4,128)S(1)} %copy-done.3, f32[4]{0:T(128)S(1)} %copy-done.4, bf16[2,512,384]{2,1,0:T(8,128)(2,1)S(1)} %collective-permute-done.17.refs_3_, ...), custom_call_target="tpu_custom_call" | custom-call | flops 1610612736 | bytes 786432 | tf_op jit(solution)/shard_map/project_qg/pallas_call | solution.py:257
  87.7 2.8 %collective-permute-start.23 = (bf16[2,4,128,128]{3,2,1,0:T(8,128)(2,1)S(1)}, bf16[2,4,128,128]{3,2,1,0:T(8,128)(2,1)S(1)}, u32[]{:S(2)}, u32[]{:S(2)}) collective-permute-start(bf16[2,4,128,128]{3,2,1,0:T(8,128)(2,1)S(1)} %extend.2.state), channel_id=1, source_target_pairs={{0,32},{16,48},{32,0},{48,16},{64,96},{80,112},{96,64},{112,80},{1... | collective-permute-start | bytes 786440 | tf_op jit(solution)/shard_map/ppermute | solution.py:62
  91.6 2.0 %collective-permute-start.25 = (bf16[2,4,128,128]{3,2,1,0:T(8,128)(2,1)S(1)}, bf16[2,4,128,128]{3,2,1,0:T(8,128)(2,1)S(1)}, u32[]{:S(2)}, u32[]{:S(2)}) collective-permute-start(bf16[2,4,128,128]{3,2,1,0:T(8,128)(2,1)S(1)} %get-tuple-element.226), channel_id=1, source_target_pairs={{0,32},{16,48},{32,0},{48,16},{64,96},{80,112},{96,64},{112,80},{1... | collective-permute-start | bytes 786440 | tf_op jit(solution)/shard_map/ppermute | solution.py:67
  95.4 2.6 %project_qg.3 = (bf16[512,512]{1,0:T(8,128)(2,1)S(1)}, f32[512,512]{1,0:T(8,128)S(1)}, f32[512,512]{1,0:T(8,128)S(1)}) custom-call(s32[18]{0:T(128)S(1)} %stack.77.refs_0_.meta, s32[4,4]{1,0:T(4,128)S(1)} %copy-done.3, f32[4]{0:T(128)S(1)} %copy-done.4, bf16[512,384]{1,0:T(8,128)(2,1)S(1)} %collective-permute-done.18.refs_3_, ...), custom_call_target="tpu_custom_call" | custom-call | flops 805306368 | bytes 786432 | tf_op jit(solution)/shard_map/project_qg/pallas_call | solution.py:257
  99.3 3.9 %collective-permute-start.27 = (bf16[2,4,128,128]{3,2,1,0:T(8,128)(2,1)S(1)}, bf16[2,4,128,128]{3,2,1,0:T(8,128)(2,1)S(1)}, u32[]{:S(2)}, u32[]{:S(2)}) collective-permute-start(bf16[2,4,128,128]{3,2,1,0:T(8,128)(2,1)S(1)} %extend.3), channel_id=1, source_target_pairs={{0,64},{16,80},{32,96},{48,112},{1,65},{17,81},{33,97},{49,113},{2... | collective-permute-start | bytes 786440 | tf_op jit(solution)/shard_map/ppermute | solution.py:58
  104.1 4.4 %collective-permute-done.25.refs_1_ = bf16[2,4,128,128]{3,2,1,0:T(8,128)(2,1)S(1)} collective-permute-done((bf16[2,4,128,128]{3,2,1,0:T(8,128)(2,1)S(1)}, bf16[2,4,128,128]{3,2,1,0:T(8,128)(2,1)S(1)}, u32[]{:S(2)}, u32[]{:S(2)}) %collective-permute-start.25) | collective-permute-done | bytes 262176 | tf_op jit(solution)/shard_map/ppermute | solution.py:67
  112.5 2.9 %collective-permute-start.29 = (f32[8,128]{1,0:T(8,128)S(1)}, f32[8,128]{1,0:T(8,128)S(1)}, u32[]{:S(2)}, u32[]{:S(2)}) collective-permute-start(f32[8,128]{1,0:T(8,128)S(1)} %add.309.first), channel_id=1, source_target_pairs={{0,8},{1,9},{2,10},{3,11},{4,12},{5,13},{6,14},{7,15},{8,0},{9,1},... | collective-permute-start | bytes 12296 | tf_op jit(solution)/shard_map/ppermute | solution.py:485
  115.4 2.2 %collective-permute-done.29.second = f32[8,128]{1,0:T(8,128)S(1)} collective-permute-done((f32[8,128]{1,0:T(8,128)S(1)}, f32[8,128]{1,0:T(8,128)S(1)}, u32[]{:S(2)}, u32[]{:S(2)}) %collective-permute-start.29) | collective-permute-done | bytes 4128 | tf_op jit(solution)/shard_map/ppermute | solution.py:485
  118.8 2.3 %collective-permute-done.30.second = f32[8,128]{1,0:T(8,128)S(1)} collective-permute-done((f32[8,128]{1,0:T(8,128)S(1)}, f32[8,128]{1,0:T(8,128)S(1)}, u32[]{:S(2)}, u32[]{:S(2)}) %collective-permute-start.30) | collective-permute-done | bytes 4128 | tf_op jit(solution)/shard_map/ppermute | solution.py:485
  122.9 3.1 %collective-permute-done.31.second = f32[8,128]{1,0:T(8,128)S(1)} collective-permute-done((f32[8,128]{1,0:T(8,128)S(1)}, f32[8,128]{1,0:T(8,128)S(1)}, u32[]{:S(2)}, u32[]{:S(2)}) %collective-permute-start.31) | collective-permute-done | bytes 4128 | tf_op jit(solution)/shard_map/ppermute | solution.py:485
  (75 shorter events, 34.7 us)
Async XLA Ops:
  0.0 6.6 %collective-permute-start = (bf16[1024,384]{1,0:T(8,128)(2,1)}, bf16[1024,384]{1,0:T(8,128)(2,1)S(1)}, u32[]{:S(2)}, u32[]{:S(2)}) collective-permute-start(bf16[1024,384]{1,0:T(8,128)(2,1)} %bitcast.22), channel_id=1, source_target_pairs={{0,1},{1,0},{2,3},{3,2},{4,5},{5,4},{6,7},{7,6},{8,9},{9,8},{10,11... | collective-permute-start | bytes 2359304 | tf_op jit(solution)/shard_map/ppermute | solution.py:53
  1.2 13.1 %collective-permute-start.1 = (bf16[512,384]{1,0:T(8,128)(2,1)S(1)}, bf16[512,384]{1,0:T(8,128)(2,1)S(1)}, u32[]{:S(2)}, u32[]{:S(2)}) collective-permute-start(bf16[512,384]{1,0:T(8,128)(2,1)S(1)} %bitcast.27), channel_id=1, source_target_pairs={{0,8},{1,9},{2,10},{3,11},{4,12},{5,13},{6,14},{7,15},{8,0},{9,1},... | collective-permute-start | bytes 1179656 | tf_op jit(solution)/shard_map/ppermute | solution.py:49
  4.6 9.8 %collective-permute-start.2 = (bf16[512,384]{1,0:T(8,128)(2,1)S(1)}, bf16[512,384]{1,0:T(8,128)(2,1)S(1)}, u32[]{:S(2)}, u32[]{:S(2)}) collective-permute-start(bf16[512,384]{1,0:T(8,128)(2,1)S(1)} %bitcast.25), channel_id=1, source_target_pairs={{0,2},{1,7},{2,4},{3,1},{4,6},{5,3},{6,0},{7,5},{8,10},{9,15},{10,... | collective-permute-start | bytes 1179656 | tf_op jit(solution)/shard_map/ppermute | solution.py:45
  14.3 9.5 %collective-permute-start.3 = (bf16[512,384]{1,0:T(8,128)(2,1)S(1)}, bf16[512,384]{1,0:T(8,128)(2,1)S(1)}, u32[]{:S(2)}, u32[]{:S(2)}) collective-permute-start(bf16[512,384]{1,0:T(8,128)(2,1)S(1)} %collective-permute-done.1.refs_1_.second), channel_id=1, source_target_pairs={{0,1},{1,0},{2,3},{3,2},{4,5},{5,4},{6,7},{7,6},{8,9},{9,8},{10,11... | collective-permute-start | bytes 1179656 | tf_op jit(solution)/shard_map/ppermute | solution.py:53
  14.6 9.2 %collective-permute-start.4 = (bf16[512,384]{1,0:T(8,128)(2,1)S(1)}, bf16[512,384]{1,0:T(8,128)(2,1)S(1)}, u32[]{:S(2)}, u32[]{:S(2)}) collective-permute-start(bf16[512,384]{1,0:T(8,128)(2,1)S(1)} %collective-permute-done.2.refs_5_.second), channel_id=1, source_target_pairs={{0,1},{1,0},{2,3},{3,2},{4,5},{5,4},{6,7},{7,6},{8,9},{9,8},{10,11... | collective-permute-start | bytes 1179656 | tf_op jit(solution)/shard_map/ppermute | solution.py:53
  16.7 21.8 %collective-permute-start.7 = (bf16[2,512,384]{2,1,0:T(8,128)(2,1)}, bf16[2,512,384]{2,1,0:T(8,128)(2,1)S(1)}, u32[]{:S(2)}, u32[]{:S(2)}) collective-permute-start(bf16[2,512,384]{2,1,0:T(8,128)(2,1)} %stack.79), channel_id=1, source_target_pairs={{0,8},{1,9},{2,10},{3,11},{4,12},{5,13},{6,14},{7,15},{8,0},{9,1},... | collective-permute-start | bytes 2359304 | tf_op jit(solution)/shard_map/ppermute | solution.py:49
  20.0 18.4 %collective-permute-start.5 = (bf16[2,512,384]{2,1,0:T(8,128)(2,1)}, bf16[2,512,384]{2,1,0:T(8,128)(2,1)S(1)}, u32[]{:S(2)}, u32[]{:S(2)}) collective-permute-start(bf16[2,512,384]{2,1,0:T(8,128)(2,1)} %stack.78), channel_id=1, source_target_pairs={{0,2},{1,7},{2,4},{3,1},{4,6},{5,3},{6,0},{7,5},{8,10},{9,15},{10,... | collective-permute-start | bytes 2359304 | tf_op jit(solution)/shard_map/ppermute | solution.py:45
  21.9 16.5 %collective-permute-start.6 = (bf16[512,384]{1,0:T(8,128)(2,1)S(1)}, bf16[512,384]{1,0:T(8,128)(2,1)S(1)}, u32[]{:S(2)}, u32[]{:S(2)}) collective-permute-start(bf16[512,384]{1,0:T(8,128)(2,1)S(1)} %collective-permute-done.2.refs_5_.second), channel_id=1, source_target_pairs={{0,2},{1,7},{2,4},{3,1},{4,6},{5,3},{6,0},{7,5},{8,10},{9,15},{10,... | collective-permute-start | bytes 1179656 | tf_op jit(solution)/shard_map/ppermute | solution.py:45
  38.4 7.1 %collective-permute-start.10 = (bf16[2,512,384]{2,1,0:T(8,128)(2,1)S(1)}, bf16[2,512,384]{2,1,0:T(8,128)(2,1)S(1)}, u32[]{:S(2)}, u32[]{:S(2)}) collective-permute-start(bf16[2,512,384]{2,1,0:T(8,128)(2,1)S(1)} %collective-permute-done.7.refs_5_), channel_id=1, source_target_pairs={{0,1},{1,0},{2,3},{3,2},{4,5},{5,4},{6,7},{7,6},{8,9},{9,8},{10,11... | collective-permute-start | bytes 2359304 | tf_op jit(solution)/shard_map/ppermute | solution.py:53
  38.4 7.1 %collective-permute-start.8 = (bf16[2,512,384]{2,1,0:T(8,128)(2,1)S(1)}, bf16[2,512,384]{2,1,0:T(8,128)(2,1)S(1)}, u32[]{:S(2)}, u32[]{:S(2)}) collective-permute-start(bf16[2,512,384]{2,1,0:T(8,128)(2,1)S(1)} %collective-permute-done.5.refs_1_), channel_id=1, source_target_pairs={{0,1},{1,0},{2,3},{3,2},{4,5},{5,4},{6,7},{7,6},{8,9},{9,8},{10,11... | collective-permute-start | bytes 2359304 | tf_op jit(solution)/shard_map/ppermute | solution.py:53
  39.0 17.7 %collective-permute-start.11 = (bf16[2,512,384]{2,1,0:T(8,128)(2,1)S(1)}, bf16[2,512,384]{2,1,0:T(8,128)(2,1)S(1)}, u32[]{:S(2)}, u32[]{:S(2)}) collective-permute-start(bf16[2,512,384]{2,1,0:T(8,128)(2,1)S(1)} %collective-permute-done.5.refs_1_), channel_id=1, source_target_pairs={{0,2},{1,7},{2,4},{3,1},{4,6},{5,3},{6,0},{7,5},{8,10},{9,15},{10,... | collective-permute-start | bytes 2359304 | tf_op jit(solution)/shard_map/ppermute | solution.py:45
  40.4 16.3 %collective-permute-start.12 = (bf16[512,384]{1,0:T(8,128)(2,1)S(1)}, bf16[512,384]{1,0:T(8,128)(2,1)S(1)}, u32[]{:S(2)}, u32[]{:S(2)}) collective-permute-start(bf16[512,384]{1,0:T(8,128)(2,1)S(1)} %collective-permute-done.6.refs_3_), channel_id=1, source_target_pairs={{0,2},{1,7},{2,4},{3,1},{4,6},{5,3},{6,0},{7,5},{8,10},{9,15},{10,... | collective-permute-start | bytes 1179656 | tf_op jit(solution)/shard_map/ppermute | solution.py:45
  42.4 14.3 %collective-permute-start.13 = (bf16[512,384]{1,0:T(8,128)(2,1)S(1)}, bf16[512,384]{1,0:T(8,128)(2,1)S(1)}, u32[]{:S(2)}, u32[]{:S(2)}) collective-permute-start(bf16[512,384]{1,0:T(8,128)(2,1)S(1)} %collective-permute-done.6.refs_3_), channel_id=1, source_target_pairs={{0,8},{1,9},{2,10},{3,11},{4,12},{5,13},{6,14},{7,15},{8,0},{9,1},... | collective-permute-start | bytes 1179656 | tf_op jit(solution)/shard_map/ppermute | solution.py:49
  57.3 13.5 %collective-permute-start.17 = (bf16[2,512,384]{2,1,0:T(8,128)(2,1)S(1)}, bf16[2,512,384]{2,1,0:T(8,128)(2,1)S(1)}, u32[]{:S(2)}, u32[]{:S(2)}) collective-permute-start(bf16[2,512,384]{2,1,0:T(8,128)(2,1)S(1)} %collective-permute-done.11.refs_1_), channel_id=1, source_target_pairs={{0,2},{1,7},{2,4},{3,1},{4,6},{5,3},{6,0},{7,5},{8,10},{9,15},{10,... | collective-permute-start | bytes 2359304 | tf_op jit(solution)/shard_map/ppermute | solution.py:45
  58.3 12.5 %collective-permute-start.18 = (bf16[512,384]{1,0:T(8,128)(2,1)S(1)}, bf16[512,384]{1,0:T(8,128)(2,1)S(1)}, u32[]{:S(2)}, u32[]{:S(2)}) collective-permute-start(bf16[512,384]{1,0:T(8,128)(2,1)S(1)} %collective-permute-done.12.refs_3_), channel_id=1, source_target_pairs={{0,8},{1,9},{2,10},{3,11},{4,12},{5,13},{6,14},{7,15},{8,0},{9,1},... | collective-permute-start | bytes 1179656 | tf_op jit(solution)/shard_map/ppermute | solution.py:49
  71.6 6.8 %collective-permute-start.20 = (bf16[512,384]{1,0:T(8,128)(2,1)S(1)}, bf16[512,384]{1,0:T(8,128)(2,1)S(1)}, u32[]{:S(2)}, u32[]{:S(2)}) collective-permute-start(bf16[512,384]{1,0:T(8,128)(2,1)S(1)} %collective-permute-done.18.refs_3_), channel_id=1, source_target_pairs={{0,1},{1,0},{2,3},{3,2},{4,5},{5,4},{6,7},{7,6},{8,9},{9,8},{10,11... | collective-permute-start | bytes 1179656 | tf_op jit(solution)/shard_map/ppermute | solution.py:53
  76.8 10.2 %collective-permute-start.21 = (bf16[2,4,128,128]{3,2,1,0:T(8,128)(2,1)S(1)}, bf16[2,4,128,128]{3,2,1,0:T(8,128)(2,1)S(1)}, u32[]{:S(2)}, u32[]{:S(2)}) collective-permute-start(bf16[2,4,128,128]{3,2,1,0:T(8,128)(2,1)S(1)} %get-tuple-element.223.state), channel_id=1, source_target_pairs={{0,16},{16,0},{32,48},{48,32},{64,80},{80,64},{96,112},{112,96},{1... | collective-permute-start | bytes 786440 | tf_op jit(solution)/shard_map/ppermute | solution.py:62
  80.7 9.8 %collective-permute-start.22 = (bf16[2,4,128,128]{3,2,1,0:T(8,128)(2,1)S(1)}, bf16[2,4,128,128]{3,2,1,0:T(8,128)(2,1)S(1)}, u32[]{:S(2)}, u32[]{:S(2)}) collective-permute-start(bf16[2,4,128,128]{3,2,1,0:T(8,128)(2,1)S(1)} %get-tuple-element.222.state), channel_id=1, source_target_pairs={{0,64},{16,80},{32,96},{48,112},{1,65},{17,81},{33,97},{49,113},{2... | collective-permute-start | bytes 786440 | tf_op jit(solution)/shard_map/ppermute | solution.py:58
  87.7 10.8 %collective-permute-start.23 = (bf16[2,4,128,128]{3,2,1,0:T(8,128)(2,1)S(1)}, bf16[2,4,128,128]{3,2,1,0:T(8,128)(2,1)S(1)}, u32[]{:S(2)}, u32[]{:S(2)}) collective-permute-start(bf16[2,4,128,128]{3,2,1,0:T(8,128)(2,1)S(1)} %extend.2.state), channel_id=1, source_target_pairs={{0,32},{16,48},{32,0},{48,16},{64,96},{80,112},{96,64},{112,80},{1... | collective-permute-start | bytes 786440 | tf_op jit(solution)/shard_map/ppermute | solution.py:62
  91.3 12.9 %collective-permute-start.24 = (bf16[2,4,128,128]{3,2,1,0:T(8,128)(2,1)S(1)}, bf16[2,4,128,128]{3,2,1,0:T(8,128)(2,1)S(1)}, u32[]{:S(2)}, u32[]{:S(2)}) collective-permute-start(bf16[2,4,128,128]{3,2,1,0:T(8,128)(2,1)S(1)} %get-tuple-element.225), channel_id=1, source_target_pairs={{0,16},{16,32},{32,48},{48,0},{64,80},{80,96},{96,112},{112,64},{1... | collective-permute-start | bytes 786440 | tf_op jit(solution)/shard_map/ppermute | solution.py:67
  91.6 17.0 %collective-permute-start.25 = (bf16[2,4,128,128]{3,2,1,0:T(8,128)(2,1)S(1)}, bf16[2,4,128,128]{3,2,1,0:T(8,128)(2,1)S(1)}, u32[]{:S(2)}, u32[]{:S(2)}) collective-permute-start(bf16[2,4,128,128]{3,2,1,0:T(8,128)(2,1)S(1)} %get-tuple-element.226), channel_id=1, source_target_pairs={{0,32},{16,48},{32,0},{48,16},{64,96},{80,112},{96,64},{112,80},{1... | collective-permute-start | bytes 786440 | tf_op jit(solution)/shard_map/ppermute | solution.py:67
  93.6 14.9 %collective-permute-start.26 = (bf16[2,4,128,128]{3,2,1,0:T(8,128)(2,1)S(1)}, bf16[2,4,128,128]{3,2,1,0:T(8,128)(2,1)S(1)}, u32[]{:S(2)}, u32[]{:S(2)}) collective-permute-start(bf16[2,4,128,128]{3,2,1,0:T(8,128)(2,1)S(1)} %get-tuple-element.227), channel_id=1, source_target_pairs={{0,48},{16,0},{32,16},{48,32},{64,112},{80,64},{96,80},{112,96},{1... | collective-permute-start | bytes 786440 | tf_op jit(solution)/shard_map/ppermute | solution.py:67
  99.3 10.6 %collective-permute-start.27 = (bf16[2,4,128,128]{3,2,1,0:T(8,128)(2,1)S(1)}, bf16[2,4,128,128]{3,2,1,0:T(8,128)(2,1)S(1)}, u32[]{:S(2)}, u32[]{:S(2)}) collective-permute-start(bf16[2,4,128,128]{3,2,1,0:T(8,128)(2,1)S(1)} %extend.3), channel_id=1, source_target_pairs={{0,64},{16,80},{32,96},{48,112},{1,65},{17,81},{33,97},{49,113},{2... | collective-permute-start | bytes 786440 | tf_op jit(solution)/shard_map/ppermute | solution.py:58
  112.5 5.1 %collective-permute-start.29 = (f32[8,128]{1,0:T(8,128)S(1)}, f32[8,128]{1,0:T(8,128)S(1)}, u32[]{:S(2)}, u32[]{:S(2)}) collective-permute-start(f32[8,128]{1,0:T(8,128)S(1)} %add.309.first), channel_id=1, source_target_pairs={{0,8},{1,9},{2,10},{3,11},{4,12},{5,13},{6,14},{7,15},{8,0},{9,1},... | collective-permute-start | bytes 12296 | tf_op jit(solution)/shard_map/ppermute | solution.py:485
  (14 other events, 83.4 us)

commit v6 on v5

--- a/solution.py
+++ b/solution.py
@@ -428,24 +428,28 @@
     )(*attns, *gates, squares)
 
 
-def stack_kernel(first, second, out, sems):
-    copies = [pltpu.make_async_copy(x, out.at[i], sems.at[i]) for i, x in enumerate((first, second))]
+def stack_kernel(n, *refs):
+    xs, outs, sems = refs[: 2 * n], refs[2 * n : 3 * n], refs[-1]
+    copies = [
+        pltpu.make_async_copy(x, outs[i // 2].at[i % 2], sems.at[i]) for i, x in enumerate(xs)
+    ]
     for copy in copies:
         copy.start()
     for copy in copies:
         copy.wait()
 
 
-def stack(first, second):
-    return pl.pallas_call(
-        stack_kernel,
-        out_shape=pltpu.HBM((2, *first.shape), first.dtype),
-        in_specs=[ANY] * 2,
-        out_specs=HBM,
-        scratch_shapes=[pltpu.SemaphoreType.DMA((2,))],
+def stack(*pairs):
+    parts = [x for pair in pairs for x in pair]
+    return pl.pallas_call(
+        functools.partial(stack_kernel, len(pairs)),
+        out_shape=[pltpu.HBM((2, *first.shape), first.dtype) for first, _ in pairs],
+        in_specs=[ANY] * len(parts),
+        out_specs=[HBM] * len(pairs),
+        scratch_shapes=[pltpu.SemaphoreType.DMA((len(parts),))],
         compiler_params=pltpu.CompilerParams(vmem_limit_bytes=2**20),
         name="stack",
-    )(first, second)
+    )(*parts)
 
 
 def add_kernel(first, second, out):
@@ -527,7 +531,8 @@
     acc = project("first", scalars, [[own_y]], held, weights, [0, 1])
     acc, y0, r1, part_z = in_order(acc, y0, r1, part_z)
 
-    a1, r2, far_a = ring(stack(part_y, y0)), ring(r1), across(stack(part_z, r1))
+    sent_y, sent_z = stack((part_y, y0), (part_z, r1))
+    a1, r2, far_a = ring(sent_y), ring(r1), across(sent_z)
     parts = [one(y0, 1, 0), [own_z] + one(r1, 0, 1)]
     acc = project("more", scalars, parts, held, weights, [2, 3, 4], acc)
     acc, a1, r2, far_a = in_order(acc, a1, r2, far_a)

time: 127 us -> 129 us (1.016)
  waiting for transfers between devices: 28.3 us -> 32.3 us
  starting transfers between devices: 45.9 us -> 42.3 us
    ppermute x4, waiting for transfers between devices: 3.44 us -> 8.07 us  [across(): return lax.ppermute(x, 'tp', ACROSS)]
    ppermute x6, waiting for transfers between devices: 8.15 us -> 3.72 us  [ring(): return lax.ppermute(x, 'tp', RING)]
    ppermute x6, starting transfers between devices: 10 us -> 7.1 us  [ring(): return lax.ppermute(x, 'tp', RING)]
    ppermute x4, starting transfers between devices: 5.95 us -> 4.05 us  [all_sum(): x = add(x, lax.ppermute(x, 'tp', route))]
    ppermute x4, waiting for transfers between devices: 8.83 us -> 10.7 us  [all_sum(): x = add(x, lax.ppermute(x, 'tp', route))]
    ppermute x11, waiting for transfers between devices: 2 us -> 3.66 us  [other_core(): return lax.ppermute(x, 'tp', CORE)]
  transfers between devices with their start and end apart: 32 -> 32, of which waited for: 13 -> 14; matrix products, arithmetic and copies ran while one was open for 1% -> 1% of each run, Pallas kernels for 38% -> 37%
where the time goes in v6:
time: 129 us; the launch traced here: 128 us
  Pallas kernels  50.2 us (39%)
  starting transfers between devices  42.3 us (33%)
  waiting for transfers between devices  32.3 us (25%)
  local copies, waits for them, and re-layouts  3.32 us (3%)
    pallas_call x8, Pallas kernels, project(): pl.pallas_call(functools.partial(project_kernel, mode, first_seq, plan),...  42.8 us
    ppermute x4, starting transfers between devices, across(): return lax.ppermute(x, 'tp', ACROSS)  13 us
    ppermute x4, waiting for transfers between devices, all_sum(): x = add(x, lax.ppermute(x, 'tp', route))  10.7 us
    ppermute x4, waiting for transfers between devices, across(): return lax.ppermute(x, 'tp', ACROSS)  8.07 us
    ppermute x2, starting transfers between devices, ahead(): lax.ppermute(x, 'ctx', [(i, i + distance) for i in range(n - distance)])  7.16 us
    ppermute x6, starting transfers between devices, ring(): return lax.ppermute(x, 'tp', RING)  7.1 us
    ppermute x3, waiting for transfers between devices, round_x(): lax.ppermute(x, 'ctx', [(i, i // 4 * 4 + (i + distance) % 4) for i in ran...  5.38 us
    ppermute x2, starting transfers between devices, swapped(): lax.ppermute(x, 'ctx', [(i, i ^ bit) for i in range(lax.axis_size('ctx'))])  4.4 us
  transfers between devices with their start and end apart: 32, of which 14 were waited for; matrix products, arithmetic and copies ran while one was open for 1% of the time, Pallas kernels for 37%

profile of v6, /device:TPU:0, one launch (start us, length us, event | category | flops | bytes accessed | tf_op | source)
XLA Modules:
  0.0 128.5 jit_solution(5936913426559510988)
XLA Ops:
  1.2 3.4 %collective-permute-start.1 = (bf16[512,384]{1,0:T(8,128)(2,1)S(1)}, bf16[512,384]{1,0:T(8,128)(2,1)S(1)}, u32[]{:S(2)}, u32[]{:S(2)}) collective-permute-start(bf16[512,384]{1,0:T(8,128)(2,1)S(1)} %bitcast.27), channel_id=1, source_target_pairs={{0,8},{1,9},{2,10},{3,11},{4,12},{5,13},{6,14},{7,15},{8,0},{9,1},... | collective-permute-start | bytes 1179656 | tf_op jit(solution)/shard_map/ppermute | solution.py:49
  7.5 5.0 %project_first.1 = (f32[512,512]{1,0:T(8,128)S(1)}, f32[512,512]{1,0:T(8,128)S(1)}, f32[512,512]{1,0:T(8,128)S(1)}, f32[512,512]{1,0:T(8,128)S(1)}, bf16[4,768,5...) custom-call(s32[18]{0:T(128)S(1)} %stack.76.refs_0_.meta, bf16[1024,384]{1,0:T(8,128)(2,1)} %bitcast.23, ...), custom_call_target="tpu_custom_call" | custom-call | flops 1610612736 | bytes 786432 | tf_op jit(solution)/shard_map/project_first/pallas_call | solution.py:257
  16.1 2.0 %collective-permute-start.5 = (bf16[2,512,384]{2,1,0:T(8,128)(2,1)}, bf16[2,512,384]{2,1,0:T(8,128)(2,1)S(1)}, u32[]{:S(2)}, u32[]{:S(2)}) collective-permute-start(bf16[2,512,384]{2,1,0:T(8,128)(2,1)} %get-tuple-element.150), channel_id=1, source_target_pairs={{0,2},{1,7},{2,4},{3,1},{4,6},{5,3},{6,0},{7,5},{8,10},{9,15},{10,... | collective-permute-start | bytes 2359304 | tf_op jit(solution)/shard_map/ppermute | solution.py:45
  18.1 3.2 %collective-permute-start.7 = (bf16[2,512,384]{2,1,0:T(8,128)(2,1)}, bf16[2,512,384]{2,1,0:T(8,128)(2,1)S(1)}, u32[]{:S(2)}, u32[]{:S(2)}) collective-permute-start(bf16[2,512,384]{2,1,0:T(8,128)(2,1)} %get-tuple-element.151), channel_id=1, source_target_pairs={{0,8},{1,9},{2,10},{3,11},{4,12},{5,13},{6,14},{7,15},{8,0},{9,1},... | collective-permute-start | bytes 2359304 | tf_op jit(solution)/shard_map/ppermute | solution.py:49
  21.3 1.9 %collective-permute-start.6 = (bf16[512,384]{1,0:T(8,128)(2,1)S(1)}, bf16[512,384]{1,0:T(8,128)(2,1)S(1)}, u32[]{:S(2)}, u32[]{:S(2)}) collective-permute-start(bf16[512,384]{1,0:T(8,128)(2,1)S(1)} %collective-permute-done.2.refs_5_.refs_3_), channel_id=1, source_target_pairs={{0,2},{1,7},{2,4},{3,1},{4,6},{5,3},{6,0},{7,5},{8,10},{9,15},{10,... | collective-permute-start | bytes 1179656 | tf_op jit(solution)/shard_map/ppermute | solution.py:45
  24.3 7.3 %project_more.3 = (f32[512,512]{1,0:T(8,128)S(1)}, f32[512,512]{1,0:T(8,128)S(1)}, f32[512,512]{1,0:T(8,128)S(1)}, f32[512,512]{1,0:T(8,128)S(1)}, f32[512,512]{...) custom-call(s32[18]{0:T(128)S(1)} %stack.76.refs_0_.meta, ...), custom_call_target="tpu_custom_call", output_to_operand_aliasing={{0}: (13, {}), {1}: (14, {}), {2}: (15, {}), {3}: (16, {})} | custom-call | flops 4831838208 | bytes 786432 | tf_op jit(solution)/shard_map/project_more/pallas_call | solution.py:257
  31.7 2.9 %collective-permute-done.6.refs_3_ = bf16[512,384]{1,0:T(8,128)(2,1)S(1)} collective-permute-done((bf16[512,384]{1,0:T(8,128)(2,1)S(1)}, bf16[512,384]{1,0:T(8,128)(2,1)S(1)}, u32[]{:S(2)}, u32[]{:S(2)}) %collective-permute-start.6) | collective-permute-done | bytes 393248 | tf_op jit(solution)/shard_map/ppermute | solution.py:45
  34.6 4.8 %collective-permute-done.7.refs_5_ = bf16[2,512,384]{2,1,0:T(8,128)(2,1)S(1)} collective-permute-done((bf16[2,512,384]{2,1,0:T(8,128)(2,1)}, bf16[2,512,384]{2,1,0:T(8,128)(2,1)S(1)}, u32[]{:S(2)}, u32[]{:S(2)}) %collective-permute-start.7) | collective-permute-done | bytes 786464 | tf_op jit(solution)/shard_map/ppermute | solution.py:49
  43.6 3.2 %collective-permute-start.13 = (bf16[512,384]{1,0:T(8,128)(2,1)S(1)}, bf16[512,384]{1,0:T(8,128)(2,1)S(1)}, u32[]{:S(2)}, u32[]{:S(2)}) collective-permute-start(bf16[512,384]{1,0:T(8,128)(2,1)S(1)} %collective-permute-done.6.refs_3_), channel_id=1, source_target_pairs={{0,8},{1,9},{2,10},{3,11},{4,12},{5,13},{6,14},{7,15},{8,0},{9,1},... | collective-permute-start | bytes 1179656 | tf_op jit(solution)/shard_map/ppermute | solution.py:49
  46.9 10.3 %project_more.4 = (f32[512,512]{1,0:T(8,128)S(1)}, f32[512,512]{1,0:T(8,128)S(1)}, f32[512,512]{1,0:T(8,128)S(1)}, f32[512,512]{1,0:T(8,128)S(1)}, f32[512,512]{...) custom-call(s32[18]{0:T(128)S(1)} %stack.76.refs_0_.meta, ...), custom_call_target="tpu_custom_call", output_to_operand_aliasing={{0}: (15, {}), {1}: (16, {}), {2}: (17, {}), {3}: (18, {}),... | custom-call | flops 8053063680 | bytes 786432 | tf_op jit(solution)/shard_map/project_more/pallas_call | solution.py:257
  58.6 3.2 %collective-permute-start.18 = (bf16[512,384]{1,0:T(8,128)(2,1)S(1)}, bf16[512,384]{1,0:T(8,128)(2,1)S(1)}, u32[]{:S(2)}, u32[]{:S(2)}) collective-permute-start(bf16[512,384]{1,0:T(8,128)(2,1)S(1)} %collective-permute-done.12.refs_3_), channel_id=1, source_target_pairs={{0,8},{1,9},{2,10},{3,11},{4,12},{5,13},{6,14},{7,15},{8,0},{9,1},... | collective-permute-start | bytes 1179656 | tf_op jit(solution)/shard_map/ppermute | solution.py:49
  61.8 8.5 %project_more.5 = (f32[512,512]{1,0:T(8,128)S(1)}, f32[512,512]{1,0:T(8,128)S(1)}, f32[512,512]{1,0:T(8,128)S(1)}, f32[512,512]{1,0:T(8,128)S(1)}, f32[512,512]{...) custom-call(s32[18]{0:T(128)S(1)} %stack.76.refs_0_.meta, ...), custom_call_target="tpu_custom_call", output_to_operand_aliasing={{0}: (14, {}), {1}: (15, {}), {2}: (16, {}), {3}: (17, {}),... | custom-call | flops 6442450944 | bytes 786432 | tf_op jit(solution)/shard_map/project_more/pallas_call | solution.py:257
  74.1 3.3 %project_kv.2 = (bf16[512,512]{1,0:T(8,128)(2,1)S(1)}, bf16[512,512]{1,0:T(8,128)(2,1)S(1)}, bf16[2,4,128,128]{3,2,1,0:T(8,128)(2,1)S(1)}) custom-call(s32[18]{0:T(128)S(1)} %stack.76.refs_0_.meta, s32[4,4]{1,0:T(4,128)S(1)} %copy-done.3, f32[4]{0:T(128)S(1)} %copy-done.4, bf16[2,512,384]{2,1,0:T(8,128)(2,1)S(1)} %collective-permute-done.17.refs_3_, ...), custom_call_target="tpu_custom_call" | custom-call | flops 1610612736 | bytes 786432 | tf_op jit(solution)/shard_map/project_kv/pallas_call | solution.py:257
  78.9 2.3 %project_kv.3 = (bf16[512,512]{1,0:T(8,128)(2,1)S(1)}, bf16[512,512]{1,0:T(8,128)(2,1)S(1)}, bf16[2,4,128,128]{3,2,1,0:T(8,128)(2,1)S(1)}) custom-call(s32[18]{0:T(128)S(1)} %stack.76.refs_0_.meta, s32[4,4]{1,0:T(4,128)S(1)} %copy-done.3, f32[4]{0:T(128)S(1)} %copy-done.4, bf16[512,384]{1,0:T(8,128)(2,1)S(1)} %collective-permute-done.18.refs_3_, ...), custom_call_target="tpu_custom_call" | custom-call | flops 805306368 | bytes 786432 | tf_op jit(solution)/shard_map/project_kv/pallas_call | solution.py:257
  81.2 3.5 %collective-permute-start.22 = (bf16[2,4,128,128]{3,2,1,0:T(8,128)(2,1)S(1)}, bf16[2,4,128,128]{3,2,1,0:T(8,128)(2,1)S(1)}, u32[]{:S(2)}, u32[]{:S(2)}) collective-permute-start(bf16[2,4,128,128]{3,2,1,0:T(8,128)(2,1)S(1)} %get-tuple-element.226.state), channel_id=1, source_target_pairs={{0,64},{16,80},{32,96},{48,112},{1,65},{17,81},{33,97},{49,113},{2... | collective-permute-start | bytes 786440 | tf_op jit(solution)/shard_map/ppermute | solution.py:58
  84.8 3.6 %project_qg.2 = (bf16[512,512]{1,0:T(8,128)(2,1)S(1)}, f32[512,512]{1,0:T(8,128)S(1)}, f32[512,512]{1,0:T(8,128)S(1)}) custom-call(s32[18]{0:T(128)S(1)} %stack.76.refs_0_.meta, s32[4,4]{1,0:T(4,128)S(1)} %copy-done.3, f32[4]{0:T(128)S(1)} %copy-done.4, bf16[2,512,384]{2,1,0:T(8,128)(2,1)S(1)} %collective-permute-done.17.refs_3_, ...), custom_call_target="tpu_custom_call" | custom-call | flops 1610612736 | bytes 786432 | tf_op jit(solution)/shard_map/project_qg/pallas_call | solution.py:257
  89.0 2.8 %collective-permute-start.23 = (bf16[2,4,128,128]{3,2,1,0:T(8,128)(2,1)S(1)}, bf16[2,4,128,128]{3,2,1,0:T(8,128)(2,1)S(1)}, u32[]{:S(2)}, u32[]{:S(2)}) collective-permute-start(bf16[2,4,128,128]{3,2,1,0:T(8,128)(2,1)S(1)} %extend.2.state), channel_id=1, source_target_pairs={{0,32},{16,48},{32,0},{48,16},{64,96},{80,112},{96,64},{112,80},{1... | collective-permute-start | bytes 786440 | tf_op jit(solution)/shard_map/ppermute | solution.py:62
  96.5 2.6 %project_qg.3 = (bf16[512,512]{1,0:T(8,128)(2,1)S(1)}, f32[512,512]{1,0:T(8,128)S(1)}, f32[512,512]{1,0:T(8,128)S(1)}) custom-call(s32[18]{0:T(128)S(1)} %stack.76.refs_0_.meta, s32[4,4]{1,0:T(4,128)S(1)} %copy-done.3, f32[4]{0:T(128)S(1)} %copy-done.4, bf16[512,384]{1,0:T(8,128)(2,1)S(1)} %collective-permute-done.18.refs_3_, ...), custom_call_target="tpu_custom_call" | custom-call | flops 805306368 | bytes 786432 | tf_op jit(solution)/shard_map/project_qg/pallas_call | solution.py:257
  100.6 3.7 %collective-permute-start.27 = (bf16[2,4,128,128]{3,2,1,0:T(8,128)(2,1)S(1)}, bf16[2,4,128,128]{3,2,1,0:T(8,128)(2,1)S(1)}, u32[]{:S(2)}, u32[]{:S(2)}) collective-permute-start(bf16[2,4,128,128]{3,2,1,0:T(8,128)(2,1)S(1)} %extend.3), channel_id=1, source_target_pairs={{0,64},{16,80},{32,96},{48,112},{1,65},{17,81},{33,97},{49,113},{2... | collective-permute-start | bytes 786440 | tf_op jit(solution)/shard_map/ppermute | solution.py:58
  105.5 4.2 %collective-permute-done.25.refs_1_ = bf16[2,4,128,128]{3,2,1,0:T(8,128)(2,1)S(1)} collective-permute-done((bf16[2,4,128,128]{3,2,1,0:T(8,128)(2,1)S(1)}, bf16[2,4,128,128]{3,2,1,0:T(8,128)(2,1)S(1)}, u32[]{:S(2)}, u32[]{:S(2)}) %collective-permute-start.25) | collective-permute-done | bytes 262176 | tf_op jit(solution)/shard_map/ppermute | solution.py:67
  113.6 2.9 %collective-permute-start.29 = (f32[8,128]{1,0:T(8,128)S(1)}, f32[8,128]{1,0:T(8,128)S(1)}, u32[]{:S(2)}, u32[]{:S(2)}) collective-permute-start(f32[8,128]{1,0:T(8,128)S(1)} %add.309.first), channel_id=1, source_target_pairs={{0,8},{1,9},{2,10},{3,11},{4,12},{5,13},{6,14},{7,15},{8,0},{9,1},... | collective-permute-start | bytes 12296 | tf_op jit(solution)/shard_map/ppermute | solution.py:489
  116.5 2.2 %collective-permute-done.29.second = f32[8,128]{1,0:T(8,128)S(1)} collective-permute-done((f32[8,128]{1,0:T(8,128)S(1)}, f32[8,128]{1,0:T(8,128)S(1)}, u32[]{:S(2)}, u32[]{:S(2)}) %collective-permute-start.29) | collective-permute-done | bytes 4128 | tf_op jit(solution)/shard_map/ppermute | solution.py:489
  118.8 3.6 %collective-permute-done.30.second = f32[8,128]{1,0:T(8,128)S(1)} collective-permute-done((f32[8,128]{1,0:T(8,128)S(1)}, f32[8,128]{1,0:T(8,128)S(1)}, u32[]{:S(2)}, u32[]{:S(2)}) %collective-permute-start.30) | collective-permute-done | bytes 4128 | tf_op jit(solution)/shard_map/ppermute | solution.py:489
  123.4 3.8 %collective-permute-done.31.second = f32[8,128]{1,0:T(8,128)S(1)} collective-permute-done((f32[8,128]{1,0:T(8,128)S(1)}, f32[8,128]{1,0:T(8,128)S(1)}, u32[]{:S(2)}, u32[]{:S(2)}) %collective-permute-start.31) | collective-permute-done | bytes 4128 | tf_op jit(solution)/shard_map/ppermute | solution.py:489
  (74 shorter events, 34.2 us)
Async XLA Ops:
  0.0 6.6 %collective-permute-start = (bf16[1024,384]{1,0:T(8,128)(2,1)}, bf16[1024,384]{1,0:T(8,128)(2,1)S(1)}, u32[]{:S(2)}, u32[]{:S(2)}) collective-permute-start(bf16[1024,384]{1,0:T(8,128)(2,1)} %bitcast.22), channel_id=1, source_target_pairs={{0,1},{1,0},{2,3},{3,2},{4,5},{5,4},{6,7},{7,6},{8,9},{9,8},{10,11... | collective-permute-start | bytes 2359304 | tf_op jit(solution)/shard_map/ppermute | solution.py:53
  1.2 13.1 %collective-permute-start.1 = (bf16[512,384]{1,0:T(8,128)(2,1)S(1)}, bf16[512,384]{1,0:T(8,128)(2,1)S(1)}, u32[]{:S(2)}, u32[]{:S(2)}) collective-permute-start(bf16[512,384]{1,0:T(8,128)(2,1)S(1)} %bitcast.27), channel_id=1, source_target_pairs={{0,8},{1,9},{2,10},{3,11},{4,12},{5,13},{6,14},{7,15},{8,0},{9,1},... | collective-permute-start | bytes 1179656 | tf_op jit(solution)/shard_map/ppermute | solution.py:49
  4.6 9.8 %collective-permute-start.2 = (bf16[512,384]{1,0:T(8,128)(2,1)S(1)}, bf16[512,384]{1,0:T(8,128)(2,1)S(1)}, u32[]{:S(2)}, u32[]{:S(2)}) collective-permute-start(bf16[512,384]{1,0:T(8,128)(2,1)S(1)} %bitcast.25), channel_id=1, source_target_pairs={{0,2},{1,7},{2,4},{3,1},{4,6},{5,3},{6,0},{7,5},{8,10},{9,15},{10,... | collective-permute-start | bytes 1179656 | tf_op jit(solution)/shard_map/ppermute | solution.py:45
  14.3 8.9 %collective-permute-start.3 = (bf16[512,384]{1,0:T(8,128)(2,1)S(1)}, bf16[512,384]{1,0:T(8,128)(2,1)S(1)}, u32[]{:S(2)}, u32[]{:S(2)}) collective-permute-start(bf16[512,384]{1,0:T(8,128)(2,1)S(1)} %collective-permute-done.1.refs_1_), channel_id=1, source_target_pairs={{0,1},{1,0},{2,3},{3,2},{4,5},{5,4},{6,7},{7,6},{8,9},{9,8},{10,11... | collective-permute-start | bytes 1179656 | tf_op jit(solution)/shard_map/ppermute | solution.py:53
  14.6 8.6 %collective-permute-start.4 = (bf16[512,384]{1,0:T(8,128)(2,1)S(1)}, bf16[512,384]{1,0:T(8,128)(2,1)S(1)}, u32[]{:S(2)}, u32[]{:S(2)}) collective-permute-start(bf16[512,384]{1,0:T(8,128)(2,1)S(1)} %collective-permute-done.2.refs_5_.refs_3_), channel_id=1, source_target_pairs={{0,1},{1,0},{2,3},{3,2},{4,5},{5,4},{6,7},{7,6},{8,9},{9,8},{10,11... | collective-permute-start | bytes 1179656 | tf_op jit(solution)/shard_map/ppermute | solution.py:53
  16.1 18.6 %collective-permute-start.5 = (bf16[2,512,384]{2,1,0:T(8,128)(2,1)}, bf16[2,512,384]{2,1,0:T(8,128)(2,1)S(1)}, u32[]{:S(2)}, u32[]{:S(2)}) collective-permute-start(bf16[2,512,384]{2,1,0:T(8,128)(2,1)} %get-tuple-element.150), channel_id=1, source_target_pairs={{0,2},{1,7},{2,4},{3,1},{4,6},{5,3},{6,0},{7,5},{8,10},{9,15},{10,... | collective-permute-start | bytes 2359304 | tf_op jit(solution)/shard_map/ppermute | solution.py:45
  18.1 21.3 %collective-permute-start.7 = (bf16[2,512,384]{2,1,0:T(8,128)(2,1)}, bf16[2,512,384]{2,1,0:T(8,128)(2,1)S(1)}, u32[]{:S(2)}, u32[]{:S(2)}) collective-permute-start(bf16[2,512,384]{2,1,0:T(8,128)(2,1)} %get-tuple-element.151), channel_id=1, source_target_pairs={{0,8},{1,9},{2,10},{3,11},{4,12},{5,13},{6,14},{7,15},{8,0},{9,1},... | collective-permute-start | bytes 2359304 | tf_op jit(solution)/shard_map/ppermute | solution.py:49
  21.3 13.3 %collective-permute-start.6 = (bf16[512,384]{1,0:T(8,128)(2,1)S(1)}, bf16[512,384]{1,0:T(8,128)(2,1)S(1)}, u32[]{:S(2)}, u32[]{:S(2)}) collective-permute-start(bf16[512,384]{1,0:T(8,128)(2,1)S(1)} %collective-permute-done.2.refs_5_.refs_3_), channel_id=1, source_target_pairs={{0,2},{1,7},{2,4},{3,1},{4,6},{5,3},{6,0},{7,5},{8,10},{9,15},{10,... | collective-permute-start | bytes 1179656 | tf_op jit(solution)/shard_map/ppermute | solution.py:45
  39.4 7.5 %collective-permute-start.10 = (bf16[2,512,384]{2,1,0:T(8,128)(2,1)S(1)}, bf16[2,512,384]{2,1,0:T(8,128)(2,1)S(1)}, u32[]{:S(2)}, u32[]{:S(2)}) collective-permute-start(bf16[2,512,384]{2,1,0:T(8,128)(2,1)S(1)} %collective-permute-done.7.refs_5_), channel_id=1, source_target_pairs={{0,1},{1,0},{2,3},{3,2},{4,5},{5,4},{6,7},{7,6},{8,9},{9,8},{10,11... | collective-permute-start | bytes 2359304 | tf_op jit(solution)/shard_map/ppermute | solution.py:53
  40.0 6.8 %collective-permute-start.8 = (bf16[2,512,384]{2,1,0:T(8,128)(2,1)S(1)}, bf16[2,512,384]{2,1,0:T(8,128)(2,1)S(1)}, u32[]{:S(2)}, u32[]{:S(2)}) collective-permute-start(bf16[2,512,384]{2,1,0:T(8,128)(2,1)S(1)} %collective-permute-done.5.refs_1_), channel_id=1, source_target_pairs={{0,1},{1,0},{2,3},{3,2},{4,5},{5,4},{6,7},{7,6},{8,9},{9,8},{10,11... | collective-permute-start | bytes 2359304 | tf_op jit(solution)/shard_map/ppermute | solution.py:53
  40.6 17.4 %collective-permute-start.11 = (bf16[2,512,384]{2,1,0:T(8,128)(2,1)S(1)}, bf16[2,512,384]{2,1,0:T(8,128)(2,1)S(1)}, u32[]{:S(2)}, u32[]{:S(2)}) collective-permute-start(bf16[2,512,384]{2,1,0:T(8,128)(2,1)S(1)} %collective-permute-done.5.refs_1_), channel_id=1, source_target_pairs={{0,2},{1,7},{2,4},{3,1},{4,6},{5,3},{6,0},{7,5},{8,10},{9,15},{10,... | collective-permute-start | bytes 2359304 | tf_op jit(solution)/shard_map/ppermute | solution.py:45
  40.6 17.4 %collective-permute-start.12 = (bf16[512,384]{1,0:T(8,128)(2,1)S(1)}, bf16[512,384]{1,0:T(8,128)(2,1)S(1)}, u32[]{:S(2)}, u32[]{:S(2)}) collective-permute-start(bf16[512,384]{1,0:T(8,128)(2,1)S(1)} %collective-permute-done.6.refs_3_), channel_id=1, source_target_pairs={{0,2},{1,7},{2,4},{3,1},{4,6},{5,3},{6,0},{7,5},{8,10},{9,15},{10,... | collective-permute-start | bytes 1179656 | tf_op jit(solution)/shard_map/ppermute | solution.py:45
  43.6 14.3 %collective-permute-start.13 = (bf16[512,384]{1,0:T(8,128)(2,1)S(1)}, bf16[512,384]{1,0:T(8,128)(2,1)S(1)}, u32[]{:S(2)}, u32[]{:S(2)}) collective-permute-start(bf16[512,384]{1,0:T(8,128)(2,1)S(1)} %collective-permute-done.6.refs_3_), channel_id=1, source_target_pairs={{0,8},{1,9},{2,10},{3,11},{4,12},{5,13},{6,14},{7,15},{8,0},{9,1},... | collective-permute-start | bytes 1179656 | tf_op jit(solution)/shard_map/ppermute | solution.py:49
  58.6 13.2 %collective-permute-start.17 = (bf16[2,512,384]{2,1,0:T(8,128)(2,1)S(1)}, bf16[2,512,384]{2,1,0:T(8,128)(2,1)S(1)}, u32[]{:S(2)}, u32[]{:S(2)}) collective-permute-start(bf16[2,512,384]{2,1,0:T(8,128)(2,1)S(1)} %collective-permute-done.11.refs_1_), channel_id=1, source_target_pairs={{0,2},{1,7},{2,4},{3,1},{4,6},{5,3},{6,0},{7,5},{8,10},{9,15},{10,... | collective-permute-start | bytes 2359304 | tf_op jit(solution)/shard_map/ppermute | solution.py:45
  58.6 13.2 %collective-permute-start.18 = (bf16[512,384]{1,0:T(8,128)(2,1)S(1)}, bf16[512,384]{1,0:T(8,128)(2,1)S(1)}, u32[]{:S(2)}, u32[]{:S(2)}) collective-permute-start(bf16[512,384]{1,0:T(8,128)(2,1)S(1)} %collective-permute-done.12.refs_3_), channel_id=1, source_target_pairs={{0,8},{1,9},{2,10},{3,11},{4,12},{5,13},{6,14},{7,15},{8,0},{9,1},... | collective-permute-start | bytes 1179656 | tf_op jit(solution)/shard_map/ppermute | solution.py:49
  71.9 7.0 %collective-permute-start.20 = (bf16[512,384]{1,0:T(8,128)(2,1)S(1)}, bf16[512,384]{1,0:T(8,128)(2,1)S(1)}, u32[]{:S(2)}, u32[]{:S(2)}) collective-permute-start(bf16[512,384]{1,0:T(8,128)(2,1)S(1)} %collective-permute-done.18.refs_3_), channel_id=1, source_target_pairs={{0,1},{1,0},{2,3},{3,2},{4,5},{5,4},{6,7},{7,6},{8,9},{9,8},{10,11... | collective-permute-start | bytes 1179656 | tf_op jit(solution)/shard_map/ppermute | solution.py:53
  77.3 11.0 %collective-permute-start.21 = (bf16[2,4,128,128]{3,2,1,0:T(8,128)(2,1)S(1)}, bf16[2,4,128,128]{3,2,1,0:T(8,128)(2,1)S(1)}, u32[]{:S(2)}, u32[]{:S(2)}) collective-permute-start(bf16[2,4,128,128]{3,2,1,0:T(8,128)(2,1)S(1)} %get-tuple-element.227.state), channel_id=1, source_target_pairs={{0,16},{16,0},{32,48},{48,32},{64,80},{80,64},{96,112},{112,96},{1... | collective-permute-start | bytes 786440 | tf_op jit(solution)/shard_map/ppermute | solution.py:62
  81.2 10.6 %collective-permute-start.22 = (bf16[2,4,128,128]{3,2,1,0:T(8,128)(2,1)S(1)}, bf16[2,4,128,128]{3,2,1,0:T(8,128)(2,1)S(1)}, u32[]{:S(2)}, u32[]{:S(2)}) collective-permute-start(bf16[2,4,128,128]{3,2,1,0:T(8,128)(2,1)S(1)} %get-tuple-element.226.state), channel_id=1, source_target_pairs={{0,64},{16,80},{32,96},{48,112},{1,65},{17,81},{33,97},{49,113},{2... | collective-permute-start | bytes 786440 | tf_op jit(solution)/shard_map/ppermute | solution.py:58
  89.0 10.8 %collective-permute-start.23 = (bf16[2,4,128,128]{3,2,1,0:T(8,128)(2,1)S(1)}, bf16[2,4,128,128]{3,2,1,0:T(8,128)(2,1)S(1)}, u32[]{:S(2)}, u32[]{:S(2)}) collective-permute-start(bf16[2,4,128,128]{3,2,1,0:T(8,128)(2,1)S(1)} %extend.2.state), channel_id=1, source_target_pairs={{0,32},{16,48},{32,0},{48,16},{64,96},{80,112},{96,64},{112,80},{1... | collective-permute-start | bytes 786440 | tf_op jit(solution)/shard_map/ppermute | solution.py:62
  92.6 12.8 %collective-permute-start.24 = (bf16[2,4,128,128]{3,2,1,0:T(8,128)(2,1)S(1)}, bf16[2,4,128,128]{3,2,1,0:T(8,128)(2,1)S(1)}, u32[]{:S(2)}, u32[]{:S(2)}) collective-permute-start(bf16[2,4,128,128]{3,2,1,0:T(8,128)(2,1)S(1)} %get-tuple-element.229), channel_id=1, source_target_pairs={{0,16},{16,32},{32,48},{48,0},{64,80},{80,96},{96,112},{112,64},{1... | collective-permute-start | bytes 786440 | tf_op jit(solution)/shard_map/ppermute | solution.py:67
  92.9 16.8 %collective-permute-start.25 = (bf16[2,4,128,128]{3,2,1,0:T(8,128)(2,1)S(1)}, bf16[2,4,128,128]{3,2,1,0:T(8,128)(2,1)S(1)}, u32[]{:S(2)}, u32[]{:S(2)}) collective-permute-start(bf16[2,4,128,128]{3,2,1,0:T(8,128)(2,1)S(1)} %get-tuple-element.230), channel_id=1, source_target_pairs={{0,32},{16,48},{32,0},{48,16},{64,96},{80,112},{96,64},{112,80},{1... | collective-permute-start | bytes 786440 | tf_op jit(solution)/shard_map/ppermute | solution.py:67
  94.7 15.0 %collective-permute-start.26 = (bf16[2,4,128,128]{3,2,1,0:T(8,128)(2,1)S(1)}, bf16[2,4,128,128]{3,2,1,0:T(8,128)(2,1)S(1)}, u32[]{:S(2)}, u32[]{:S(2)}) collective-permute-start(bf16[2,4,128,128]{3,2,1,0:T(8,128)(2,1)S(1)} %get-tuple-element.231), channel_id=1, source_target_pairs={{0,48},{16,0},{32,16},{48,32},{64,112},{80,64},{96,80},{112,96},{1... | collective-permute-start | bytes 786440 | tf_op jit(solution)/shard_map/ppermute | solution.py:67
  100.6 10.4 %collective-permute-start.27 = (bf16[2,4,128,128]{3,2,1,0:T(8,128)(2,1)S(1)}, bf16[2,4,128,128]{3,2,1,0:T(8,128)(2,1)S(1)}, u32[]{:S(2)}, u32[]{:S(2)}) collective-permute-start(bf16[2,4,128,128]{3,2,1,0:T(8,128)(2,1)S(1)} %extend.3), channel_id=1, source_target_pairs={{0,64},{16,80},{32,96},{48,112},{1,65},{17,81},{33,97},{49,113},{2... | collective-permute-start | bytes 786440 | tf_op jit(solution)/shard_map/ppermute | solution.py:58
  113.6 5.1 %collective-permute-start.29 = (f32[8,128]{1,0:T(8,128)S(1)}, f32[8,128]{1,0:T(8,128)S(1)}, u32[]{:S(2)}, u32[]{:S(2)}) collective-permute-start(f32[8,128]{1,0:T(8,128)S(1)} %add.309.first), channel_id=1, source_target_pairs={{0,8},{1,9},{2,10},{3,11},{4,12},{5,13},{6,14},{7,15},{8,0},{9,1},... | collective-permute-start | bytes 12296 | tf_op jit(solution)/shard_map/ppermute | solution.py:489
  (14 other events, 77.1 us)
